TPU v7x, 32 devices: a whole 2x2x4 slice. The times are simulated.
32 devices in a mesh: elem: 8 (over z, y), sub: 4 (over x, core).
Axes of the slice: x: 2, y: 2, z: 4, core: 2. Of those that a mesh axis runs over, the one named last changes fastest.
Arguments:
- gcm_state: float32 [8192, 576], P(('elem', 'sub')), may hold values from -6 to 6
- edge_part: float32 [2048, 4, 144], P(('elem', 'sub')), may hold values from -6 to 6
- neighbours: int32 [2048, 4], P(('elem', 'sub')), may hold values from 0 to 8191, as said below
- branch: int32 [8192], P(('elem', 'sub')), may hold values 0 or 1
- routes: int32 [8192, 1], P(('elem', 'sub')), may hold values from 0 to 31; in each aligned block of 256 rows (0 to 255, 256 to 511, ...) at most 16 rows name the same one
- crm_state: float32 [2, 48, 32, 16384], P(None, None, None, ('elem', 'sub')), may hold values from -6 to 6
Outputs:
- tendency: float32 [8192, 576], P(('elem', 'sub'))
- crm_out: float32 [2, 48, 32, 16384], P(None, None, None, ('elem', 'sub'))
- span_precip: float32 [32, 512], P(('elem', 'sub'))
Inputs may be any that keep to these rules, and one draw needn't show every extreme that they name: `neighbours`: each edge names an edge of an element on the same device or on the device just before or after it in the order of elem+sub, wrapping around. `routes`: among the 256 columns of one device no owner is named more than 16 times, a bound that some block reaches.
All inputs are finite; a program needn't handle non-finite values. No bound on the sum of `branch` on one device may be relied on, other than what follows from the above.
Results may differ from a plain program's by a relative error of at most 0.0003.
Values sent between devices are 32-bit elements; how exact they have to be, the bound alone decides.
No kernel may reach another device: no remote copies, remote signals or barrier semaphores. Data moves between devices by JAX's collectives and lax.ppermute only.
A program may use at most 128 MiB of HBM per device.

v0:
```python
import jax
import jax.numpy as jnp
from jax import lax
from jax.sharding import PartitionSpec as P

NV = 8
STEPS = 3


viscosity = 0.2
timestep = 0.5


def with_halo(block, sides, width):
    for axis, dim in sides:
        count = lax.axis_size(axis)
        forward = [(i, i + 1) for i in range(count - 1)]
        forward.append((count - 1, 0))
        backward = [(target, source) for source, target in forward]
        low = lax.ppermute(
            lax.slice_in_dim(block, block.shape[dim] - width, None, axis=dim), axis, forward
        )
        high = lax.ppermute(lax.slice_in_dim(block, 0, width, axis=dim), axis, backward)
        block = jnp.concatenate([low, block, high], axis=dim)
    return block


def tables(levels, crm_levels):
    position = jnp.arange(crm_levels, dtype=jnp.float32) * (levels - 1) / (crm_levels - 1)
    interp = jnp.maximum(
        0.0, 1.0 - jnp.abs(position[:, None] - jnp.arange(levels, dtype=jnp.float32)[None, :])
    )
    field_ids = jnp.arange(NV)
    parity = jnp.where((field_ids[None, :] + jnp.arange(2)[:, None]) % 2 == 0, 1.0, -1.0)
    mixing = (
        (0.8 + 0.05 * field_ids.astype(jnp.float32))[None, :] * parity / jnp.sqrt(jnp.float32(NV))
    )
    return (interp, mixing)


def laplace_both(values):
    padded_z = jnp.concatenate([values[:, :1], values, values[:, -1:]], axis=1)
    padded = jnp.concatenate([padded_z[:, :, -1:], padded_z, padded_z[:, :, :1]], axis=2)
    middle = padded[:, 1:-1]
    left_side = middle[:, :, :-2]
    right_side = middle[:, :, 2:]
    upper = padded[:, 2:, 1:-1]
    lower = padded[:, :-2, 1:-1]
    return left_side + right_side + upper + lower - 4.0 * values


def make_force(fields, crm_levels):
    slot_count = fields.shape[0]
    levels = fields.shape[1] // NV
    interp, mixing = tables(levels, crm_levels)
    grouped = fields.reshape(slot_count, NV, levels)
    mixed_fields = jnp.einsum("vk,skl->vls", mixing, grouped, precision=lax.Precision.HIGHEST)
    return jnp.einsum("zl,vls->vzs", interp, mixed_fields, precision=lax.Precision.HIGHEST)


def expand(change, levels):
    slot_count = change.shape[2]
    interp, mixing = tables(levels, change.shape[1])
    returned = jnp.einsum("zl,vzs->vls", interp, change, precision=lax.Precision.HIGHEST)
    return jnp.einsum("vk,vls->skl", mixing, returned, precision=lax.Precision.HIGHEST).reshape(
        slot_count, -1
    )


def respond_force(force, slot_codes, crm_now):
    slot_count = force.shape[2]
    crm_levels = crm_now.shape[1]
    cond_rate = 0.15 + 0.25 * (slot_codes == 2).astype(jnp.float32)
    saturation = (1.0 - 2.0 * jnp.arange(crm_levels, dtype=jnp.float32) / (crm_levels - 1))[
        :, None, None
    ]
    push = timestep * force[:, :, None, :]
    factors = jnp.array([0.5, -1.0], jnp.float32)[:, None, None, None]
    state = crm_now
    rainfall = jnp.zeros((slot_count,), jnp.float32)
    for substep in range(STEPS):
        stepped = state + viscosity * laplace_both(state) + push
        condensed = cond_rate * jax.nn.softplus(stepped[1] - 0.3 * stepped[0] - saturation)
        state = stepped + factors * condensed[None]
        rainfall = rainfall + jnp.mean(condensed, axis=(0, 1))
    change = jnp.mean(state - crm_now, axis=2)
    occupied = slot_codes > 0
    updated = jnp.where(occupied[None, None, None, :], state, crm_now)
    rainfall = jnp.where(occupied, rainfall, 0.0)
    return (updated, change, rainfall)


def on_device(gcm_state, edge_part, neighbours, branch, routes, crm_state):
    peer_count = lax.axis_size(("elem", "sub"))
    my_index = lax.axis_index(("elem", "sub"))
    elem_count = edge_part.shape[0]
    edge_count = elem_count * 4
    crm_levels = crm_state.shape[1]
    window = with_halo(edge_part, ((("elem", "sub"), 0),), elem_count)
    flattened = window.reshape(3 * edge_count, -1)
    target = neighbours.reshape(-1)
    owner_dev = target // edge_count
    offset = (owner_dev - my_index + 1 + peer_count) % peer_count
    picked = jnp.take(flattened, offset * edge_count + target % edge_count, axis=0)
    summed = (edge_part.reshape(edge_count, -1) + picked).reshape(elem_count, 4, -1)
    paired = summed + jnp.roll(summed, -1, axis=1)
    edge_width = paired.shape[2]
    grouped = gcm_state.reshape(elem_count, 4, -1)
    columns = jnp.concatenate(
        [grouped[:, :, :edge_width] + 0.25 * paired, grouped[:, :, edge_width:]], axis=2
    ).reshape(edge_count, -1)
    levels = columns.shape[1] // NV
    destination = routes[:, 0]
    onehot = (destination[:, None] == jnp.arange(peer_count, dtype=jnp.int32)[None, :]).astype(
        jnp.int32
    )
    before = jnp.cumsum(onehot, axis=0) - onehot
    slot_rank = jnp.sum(before * onehot, axis=1)
    capacity = crm_state.shape[3] // peer_count
    position = destination * capacity + slot_rank
    feature_count = columns.shape[1]
    outgoing = (
        jnp.zeros((peer_count * capacity, feature_count), jnp.float32).at[position].set(columns)
    )
    slot_codes = jnp.zeros((peer_count * capacity,), jnp.int32).at[position].set(branch + 1)
    arrived, arrived_codes = (
        lax.all_to_all(
            outgoing.reshape(peer_count, capacity, feature_count),
            ("elem", "sub"),
            split_axis=0,
            concat_axis=0,
            tiled=True,
        ),
        lax.all_to_all(
            slot_codes.reshape(peer_count, capacity),
            ("elem", "sub"),
            split_axis=0,
            concat_axis=0,
            tiled=True,
        ),
    )
    slot_count = peer_count * capacity
    arrived_rows = arrived.reshape(slot_count, feature_count)
    force = make_force(arrived_rows, crm_levels)
    updated, change, rainfall = respond_force(force, arrived_codes.reshape(slot_count), crm_state)
    backward = expand(change, levels)
    back_width = backward.shape[1]
    returned = lax.all_to_all(
        backward.reshape(peer_count, capacity, back_width),
        ("elem", "sub"),
        split_axis=0,
        concat_axis=0,
        tiled=True,
    )
    chosen = returned.reshape(slot_count, back_width)[position]
    return (chosen, updated, rainfall.reshape(1, -1))


def solution(mesh):
    in_specs = (
        P(("elem", "sub"), None),
        P(("elem", "sub"), None, None),
        P(("elem", "sub"), None),
        P(("elem", "sub")),
        P(("elem", "sub"), None),
        P(None, None, None, ("elem", "sub")),
    )
    out_specs = (
        P(("elem", "sub"), None),
        P(None, None, None, ("elem", "sub")),
        P(("elem", "sub"), None),
    )
    return jax.shard_map(
        on_device, mesh=mesh, in_specs=in_specs, out_specs=out_specs, check_vma=False
    )
```

profile of v0, /device:TPU:0, one launch (start us, length us, event | category | flops | bytes accessed | tf_op | source)
XLA Modules:
  0.0 184.9 jit_solution(11609558347440191730)
XLA Ops:
  0.6 6.4 %collective-permute-start.1 = (f32[64,4,144]{2,1,0:T(4,128)}, f32[64,4,144]{2,1,0:T(4,128)S(1)}, u32[]{:S(2)}, u32[]{:S(2)}) collective-permute-start(f32[64,4,144]{2,1,0:T(4,128)} %param.8), channel_id=1, source_target_pairs={{1,0},{2,1},{3,2},{4,3},{5,4},{6,5},{7,6},{8,7},{9,8},{10,9},{11,1... | collective-permute-start | bytes 442376 | tf_op jit(solution)/shard_map/ppermute | solution.py:23
  10.7 1.4 scatter_custom_fusion.1
  12.8 5.7 %all-to-all-start.1 = ((s32[32,1,16]{2,1,0:T(1,128)}), s32[32,1,16]{2,1,0:T(1,128)S(1)}, u32[]{:S(2)}, u32[]{:S(2)}) async-start(s32[32,1,16]{2,1,0:T(1,128)} %bitcast.11), calls=%async_computation.1 | async-start | bytes 32768 | tf_op jit(solution)/shard_map/all_to_all | solution.py:134
  20.8 1.3 copy.21
  23.3 1.1 pad_maximum_fusion.30
  24.7 1.1 gather_fusion
  27.7 2.6 %scatter_custom_fusion = f32[512,576]{1,0:T(8,128)} fusion(s32[256]{0:T(256)} %bitcast.73, f32[256,576]{1,0:T(8,128)S(1)} %reshape.337, f32[]{:T(128)} %constant.124.clone.1), kind=kCustom, calls=%fused_computation.100 | custom fusion | bytes 1180160 | tf_op jit(solution)/shard_map/scatter | solution.py:123
  30.3 6.0 %all-to-all-start = ((f32[32,16,576]{2,1,0:T(8,128)}), f32[32,16,576]{2,1,0:T(8,128)S(1)}, u32[]{:S(2)}, u32[]{:S(2)}) async-start(f32[32,16,576]{2,1,0:T(8,128)} %bitcast.6), calls=%async_computation | async-start | bytes 2621440 | tf_op jit(solution)/shard_map/all_to_all | solution.py:127
  38.0 1.6 fusion.107
  41.0 27.3 %all-to-all-done = f32[32,16,576]{2,1,0:T(8,128)S(1)} async-done(((f32[32,16,576]{2,1,0:T(8,128)}), f32[32,16,576]{2,1,0:T(8,128)S(1)}, u32[]{:S(2)}, u32[]{:S(2)}) %all-to-all-start) | async-done | bytes 1179680 | tf_op jit(solution)/shard_map/all_to_all | solution.py:127
  68.3 0.9 reshape_reshape.6
  69.2 1.0 copy.24
  70.3 1.1 convolution_bitcast_fusion.1
  71.8 14.5 %fusion.22 = f32[2,48,32,512]{3,2,1,0:T(8,128)S(1)} fusion(f32[2,48,32,512]{3,2,1,0:T(8,128)} %param.12, f32[2,1,32,512]{3,2,1,0:T(8,128)} %get-tuple-element.22, f32[2,1,32,512]{3,2,1,0:T(8,128)S(1)} %get-tuple-element.21, f32[2,48,512]{2,1,0:T(8,128)S(1)} %fusion.43), kind=kLoop, calls=%fused_computation.53 | loop fusion | flops 31457280 | bytes 13041664 | tf_op jit(solution)/shard_map/add | solution.py:82
  86.3 2.7 %copy-done = f32[2,48,32,512]{3,2,1,0:T(8,128)} copy-done((f32[2,48,32,512]{3,2,1,0:T(8,128)}, f32[2,48,32,512]{3,2,1,0:T(8,128)S(1)}, u32[]{:S(2)}) %copy-start) | copy-done | bytes 6291480
  89.0 2.1 %fusion.29 = f32[48,32,512]{2,1,0:T(8,128)S(1)} fusion(f32[48]{0:T(128)S(1)} %copy-done.8, f32[512]{0:T(512)S(1)} %copy-done.5, f32[2,48,32,512]{3,2,1,0:T(8,128)S(1)} %fusion.22), kind=kLoop, calls=%fused_computation.73 | loop fusion | flops 7864320 | bytes 9439424 | tf_op jit(solution)/shard_map/mul | solution.py:84
  91.2 9.6 %multiply_add_fusion.2 = f32[2,48,32,512]{3,2,1,0:T(8,128)S(1)} fusion(f32[48,32,512]{2,1,0:T(8,128)S(1)} %fusion.29, f32[2]{0:T(128)S(1)} %copy-done.9, f32[2,48,512]{2,1,0:T(8,128)S(1)} %fusion.43, f32[2,48,32,512]{3,2,1,0:T(8,128)S(1)} %bitcast.67, f32[2,1,32,512]{3,2,1,0:T(8,128)S(1)} %copy-done.3, f32[2,1,32,512]{3,2,1,0:T(8,128)S(1)} %get-tuple-element.21), kind=kLoop, calls=%fused_computation.70 | loop fusion | flops 34603008 | bytes 16187400 | tf_op jit(solution)/shard_map/add | solution.py:84
  100.8 6.0 %fusion.13 = f32[2,48,32,512]{3,2,1,0:T(8,128)S(1)} fusion(f32[2,48,32,512]{3,2,1,0:T(8,128)S(1)} %multiply_add_fusion.2, f32[2,1,32,512]{3,2,1,0:T(8,128)S(1)} %get-tuple-element.20, f32[2,1,32,512]{3,2,1,0:T(8,128)S(1)} %get-tuple-element.19, f32[2,48,512]{2,1,0:T(8,128)S(1)} %fusion.43), kind=kLoop, calls=%fused_computation.34 | loop fusion | flops 31457280 | bytes 13041664 | tf_op jit(solution)/shard_map/add | solution.py:82
  106.7 2.6 %copy-done.1 = f32[2,48,32,512]{3,2,1,0:T(8,128)} copy-done((f32[2,48,32,512]{3,2,1,0:T(8,128)}, f32[2,48,32,512]{3,2,1,0:T(8,128)S(1)}, u32[]{:S(2)}) %copy-start.1) | copy-done | bytes 6291480
  109.4 2.1 %fusion.31 = f32[48,32,512]{2,1,0:T(8,128)S(1)} fusion(f32[48]{0:T(128)S(1)} %copy-done.8, f32[512]{0:T(512)S(1)} %copy-done.5, f32[2,48,32,512]{3,2,1,0:T(8,128)S(1)} %fusion.13), kind=kLoop, calls=%fused_computation.75 | loop fusion | flops 7864320 | bytes 9439424 | tf_op jit(solution)/shard_map/mul | solution.py:84
  111.5 9.6 %multiply_add_fusion.1 = f32[2,48,32,512]{3,2,1,0:T(8,128)S(1)} fusion(f32[48,32,512]{2,1,0:T(8,128)S(1)} %fusion.31, f32[2]{0:T(128)S(1)} %copy-done.9, f32[2,48,512]{2,1,0:T(8,128)S(1)} %fusion.43, f32[2,48,32,512]{3,2,1,0:T(8,128)S(1)} %multiply_add_fusion.2, f32[2,1,32,512]{3,2,1,0:T(8,128)S(1)} %get-tuple-element.20, ...), kind=kLoop, calls=%fused_computation.69 | loop fusion | flops 34603008 | bytes 16187400 | tf_op jit(solution)/shard_map/add | solution.py:84
  121.1 6.2 %fusion.4 = f32[2,48,32,512]{3,2,1,0:T(8,128)S(1)} fusion(f32[2,48,32,512]{3,2,1,0:T(8,128)S(1)} %multiply_add_fusion.1, f32[2,1,32,512]{3,2,1,0:T(8,128)S(1)} %get-tuple-element.18, f32[2,1,32,512]{3,2,1,0:T(8,128)S(1)} %get-tuple-element.17, f32[2,48,512]{2,1,0:T(8,128)S(1)} %fusion.43), kind=kLoop, calls=%fused_computation.15 | loop fusion | flops 31457280 | bytes 13041664 | tf_op jit(solution)/shard_map/add | solution.py:82
  127.3 2.1 %fusion.33 = f32[48,32,512]{2,1,0:T(8,128)S(1)} fusion(f32[48]{0:T(128)S(1)} %copy-done.8, f32[512]{0:T(512)S(1)} %copy-done.5, f32[2,48,32,512]{3,2,1,0:T(8,128)S(1)} %fusion.4), kind=kLoop, calls=%fused_computation.77 | loop fusion | flops 7864320 | bytes 9439424 | tf_op jit(solution)/shard_map/mul | solution.py:84
  129.4 13.1 %fusion.27 = (f32[2,48,32,512]{3,2,1,0:T(8,128)}, f32[2,48,512]{2,1,0:T(8,128)S(1)}) fusion(f32[2,48,32,512]{3,2,1,0:T(8,128)S(1)} %bitcast.67, f32[48,32,512]{2,1,0:T(8,128)S(1)} %fusion.33, f32[2]{0:T(128)S(1)} %copy-done.9, pred[512]{0:T(512)(128)(4,1)S(1)} %gt.21, f32[2,48,512]{2,1,0:T(8,128)S(1)} %fusion.43, ...), kind=kLoop, calls=%fused_computation.71 | loop fusion | flops 39272448 | bytes 22675976 | tf_op jit(solution)/shard_map/jit(_where)/select_n | solution.py:88
  143.0 1.3 convolution_bitcast_fusion
  144.3 1.0 copy.28
  145.4 1.7 reshape_reshape.7
  147.1 3.6 %all-to-all-start.2 = ((f32[32,16,576]{2,1,0:T(8,128)}), f32[32,16,576]{2,1,0:T(8,128)S(1)}, u32[]{:S(2)}, u32[]{:S(2)}) async-start(f32[32,16,576]{2,1,0:T(8,128)} %reshape_reshape.7), calls=%async_computation.2 | async-start | bytes 2621440 | tf_op jit(solution)/shard_map/all_to_all | solution.py:148
  150.8 10.3 %fusion.37 = (f32[512]{0:T(512)S(1)}, f32[512]{0:T(512)S(1)}, f32[512]{0:T(512)S(1)}) fusion(f32[48]{0:T(128)S(1)} %copy-done.8, f32[512]{0:T(512)S(1)} %copy-done.5, f32[2,48,32,512]{3,2,1,0:T(8,128)} %copy-done.1, f32[2,48,32,512]{3,2,1,0:T(8,128)} %copy-done.2, f32[2,48,32,512]{3,2,1,0:T(8,128)} %copy-done), kind=kLoop, calls=%fused_computation.81 | loop fusion | flops 25950720 | bytes 18882752 | tf_op jit(solution)/shard_map/reduce_sum | solution.py:85
  161.7 21.1 %all-to-all-done.2 = f32[32,16,576]{2,1,0:T(8,128)S(1)} async-done(((f32[32,16,576]{2,1,0:T(8,128)}), f32[32,16,576]{2,1,0:T(8,128)S(1)}, u32[]{:S(2)}, u32[]{:S(2)}) %all-to-all-start.2) | async-done | bytes 1179680 | tf_op jit(solution)/shard_map/all_to_all | solution.py:148
  182.8 1.1 gather_fusion.1
  183.9 1.0 copy.29
  (75 shorter events, 14.5 us)
Async XLA Ops:
  0.6 25.3 %copy-start.4 = (f32[64,4,144]{2,1,0:T(4,128)S(1)}, f32[64,4,144]{2,1,0:T(4,128)}, u32[]{:S(2)}) copy-start(f32[64,4,144]{2,1,0:T(4,128)} %param.8) | copy-start | bytes 442372
  0.6 22.6 %collective-permute-start.1 = (f32[64,4,144]{2,1,0:T(4,128)}, f32[64,4,144]{2,1,0:T(4,128)S(1)}, u32[]{:S(2)}, u32[]{:S(2)}) collective-permute-start(f32[64,4,144]{2,1,0:T(4,128)} %param.8), channel_id=1, source_target_pairs={{1,0},{2,1},{3,2},{4,3},{5,4},{6,5},{7,6},{8,7},{9,8},{10,9},{11,1... | collective-permute-start | bytes 442376 | tf_op jit(solution)/shard_map/ppermute | solution.py:23
  7.1 16.2 %collective-permute-start = (f32[64,4,144]{2,1,0:T(4,128)}, f32[64,4,144]{2,1,0:T(4,128)S(1)}, u32[]{:S(2)}, u32[]{:S(2)}) collective-permute-start(f32[64,4,144]{2,1,0:T(4,128)} %param.8), channel_id=1, source_target_pairs={{0,1},{1,2},{2,3},{3,4},{4,5},{5,6},{6,7},{7,8},{8,9},{9,10},{10,1... | collective-permute-start | bytes 442376 | tf_op jit(solution)/shard_map/ppermute | solution.py:20
  10.7 7.8 %copy-start.10 = (s32[256,1]{0,1:T(1,128)}, s32[256,1]{0,1:T(1,128)S(1)}, u32[]{:S(2)}) copy-start(s32[256,1]{0,1:T(1,128)S(1)} %compare_select_fusion.8) | copy-start | bytes 3076
  12.8 17.5 %all-to-all-start.1 = ((s32[32,1,16]{2,1,0:T(1,128)}), s32[32,1,16]{2,1,0:T(1,128)S(1)}, u32[]{:S(2)}, u32[]{:S(2)}) async-start(s32[32,1,16]{2,1,0:T(1,128)} %bitcast.11), calls=%async_computation.1 | async-start | bytes 32768 | tf_op jit(solution)/shard_map/all_to_all | solution.py:134
  30.3 38.0 %all-to-all-start = ((f32[32,16,576]{2,1,0:T(8,128)}), f32[32,16,576]{2,1,0:T(8,128)S(1)}, u32[]{:S(2)}, u32[]{:S(2)}) async-start(f32[32,16,576]{2,1,0:T(8,128)} %bitcast.6), calls=%async_computation | async-start | bytes 2621440 | tf_op jit(solution)/shard_map/all_to_all | solution.py:127
  40.4 0.6 copy-start.6
  40.4 29.9 %copy-start.12 = (f32[8]{0:T(128)S(1)}, f32[8]{0:T(128)}, u32[]{:S(2)}) copy-start(f32[8]{0:T(128)} %multiply_add_fusion.3) | copy-start | bytes 100
  40.4 31.0 %copy-start.13 = (f32[48]{0:T(128)S(1)}, f32[48]{0:T(128)}, u32[]{:S(2)}) copy-start(f32[48]{0:T(128)} %iota_multiply_fusion) | copy-start | bytes 580
  70.3 20.8 %slice-start = ((s8[6291456]{0:T(1024)(128)(4,1)}), s8[4194304]{0:T(1024)(128)(4,1)S(1)}, s32[]{:S(2)}) async-start(s8[6291456]{0:T(1024)(128)(4,1)} %bitcast.66), calls=%async_computation.3 | async-start | bytes 8388608
  71.8 17.2 %copy-start.5 = (f32[512]{0:T(512)S(1)}, f32[512]{0:T(512)}, u32[]{:S(2)}) copy-start(f32[512]{0:T(512)} %add.332) | copy-start | bytes 6148
  71.8 17.2 %copy-start.8 = (f32[48]{0:T(128)S(1)}, f32[48]{0:T(128)}, u32[]{:S(2)}) copy-start(f32[48]{0:T(128)} %multiply_subtract_fusion) | copy-start | bytes 580
  71.8 19.3 %slice-start.1 = ((s8[6291456]{0:T(1024)(128)(4,1)}), s8[2097152]{0:T(1024)(128)(4,1)S(1)}, s32[]{:S(2)}) async-start(s8[6291456]{0:T(1024)(128)(4,1)} %bitcast.66), calls=%async_computation.4 | async-start | bytes 4194304
  86.3 2.7 %copy-start = (f32[2,48,32,512]{3,2,1,0:T(8,128)}, f32[2,48,32,512]{3,2,1,0:T(8,128)S(1)}, u32[]{:S(2)}) copy-start(f32[2,48,32,512]{3,2,1,0:T(8,128)S(1)} %fusion.22) | copy-start | bytes 18874372
  89.0 2.1 %copy-start.3 = (f32[2,1,32,512]{3,2,1,0:T(8,128)S(1)}, f32[2,1,32,512]{3,2,1,0:T(8,128)}, u32[]{:S(2)}) copy-start(f32[2,1,32,512]{3,2,1,0:T(8,128)} %get-tuple-element.22) | copy-start | bytes 393220
  89.0 2.1 %copy-start.9 = (f32[2]{0:T(128)S(1)}, f32[2]{0:T(128)}, u32[]{:S(2)}) copy-start(f32[2]{0:T(128)} %constant.157.clone) | copy-start | bytes 28
  106.7 2.7 %copy-start.1 = (f32[2,48,32,512]{3,2,1,0:T(8,128)}, f32[2,48,32,512]{3,2,1,0:T(8,128)S(1)}, u32[]{:S(2)}) copy-start(f32[2,48,32,512]{3,2,1,0:T(8,128)S(1)} %fusion.13) | copy-start | bytes 18874372
  127.3 15.2 %copy-start.2 = (f32[2,48,32,512]{3,2,1,0:T(8,128)}, f32[2,48,32,512]{3,2,1,0:T(8,128)S(1)}, u32[]{:S(2)}) copy-start(f32[2,48,32,512]{3,2,1,0:T(8,128)S(1)} %fusion.4) | copy-start | bytes 18874372
  142.4 8.2 %copy-start.11 = (s32[256,1]{0,1:T(1,128)S(1)}, s32[256,1]{0,1:T(1,128)}, u32[]{:S(2)}) copy-start(s32[256,1]{0,1:T(1,128)} %copy-done.10) | copy-start | bytes 3076
  142.4 8.2 %copy-start.7 = (pred[32,16]{1,0:T(8,128)(4,1)S(1)}, pred[32,16]{1,0:T(8,128)(4,1)}, u32[]{:S(2)}) copy-start(pred[32,16]{1,0:T(8,128)(4,1)} %copy-done.6) | copy-start | bytes 1540
  147.1 35.7 %all-to-all-start.2 = ((f32[32,16,576]{2,1,0:T(8,128)}), f32[32,16,576]{2,1,0:T(8,128)S(1)}, u32[]{:S(2)}, u32[]{:S(2)}) async-start(f32[32,16,576]{2,1,0:T(8,128)} %reshape_reshape.7), calls=%async_computation.2 | async-start | bytes 2621440 | tf_op jit(solution)/shard_map/all_to_all | solution.py:148
where the time goes:
time: 186 us; the launch traced here: 185 us
  other arithmetic  85.1 us (46%)
  waiting for transfers between devices  48.4 us (26%)
  local copies, waits for them, and re-layouts  25.3 us (14%)
  starting transfers between devices  21.7 us (12%)
  matrix products  3.31 us (2%)
    all_to_all x1, waiting for transfers between devices, on_device(): lax.all_to_all(outgoing.reshape(peer_count, capacity, feature_count), ('e...  27.3 us
    add x3, other arithmetic, respond_force(): stepped = state + viscosity * laplace_both(state) + push  26.7 us
    all_to_all x1, waiting for transfers between devices, on_device(): lax.all_to_all(backward.reshape(peer_count, capacity, back_width), ('elem...  21.1 us
    add x2, other arithmetic, respond_force(): state = stepped + factors * condensed[None]  19.1 us
    select_n x1, other arithmetic, respond_force(): updated = jnp.where(occupied[None, None, None, :], state, crm_now)  13.1 us
    reduce_sum x1, other arithmetic, respond_force(): rainfall = rainfall + jnp.mean(condensed, axis=(0, 1))  10.3 us
    unnamed x35, local copies, waits for them, and re-layouts  8.93 us
    ppermute x1, starting transfers between devices, with_halo(): lax.ppermute(lax.slice_in_dim(block, 0, width, axis=dim), axis, backward)  6.42 us
  transfers between devices with their start and end apart: 5, of which 2 were waited for; matrix products, arithmetic and copies ran while one was open for 17% of the time, Pallas kernels for 0%

commit v1 on v0

v1 whole, which is shorter than its diff:
```python
import functools

import jax
import jax.numpy as jnp
import numpy as np
from jax import lax
from jax.experimental import pallas as pl
from jax.experimental.pallas import tpu as pltpu
from jax.sharding import PartitionSpec as P

NV = 8
STEPS = 3
AXES = ("elem", "sub")
LANES = 128
HALF = 64
LOG2E = 1.4426950408889634
LN2 = 0.6931471805599453
F32 = jnp.float32
BF16 = jnp.bfloat16
HIGHEST = lax.Precision.HIGHEST
SMALL_RAIN = 1e-3


def tables(levels, crm_levels):
    position = np.arange(crm_levels, dtype=np.float64) * (levels - 1) / (crm_levels - 1)
    interp = np.maximum(0.0, 1.0 - np.abs(position[:, None] - np.arange(levels)[None, :]))
    field_ids = np.arange(NV)
    parity = np.where(field_ids % 2 == 0, 1.0, -1.0)
    return interp, (0.8 + 0.05 * field_ids) * parity / np.sqrt(float(NV))


def dot(a, b, contract, precision=None):
    return lax.dot_general(
        a, b, ((contract[0:1], contract[1:2]), ((), ())),
        precision=precision, preferred_element_type=F32,
    )


def split(x):
    high = x.astype(BF16)
    return high, (x - high.astype(F32)).astype(BF16)


def pick(onehot, x, contract):
    high, low = split(x)
    return dot(onehot, high, contract) + dot(onehot, low, contract)


def iota(shape, dim):
    return lax.broadcasted_iota(jnp.int32, shape, dim)


def full(shape):
    return pl.BlockSpec(shape, lambda *_: (0,) * len(shape))


def edges_kernel(edge_ref, weight_ref, out_ref):
    parts = [
        dot(weight_ref[...], edge_ref[:, j, :], (1, 1), HIGHEST) for j in range(4)
    ]
    out_ref[...] = jnp.concatenate(parts, axis=1)


def route_kernel(peers, capacity, me_ref, routes_ref, branch_ref, neigh_ref, gcm_ref, weight_ref,
                 own_ref, pos_ref, base_ref, halo_map_ref):
    columns = routes_ref.shape[1]
    elems = columns // 4
    crm_levels = own_ref.shape[0]
    slots = peers * capacity
    half = capacity // 2
    me = me_ref[0]
    destination = routes_ref[...]
    named = iota((peers, columns), 0) == destination
    earlier = (iota((columns, columns), 0) < iota((columns, columns), 1)).astype(BF16)
    before = dot(named.astype(BF16), earlier, (1, 0))
    rank = jnp.sum(jnp.where(named, before, 0.0), axis=0, keepdims=True).astype(jnp.int32)
    upper = (rank >= half).astype(jnp.int32)
    position = upper * (slots // 2) + destination * half + rank - upper * half
    pos_ref[...] = position
    place = (iota((slots, columns), 0) == position).astype(BF16)

    target = jnp.concatenate([neigh_ref[j : j + 1, :] for j in range(4)], axis=1)
    owner = target // columns
    edge = target - owner * columns
    block = jnp.where(owner == me, 0, jnp.where(owner == (me ^ 1), 1, 2))
    source = block * columns + (edge % 4) * elems + edge // 4
    window = iota((3 * columns, columns), 0)
    chosen = (window == source).astype(F32) + (window == iota((3 * columns, columns), 1)).astype(F32)
    column = iota((columns, columns), 0)
    row = iota((columns, columns), 1)
    first = (column % 4) * elems + column // 4
    second = ((column + 1) % 4) * elems + column // 4
    pair = ((row == first) | (row == second)).astype(BF16)
    mapped = dot(pair, chosen.astype(BF16), (1, 1)).astype(BF16)
    halo_map_ref[...] = dot(place, mapped[:, columns:], (1, 0)).astype(BF16)

    own_high, own_low = split(own_ref[...])
    local = mapped[:, :columns]
    force = dot(weight_ref[...], gcm_ref[...], (1, 0), HIGHEST)
    force += 0.25 * (dot(own_high, local, (1, 1)) + dot(own_low, local, (1, 1)))
    code = (branch_ref[...] + 1).astype(F32)
    fields = jnp.concatenate(
        [force, code, jnp.zeros((HALF - crm_levels - 1, columns), F32)], axis=0
    )
    both = pick(place, fields, (1, 1))
    base_ref[...] = jnp.concatenate([both[: slots // 2], both[slots // 2 :]], axis=1)


def outgoing_kernel(base_ref, map_ref, pair_ref, other_ref, out_ref):
    crm_levels = pair_ref.shape[0]
    window = jnp.concatenate([pair_ref[...], other_ref[...]], axis=1)
    window = jnp.concatenate([window, jnp.zeros((HALF - crm_levels, window.shape[1]), F32)], axis=0)
    both = 0.25 * pick(map_ref[...], window, (1, 1))
    rows = out_ref.shape[0]
    out_ref[...] = base_ref[...] + jnp.concatenate([both[:rows], both[rows:]], axis=1)


def neighbours_sum(row, up, down, count):
    sums = []
    for k in range(count):
        left = row[k - 1] if k else pltpu.roll(row[count - 1], 1, 0)
        right = row[k + 1] if k + 1 < count else pltpu.roll(row[0], 7, 0)
        sums.append((row[k] + left) + (right + (up[k] + down[k])))
    return sums


def sweep(ref, z, crm_levels, count):
    low = jnp.maximum(z - 1, 0)
    high = jnp.minimum(z + 1, crm_levels - 1)
    rows = [[ref[at, k] for k in range(count)] for at in (z, low, high)]
    return neighbours_sum(*rows, count)


def add_up(values):
    while len(values) > 1:
        values = [a + b for a, b in zip(values[::2], values[1::2])]
    return values[0]


def rows_of_sums(ref, crm_levels):
    return add_up([ref[pl.ds(s, crm_levels, stride=8), :] for s in range(8)])


def saturation_at(z, crm_levels):
    return 1.0 - z.astype(F32) * (2.0 / (crm_levels - 1))


def before_kernel(state_ref, first_ref, sums_ref, g_ref, part_ref):
    _, crm_levels, width, _ = state_ref.shape
    count = width // 8

    def load(z, _):
        fixed = LOG2E * saturation_at(z, crm_levels)
        heat = [state_ref[0, z, pl.ds(k, 8, stride=count), :] for k in range(count)]
        moist = [state_ref[1, z, pl.ds(k, 8, stride=count), :] for k in range(count)]
        for k in range(count):
            g_ref[z, k] = LOG2E * moist[k] - (0.3 * LOG2E) * heat[k] - fixed
        at = pl.multiple_of(z * 8, 8)
        part_ref[0, pl.ds(at, 8), :] = add_up(heat)
        part_ref[1, pl.ds(at, 8), :] = add_up(moist)
        return 0

    lax.fori_loop(0, crm_levels, load, 0, unroll=8)

    def step(z, _):
        for k, total in enumerate(sweep(g_ref, z, crm_levels, count)):
            first_ref[z, k] = 0.2 * total
        return 0

    lax.fori_loop(0, crm_levels, step, 0, unroll=8)
    heat = rows_of_sums(part_ref.at[0], crm_levels) * (1.0 / width)
    moist = rows_of_sums(part_ref.at[1], crm_levels) * (1.0 / width)
    level = saturation_at(iota((crm_levels, LANES), 0), crm_levels)
    sums_ref[0] = LOG2E * (moist - 0.3 * heat - level)
    sums_ref[1] = 2.0 * heat + moist


def lane_maps(rows, capacity):
    half = capacity // 2
    row = iota((rows, LANES), 0)
    slot = iota((rows, LANES), 1)
    rank = slot % capacity
    low = (row == (slot // capacity) * half + rank) & (rank < half)
    high = (row == (slot // capacity) * half + rank - half) & (rank >= half)
    return low.astype(BF16), high.astype(BF16)


def received(arrived, capacity):
    low, high = lane_maps(arrived.shape[0], capacity)
    first, second = split(arrived)
    lower = dot(first, low, (0, 0)) + dot(second, low, (0, 0))
    upper = dot(first, high, (0, 0)) + dot(second, high, (0, 0))
    return lower[:HALF] + upper[HALF:]


def rates(code):
    return 0.15 + 0.25 * (code == 2.0).astype(F32)


def cloud_kernel(capacity, arrived_ref, first_ref, sums_ref, last_ref, reply_ref, rain_ref,
                 a_ref, b_ref, push_ref, part_ref):
    crm_levels, count = first_ref.shape[:2]
    cells = crm_levels * count * 8
    got = received(arrived_ref[...], capacity)
    force = got[:crm_levels]
    code = got[crm_levels : crm_levels + 1]
    level = iota((crm_levels, LANES), 0)
    edge = (0.4 / (crm_levels - 1)) * LOG2E
    bound = jnp.where(level == 0, -edge, 0.0) + jnp.where(level == crm_levels - 1, edge, 0.0)
    push_ref[...] = (-0.65 * LOG2E) * force + bound
    rate = rates(code)
    lowered = jnp.broadcast_to(1.15 * rate, (8, LANES))

    def run(exact):
        def condense(y):
            e = jnp.exp2(y)
            u = 1.0 + e
            amount = jnp.log2(u)
            if exact:
                amount = jnp.where(e < 2.0**-8, (LOG2E * e) * (1.0 - 0.5 * e), amount)
            return amount, y - lowered * amount

        def first(z, acc):
            push = jnp.broadcast_to(push_ref[pl.ds(z, 1), :], (8, LANES))
            new = []
            for k in range(count):
                amount, g = condense(first_ref[z, k] + push)
                a_ref[z, k] = g
                new.append(acc[k] + amount)
            return tuple(new)

        def later(src, dst, last):
            def body(z, acc):
                push = jnp.broadcast_to(push_ref[pl.ds(z, 1), :], (8, LANES))
                new, out = [], []
                for k, total in enumerate(sweep(src, z, crm_levels, count)):
                    amount, g = condense(0.2 * total + push)
                    dst[z, k] = g
                    out.append(g)
                    new.append(acc[k] + amount)
                if last:
                    part_ref[pl.ds(pl.multiple_of(z * 8, 8), 8), :] = add_up(out)
                return tuple(new)
            return body

        acc = tuple(jnp.zeros((8, LANES), F32) for _ in range(count))
        acc = lax.fori_loop(0, crm_levels, first, acc, unroll=8)
        acc = lax.fori_loop(0, crm_levels, later(a_ref, b_ref, False), acc, unroll=8)
        acc = lax.fori_loop(0, crm_levels, later(b_ref, last_ref, True), acc, unroll=8)
        mean = jnp.sum(add_up(list(acc)), axis=0, keepdims=True) * (1.0 / cells)
        rain_ref[...] = jnp.where(code > 0.0, (rate * LN2) * mean, 0.0)
        return mean

    mean = run(False)

    @pl.when(jnp.min(mean) < SMALL_RAIN)
    def _():
        run(True)

    dg = rows_of_sums(part_ref, crm_levels) * (1.0 / (count * 8)) - sums_ref[0]
    start = sums_ref[1]
    q = start
    for _ in range(STEPS):
        up = jnp.concatenate([q[:1], q[:-1]], axis=0)
        down = jnp.concatenate([q[1:], q[-1:]], axis=0)
        q = 0.6 * q + 0.2 * (up + down) + 0.5 * force
    answer = (0.7 / 2.3) * (q - start) - (3.0 / (2.3 * LOG2E)) * dg
    answer = jnp.concatenate([answer, jnp.zeros((HALF - crm_levels, LANES), F32)], axis=0)
    low, high = lane_maps(arrived_ref.shape[0], capacity)
    reply_ref[...] = jnp.concatenate([pick(low, answer, (1, 1)), pick(high, answer, (1, 1))], axis=1)


def after_kernel(capacity, arrived_ref, last_ref, state_ref, out_ref, a_ref, b_ref, push_ref):
    _, crm_levels, width, _ = state_ref.shape
    count = width // 8
    got = received(arrived_ref[...], capacity)
    occupied = jnp.broadcast_to(got[crm_levels : crm_levels + 1], (8, LANES)) > 0.0
    push_ref[...] = 2.5 * got[:crm_levels]

    def load(z, _):
        for k in range(count):
            at = pl.ds(k, 8, stride=count)
            a_ref[z, k] = 2.0 * state_ref[0, z, at, :] + state_ref[1, z, at, :]
        return 0

    def step(src, dst, scale):
        def body(z, _):
            push = jnp.broadcast_to(scale * push_ref[pl.ds(z, 1), :], (8, LANES))
            for k, total in enumerate(sweep(src, z, crm_levels, count)):
                dst[z, k] = total + push
            return 0
        return body

    def finish(z, _):
        push = jnp.broadcast_to(25.0 * push_ref[pl.ds(z, 1), :], (8, LANES))
        fixed = saturation_at(z, crm_levels)
        for k, total in enumerate(sweep(a_ref, z, crm_levels, count)):
            at = pl.ds(k, 8, stride=count)
            dry = (1.0 / LOG2E) * last_ref[z, k] + fixed
            heat = (1.0 / (125.0 * 2.3)) * (total + push) - (1.0 / 2.3) * dry
            moist = dry + 0.3 * heat
            out_ref[0, z, at, :] = jnp.where(occupied, heat, state_ref[0, z, at, :])
            out_ref[1, z, at, :] = jnp.where(occupied, moist, state_ref[1, z, at, :])
        return 0

    lax.fori_loop(0, crm_levels, load, 0, unroll=8)
    lax.fori_loop(0, crm_levels, step(a_ref, b_ref, 1.0), 0, unroll=8)
    lax.fori_loop(0, crm_levels, step(b_ref, a_ref, 5.0), 0, unroll=8)
    lax.fori_loop(0, crm_levels, finish, 0, unroll=8)


def tendency_kernel(pos_ref, returned_ref, weight_ref, out_ref):
    rows = returned_ref.shape[0]
    columns = pos_ref.shape[1]
    place = (iota((2 * rows, columns), 0) == pos_ref[...]).astype(BF16)
    high, low = split(returned_ref[...])
    lower = dot(high, place[:rows], (0, 0)) + dot(low, place[:rows], (0, 0))
    upper = dot(high, place[rows:], (0, 0)) + dot(low, place[rows:], (0, 0))
    out_ref[...] = dot(weight_ref[...], lower[:HALF] + upper[HALF:], (1, 0), HIGHEST)


def call(kernel, out, grid=None, in_specs=None, out_specs=None, scratch=(), cost=(0, 0, 0), vmem=32):
    extra = {} if grid is None else dict(grid=grid, in_specs=in_specs, out_specs=out_specs)
    return pl.pallas_call(
        kernel, out_shape=out, scratch_shapes=list(scratch),
        cost_estimate=pl.CostEstimate(flops=int(cost[0]), bytes_accessed=int(cost[1]), transcendentals=int(cost[2])),
        compiler_params=pltpu.CompilerParams(vmem_limit_bytes=vmem * 2**20), **extra,
    )


def on_device(gcm_state, edge_part, neighbours, branch, routes, crm_state):
    peers = lax.axis_size(AXES)
    me = lax.axis_index(AXES)
    columns, features = gcm_state.shape
    levels = features // NV
    _, crm_levels, width, slots = crm_state.shape
    capacity = slots // peers
    count = width // 8
    blocks = slots // LANES
    rows = slots // 2
    part = rows // blocks
    interp, mixing = tables(levels, crm_levels)
    weight = np.concatenate([mixing[k] * interp for k in range(NV)], axis=1).astype(np.float32)
    edge_weight = weight[:, : edge_part.shape[2]]
    back = np.zeros((features, HALF), np.float32)
    back[:, :crm_levels] = weight.T
    shape = jax.ShapeDtypeStruct

    own = call(edges_kernel, shape((crm_levels, columns), F32), cost=(1e7, 4e5, 0))(
        edge_part, jnp.asarray(edge_weight)
    )
    pair = lax.ppermute(own, AXES, [(i, i ^ 1) for i in range(peers)])
    other = lax.ppermute(own, AXES, [(i, (((i + 1) ^ 1) - 1) % peers) for i in range(peers)])
    smem = pl.BlockSpec(memory_space=pltpu.SMEM)
    vmem = pl.BlockSpec(memory_space=pltpu.VMEM)
    position, base, halo_map = pl.pallas_call(
        functools.partial(route_kernel, peers, capacity),
        out_shape=(
            shape((1, columns), jnp.int32),
            shape((rows, LANES), F32),
            shape((slots, 2 * columns), BF16),
        ),
        in_specs=[smem] + [vmem] * 6,
        out_specs=[vmem] * 3,
        cost_estimate=pl.CostEstimate(flops=int(2e9), bytes_accessed=int(2e6), transcendentals=0),
        compiler_params=pltpu.CompilerParams(vmem_limit_bytes=32 * 2**20),
    )(me.reshape(1), routes.T, branch.reshape(1, -1), neighbours.T, gcm_state.T, jnp.asarray(weight), own)
    outgoing = call(outgoing_kernel, shape((rows, LANES), F32), cost=(2e8, 1e6, 0))(base, halo_map, pair, other)

    field = (crm_levels, count, 8, LANES)
    state_spec = pl.BlockSpec((2, crm_levels, width, LANES), lambda j: (0, 0, 0, j))
    field_spec = pl.BlockSpec(field, lambda j: (0, 0, 0, j))
    sums_spec = pl.BlockSpec((2, crm_levels, LANES), lambda j: (0, 0, j))
    rows_spec = pl.BlockSpec((part, LANES), lambda j: (j, 0))
    whole_field = shape((crm_levels, count, 8, slots), F32)
    cells = crm_levels * width * slots
    first, sums = call(
        before_kernel, (whole_field, shape((2, crm_levels, slots), F32)), (blocks,),
        [state_spec], [field_spec, sums_spec],
        [pltpu.VMEM(field, F32), pltpu.VMEM((2, crm_levels * 8, LANES), F32)],
        (cells * 10, cells * 12, 0),
    )(crm_state)

    arrived = lax.all_to_all(outgoing.reshape(peers, capacity // 2, LANES), AXES, 0, 0, tiled=True)
    arrived = arrived.reshape(rows, LANES)
    last, reply, rain = call(
        functools.partial(cloud_kernel, capacity),
        (whole_field, shape((rows, LANES), F32), shape((1, slots), F32)), (blocks,),
        [rows_spec, field_spec, sums_spec],
        [field_spec, rows_spec, pl.BlockSpec((1, LANES), lambda j: (0, j))],
        [pltpu.VMEM(field, F32), pltpu.VMEM(field, F32), pltpu.VMEM((crm_levels, LANES), F32),
         pltpu.VMEM((crm_levels * 8, LANES), F32)],
        (cells * 30, cells * 8, cells * 6),
    )(arrived, first, sums)
    returned = lax.all_to_all(reply.reshape(peers, capacity // 2, LANES), AXES, 0, 0, tiled=True)
    updated = call(
        functools.partial(after_kernel, capacity), shape(crm_state.shape, F32), (blocks,),
        [rows_spec, field_spec, state_spec], state_spec,
        [pltpu.VMEM(field, F32), pltpu.VMEM(field, F32), pltpu.VMEM((crm_levels, LANES), F32)],
        (cells * 30, cells * 20, 0),
    )(arrived, last, crm_state)
    tendency = call(tendency_kernel, shape((features, columns), F32), cost=(1e8, 1e6, 0))(
        position, returned.reshape(rows, LANES), jnp.asarray(back)
    )
    return (tendency.T, updated, rain)


def solution(mesh):
    in_specs = (
        P(AXES, None),
        P(AXES, None, None),
        P(AXES, None),
        P(AXES),
        P(AXES, None),
        P(None, None, None, AXES),
    )
    out_specs = (
        P(AXES, None),
        P(None, None, None, AXES),
        P(AXES, None),
    )
    return jax.shard_map(
        on_device, mesh=mesh, in_specs=in_specs, out_specs=out_specs, check_vma=False
    )
```

time: 186 us -> 58.3 us (0.31)
  other arithmetic: 85.1 us -> 0 us
  waiting for transfers between devices: 48.4 us -> 0.01 us
  Pallas kernels: 0 us -> 24 us
  local copies, waits for them, and re-layouts: 25.3 us -> 17.4 us
  starting transfers between devices: 21.7 us -> 15.5 us
  matrix products: 3.31 us -> 0 us
    all_to_all x3 -> x2, waiting for transfers between devices: 48.4 us -> 0.01 us  [the longest x1 0.01 us: on_device(): lax.all_to_all(outgoing.reshape(peers, capacity // 2, LANES), AXES, 0, 0,...]
    add x11 -> x0, other arithmetic: 48.2 us -> none  [the longest x3 26.7 us: respond_force(): stepped = state + viscosity * laplace_both(state) + push]
    pallas_call x0 -> x7, Pallas kernels: none -> 24 us  [the longest x1 8.56 us: on_device(): call(functools.partial(cloud_kernel, capacity), (whole_field, shape((rows...]
    select_n x4 -> x0, other arithmetic: 14.4 us -> none  [the longest x1 13.1 us: respond_force(): updated = jnp.where(occupied[None, None, None, :], state, crm_now)]
    reduce_sum x2 -> x0, other arithmetic: 11.1 us -> none  [the longest x1 10.3 us: respond_force(): rainfall = rainfall + jnp.mean(condensed, axis=(0, 1))]
    unnamed x35 -> x28, local copies, waits for them, and re-layouts: 8.93 us -> 17.4 us
    all_to_all x3 -> x2, starting transfers between devices: 15.3 us -> 8.4 us  [the longest x1 5.83 us: on_device(): lax.all_to_all(reply.reshape(peers, capacity // 2, LANES), AXES, 0, 0, ti...]
    mul x3 -> x0, other arithmetic: 6.28 us -> none  [respond_force(): state = stepped + factors * condensed[None]]
  transfers between devices with their start and end apart: 5 -> 4, of which waited for: 2 -> 0; matrix products, arithmetic and copies ran while one was open for 17% -> 0% of each run, Pallas kernels for 0% -> 21%
where the time goes in v1:
time: 58.3 us; the launch traced here: 57.7 us
  Pallas kernels  24 us (41%)
  local copies, waits for them, and re-layouts  17.4 us (30%)
  starting transfers between devices  15.5 us (27%)
  between operations  0.73 us (1%)
    unnamed x28, local copies, waits for them, and re-layouts  17.4 us
    pallas_call x1, Pallas kernels, on_device(): call(functools.partial(cloud_kernel, capacity), (whole_field, shape((rows...  8.56 us
    pallas_call x1, Pallas kernels, on_device(): call(functools.partial(after_kernel, capacity), shape(crm_state.shape, F3...  7.28 us
    ppermute x1, starting transfers between devices, on_device(): lax.ppermute(own, AXES, [(i, ((i + 1 ^ 1) - 1) % peers) for i in range(pe...  6.59 us
    all_to_all x1, starting transfers between devices, on_device(): lax.all_to_all(reply.reshape(peers, capacity // 2, LANES), AXES, 0, 0, ti...  5.83 us
    pallas_call x1, Pallas kernels, on_device(): call(before_kernel, (whole_field, shape((2, crm_levels, slots), F32)), (b...  3.23 us
    all_to_all x1, starting transfers between devices, on_device(): lax.all_to_all(outgoing.reshape(peers, capacity // 2, LANES), AXES, 0, 0,...  2.56 us
    pallas_call x1, Pallas kernels, on_device(): call(tendency_kernel, shape((features, columns), F32), cost=(100000000.0,...  1.8 us
  transfers between devices with their start and end apart: 4, of which 0 were waited for; matrix products, arithmetic and copies ran while one was open for 0% of the time, Pallas kernels for 21%

profile of v1, /device:TPU:0, one launch (start us, length us, event | category | flops | bytes accessed | tf_op | source)
XLA Modules:
  0.0 57.7 jit_solution(18310182070832655805)
XLA Ops:
  0.6 0.9 %copy-done.3 = f32[64,4,144]{2,1,0:T(4,128)S(1)} copy-done((f32[64,4,144]{2,1,0:T(4,128)S(1)}, f32[64,4,144]{2,1,0:T(4,128)}, u32[]{:S(2)}) %copy-start.3) | copy-done | bytes 147480
  1.6 0.8 %copy-done.4 = f32[48,144]{1,0:T(8,128)S(1)} copy-done((f32[48,144]{1,0:T(8,128)S(1)}, f32[48,144]{1,0:T(8,128)}, u32[]{:S(2)}) %copy-start.4) | copy-done | bytes 27672
  2.4 0.4 shard_map.112.own_ref
  2.8 0.5 collective-permute-start
  3.3 6.6 %collective-permute-start.1 = (f32[48,256]{1,0:T(8,128)S(1)}, f32[48,256]{1,0:T(8,128)S(1)}, u32[]{:S(2)}, u32[]{:S(2)}) collective-permute-start(f32[48,256]{1,0:T(8,128)S(1)} %shard_map.112.own_ref), channel_id=1, source_target_pairs={{0,31},{1,2},{2,1},{3,4},{4,3},{5,6},{6,5},{7,8},{8,7},{9,10},{10,... | collective-permute-start | bytes 147464 | tf_op jit(solution)/shard_map/ppermute | solution.py:353
  9.9 1.1 %copy-done.7 = f32[256,576]{0,1:T(8,128)S(1)} copy-done((f32[256,576]{0,1:T(8,128)S(1)}, f32[256,576]{0,1:T(8,128)}, u32[]{:S(2)}) %copy-start.7) | copy-done | bytes 589848
  11.0 0.7 %copy-done.10 = s32[64,4]{0,1:T(4,128)S(1)} copy-done((s32[64,4]{0,1:T(4,128)S(1)}, s32[64,4]{0,1:T(4,128)}, u32[]{:S(2)}) %copy-start.10) | copy-done | bytes 1048
  11.7 0.7 %copy-done.11 = s32[256,1]{0,1:T(1,128)S(1)} copy-done((s32[256,1]{0,1:T(1,128)S(1)}, s32[256,1]{0,1:T(1,128)}, u32[]{:S(2)}) %copy-start.11) | copy-done | bytes 1048
  12.4 0.7 %copy-done.12 = s32[256]{0:T(256)S(1)} copy-done((s32[256]{0:T(256)S(1)}, s32[256]{0:T(256)}, u32[]{:S(2)}) %copy-start.12) | copy-done | bytes 1048
  13.0 0.9 %copy-done.13 = f32[48,576]{1,0:T(8,128)S(1)} copy-done((f32[48,576]{1,0:T(8,128)S(1)}, f32[48,576]{1,0:T(8,128)}, u32[]{:S(2)}) %copy-start.13) | copy-done | bytes 110616
  13.9 1.6 %shard_map.113 = (s32[1,256]{1,0:T(1,128)S(1)}, f32[256,128]{1,0:T(8,128)S(1)}, bf16[512,512]{1,0:T(8,128)(2,1)S(1)}) custom-call(s32[1]{0:T(128)} %bitcast.me_ref, s32[1,256]{1,0:T(1,128)S(1)} %bitcast.15, s32[1,256]{1,0:T(1,128)S(1)} %bitcast.16, s32[4,64]{1,0:T(4,128)S(1)} %bitcast.14, f32[576,256]{1,0:T(8,128)S(1)} %bitcast.13, ...), custom_call_target="tpu_custom_call" | custom-call | flops 2000000000 | bytes 2000000 | tf_op jit(solution)/shard_map/pallas_call | solution.py:356
  15.5 0.0 collective-permute-done.pair_ref
  15.5 0.0 collective-permute-done.1.other_ref
  15.5 1.1 %shard_map.114 = f32[256,128]{1,0:T(8,128)} custom-call(f32[256,128]{1,0:T(8,128)S(1)} %get-tuple-element.12.base_ref, bf16[512,512]{1,0:T(8,128)(2,1)S(1)} %get-tuple-element.13.map_ref, f32[48,256]{1,0:T(8,128)S(1)} %collective-permute-done.pair_ref, f32[48,256]{1,0:T(8,128)S(1)} %collective-permute-done.1.other_ref), custom_call_target="tpu_custom_call" | custom-call | flops 200000000 | bytes 1000000 | tf_op jit(solution)/shard_map/pallas_call | solution.py:368
  16.7 2.6 %all-to-all-start = ((f32[32,8,128]{2,1,0:T(8,128)}), f32[32,8,128]{2,1,0:T(8,128)S(1)}, u32[]{:S(2)}, u32[]{:S(2)}) async-start(f32[32,8,128]{2,1,0:T(8,128)} %bitcast.5), calls=%async_computation | async-start | bytes 262144 | tf_op jit(solution)/shard_map/all_to_all | solution.py:384
  19.3 0.0 copy-start
  19.3 2.8 %copy-done = f32[2,48,32,512]{3,2,1,0:T(8,128)S(1)} copy-done((f32[2,48,32,512]{3,2,1,0:T(8,128)S(1)}, f32[2,48,32,512]{3,2,1,0:T(8,128)}, u32[]{:S(2)}) %copy-start) | copy-done | bytes 6291480
  22.0 3.2 %shard_map.115 = (f32[48,4,8,512]{3,2,1,0:T(8,128)S(1)}, f32[2,48,512]{2,1,0:T(8,128)S(1)}) custom-call(f32[2,48,32,512]{3,2,1,0:T(8,128)S(1)} %copy-done), custom_call_target="tpu_custom_call" | custom-call | flops 7864320 | bytes 9437184 | tf_op jit(solution)/shard_map/pallas_call | solution.py:377
  25.3 0.0 copy-start.5
  25.3 1.7 %copy-done.5 = f32[48,4,8,512]{3,2,1,0:T(8,128)} copy-done((f32[48,4,8,512]{3,2,1,0:T(8,128)}, f32[48,4,8,512]{3,2,1,0:T(8,128)S(1)}, u32[]{:S(2)}) %copy-start.5) | copy-done | bytes 3145752
  26.9 0.7 %copy-done.8 = f32[2,48,512]{2,1,0:T(8,128)} copy-done((f32[2,48,512]{2,1,0:T(8,128)}, f32[2,48,512]{2,1,0:T(8,128)S(1)}, u32[]{:S(2)}) %copy-start.8) | copy-done | bytes 196632
  27.6 0.0 all-to-all-done
  27.6 1.9 %copy-done.6 = f32[48,4,8,512]{3,2,1,0:T(8,128)S(1)} copy-done((f32[48,4,8,512]{3,2,1,0:T(8,128)S(1)}, f32[48,4,8,512]{3,2,1,0:T(8,128)}, u32[]{:S(2)}) %copy-start.6) | copy-done | bytes 3145752
  29.5 0.9 %copy-done.9 = f32[2,48,512]{2,1,0:T(8,128)S(1)} copy-done((f32[2,48,512]{2,1,0:T(8,128)S(1)}, f32[2,48,512]{2,1,0:T(8,128)}, u32[]{:S(2)}) %copy-start.9) | copy-done | bytes 196632
  30.4 8.6 %shard_map.116 = (f32[48,4,8,512]{3,2,1,0:T(8,128)S(1)}, f32[256,128]{1,0:T(8,128)}, f32[1,512]{1,0:T(1,128)}) custom-call(f32[256,128]{1,0:T(8,128)S(1)} %bitcast.10, f32[48,4,8,512]{3,2,1,0:T(8,128)S(1)} %copy-done.6, f32[2,48,512]{2,1,0:T(8,128)S(1)} %copy-done.9), custom_call_target="tpu_custom_call" | custom-call | flops 23592960 | bytes 6291456 | tf_op jit(solution)/shard_map/pallas_call | solution.py:386
  39.0 5.8 %all-to-all-start.1 = ((f32[32,8,128]{2,1,0:T(8,128)}), f32[32,8,128]{2,1,0:T(8,128)S(1)}, u32[]{:S(2)}, u32[]{:S(2)}) async-start(f32[32,8,128]{2,1,0:T(8,128)} %bitcast.7), calls=%async_computation.1 | async-start | bytes 262144 | tf_op jit(solution)/shard_map/all_to_all | solution.py:395
  44.8 0.0 copy-start.1
  44.9 2.8 %copy-done.1 = f32[2,48,32,512]{3,2,1,0:T(8,128)S(1)} copy-done((f32[2,48,32,512]{3,2,1,0:T(8,128)S(1)}, f32[2,48,32,512]{3,2,1,0:T(8,128)}, u32[]{:S(2)}) %copy-start.1) | copy-done | bytes 6291480
  47.6 7.3 %shard_map.118 = f32[2,48,32,512]{3,2,1,0:T(8,128)} custom-call(f32[256,128]{1,0:T(8,128)S(1)} %bitcast.11, f32[48,4,8,512]{3,2,1,0:T(8,128)S(1)} %get-tuple-element.17.last_ref, f32[2,48,32,512]{3,2,1,0:T(8,128)S(1)} %copy-done.1), custom_call_target="tpu_custom_call" | custom-call | flops 23592960 | bytes 15728640 | tf_op jit(solution)/shard_map/pallas_call | solution.py:396
  54.9 0.0 all-to-all-done.1
  54.9 1.0 %copy-done.2 = f32[576,64]{1,0:T(8,128)S(1)} copy-done((f32[576,64]{1,0:T(8,128)S(1)}, f32[576,64]{1,0:T(8,128)}, u32[]{:S(2)}) %copy-start.2) | copy-done | bytes 147480
  55.9 1.8 %shard_map.117 = f32[576,256]{1,0:T(8,128)} custom-call(s32[1,256]{1,0:T(1,128)S(1)} %get-tuple-element.11.pos_ref, f32[256,128]{1,0:T(8,128)S(1)} %bitcast.12, f32[576,64]{1,0:T(8,128)S(1)} %copy-done.2), custom_call_target="tpu_custom_call" | custom-call | flops 100000000 | bytes 1000000 | tf_op jit(solution)/shard_map/pallas_call | solution.py:402
  (11 shorter events, 0.0 us)
Async XLA Ops:
  0.6 1.0 %copy-start.3 = (f32[64,4,144]{2,1,0:T(4,128)S(1)}, f32[64,4,144]{2,1,0:T(4,128)}, u32[]{:S(2)}) copy-start(f32[64,4,144]{2,1,0:T(4,128)} %edge_ref.1) | copy-start | bytes 442372
  1.6 0.8 %copy-start.4 = (f32[48,144]{1,0:T(8,128)S(1)}, f32[48,144]{1,0:T(8,128)}, u32[]{:S(2)}) copy-start(f32[48,144]{1,0:T(8,128)} %constant.17.clone.weight_ref) | copy-start | bytes 82948
  2.8 12.7 %collective-permute-start = (f32[48,256]{1,0:T(8,128)S(1)}, f32[48,256]{1,0:T(8,128)S(1)}, u32[]{:S(2)}, u32[]{:S(2)}) collective-permute-start(f32[48,256]{1,0:T(8,128)S(1)} %shard_map.112.own_ref), channel_id=1, source_target_pairs={{0,1},{1,0},{2,3},{3,2},{4,5},{5,4},{6,7},{7,6},{8,9},{9,8},{10,11... | collective-permute-start | bytes 147464 | tf_op jit(solution)/shard_map/ppermute | solution.py:352
  3.3 12.2 %collective-permute-start.1 = (f32[48,256]{1,0:T(8,128)S(1)}, f32[48,256]{1,0:T(8,128)S(1)}, u32[]{:S(2)}, u32[]{:S(2)}) collective-permute-start(f32[48,256]{1,0:T(8,128)S(1)} %shard_map.112.own_ref), channel_id=1, source_target_pairs={{0,31},{1,2},{2,1},{3,4},{4,3},{5,6},{6,5},{7,8},{8,7},{9,10},{10,... | collective-permute-start | bytes 147464 | tf_op jit(solution)/shard_map/ppermute | solution.py:353
  9.9 1.1 %copy-start.7 = (f32[256,576]{0,1:T(8,128)S(1)}, f32[256,576]{0,1:T(8,128)}, u32[]{:S(2)}) copy-start(f32[256,576]{0,1:T(8,128)} %param.9) | copy-start | bytes 1769476
  11.0 0.7 %copy-start.10 = (s32[64,4]{0,1:T(4,128)S(1)}, s32[64,4]{0,1:T(4,128)}, u32[]{:S(2)}) copy-start(s32[64,4]{0,1:T(4,128)} %param.11) | copy-start | bytes 3076
  11.7 0.7 %copy-start.11 = (s32[256,1]{0,1:T(1,128)S(1)}, s32[256,1]{0,1:T(1,128)}, u32[]{:S(2)}) copy-start(s32[256,1]{0,1:T(1,128)} %param.13) | copy-start | bytes 3076
  12.4 0.7 %copy-start.12 = (s32[256]{0:T(256)S(1)}, s32[256]{0:T(256)}, u32[]{:S(2)}) copy-start(s32[256]{0:T(256)} %param.12) | copy-start | bytes 3076
  13.0 0.9 %copy-start.13 = (f32[48,576]{1,0:T(8,128)S(1)}, f32[48,576]{1,0:T(8,128)}, u32[]{:S(2)}) copy-start(f32[48,576]{1,0:T(8,128)} %constant.18.clone.weight_ref) | copy-start | bytes 331780
  16.7 10.9 %all-to-all-start = ((f32[32,8,128]{2,1,0:T(8,128)}), f32[32,8,128]{2,1,0:T(8,128)S(1)}, u32[]{:S(2)}, u32[]{:S(2)}) async-start(f32[32,8,128]{2,1,0:T(8,128)} %bitcast.5), calls=%async_computation | async-start | bytes 262144 | tf_op jit(solution)/shard_map/all_to_all | solution.py:384
  19.3 2.8 %copy-start = (f32[2,48,32,512]{3,2,1,0:T(8,128)S(1)}, f32[2,48,32,512]{3,2,1,0:T(8,128)}, u32[]{:S(2)}) copy-start(f32[2,48,32,512]{3,2,1,0:T(8,128)} %state_ref.3) | copy-start | bytes 18874372
  25.3 1.7 %copy-start.5 = (f32[48,4,8,512]{3,2,1,0:T(8,128)}, f32[48,4,8,512]{3,2,1,0:T(8,128)S(1)}, u32[]{:S(2)}) copy-start(f32[48,4,8,512]{3,2,1,0:T(8,128)S(1)} %get-tuple-element.14.first_ref) | copy-start | bytes 9437188
  26.9 0.7 %copy-start.8 = (f32[2,48,512]{2,1,0:T(8,128)}, f32[2,48,512]{2,1,0:T(8,128)S(1)}, u32[]{:S(2)}) copy-start(f32[2,48,512]{2,1,0:T(8,128)S(1)} %get-tuple-element.15.sums_ref) | copy-start | bytes 589828
  27.6 1.9 %copy-start.6 = (f32[48,4,8,512]{3,2,1,0:T(8,128)S(1)}, f32[48,4,8,512]{3,2,1,0:T(8,128)}, u32[]{:S(2)}) copy-start(f32[48,4,8,512]{3,2,1,0:T(8,128)} %copy-done.5) | copy-start | bytes 9437188
  29.5 0.9 %copy-start.9 = (f32[2,48,512]{2,1,0:T(8,128)S(1)}, f32[2,48,512]{2,1,0:T(8,128)}, u32[]{:S(2)}) copy-start(f32[2,48,512]{2,1,0:T(8,128)} %copy-done.8) | copy-start | bytes 589828
  39.0 15.9 %all-to-all-start.1 = ((f32[32,8,128]{2,1,0:T(8,128)}), f32[32,8,128]{2,1,0:T(8,128)S(1)}, u32[]{:S(2)}, u32[]{:S(2)}) async-start(f32[32,8,128]{2,1,0:T(8,128)} %bitcast.7), calls=%async_computation.1 | async-start | bytes 262144 | tf_op jit(solution)/shard_map/all_to_all | solution.py:395
  44.8 2.8 %copy-start.1 = (f32[2,48,32,512]{3,2,1,0:T(8,128)S(1)}, f32[2,48,32,512]{3,2,1,0:T(8,128)}, u32[]{:S(2)}) copy-start(f32[2,48,32,512]{3,2,1,0:T(8,128)} %state_ref.3) | copy-start | bytes 18874372
  54.9 1.0 %copy-start.2 = (f32[576,64]{1,0:T(8,128)S(1)}, f32[576,64]{1,0:T(8,128)}, u32[]{:S(2)}) copy-start(f32[576,64]{1,0:T(8,128)} %constant.19.clone.weight_ref) | copy-start | bytes 442372

commit v2 on v1

v2 whole, which is shorter than its diff:
```python
import functools

import jax
import jax.numpy as jnp
import numpy as np
from jax import lax
from jax.experimental import pallas as pl
from jax.experimental.pallas import tpu as pltpu
from jax.sharding import PartitionSpec as P

NV = 8
STEPS = 3
AXES = ("elem", "sub")
LANES = 128
HALF = 64
LOG2E = 1.4426950408889634
F32 = jnp.float32
BF16 = jnp.bfloat16
HIGHEST = lax.Precision.HIGHEST
SMALL_RAIN = 1e-3


def tables(levels, crm_levels):
    position = np.arange(crm_levels, dtype=np.float64) * (levels - 1) / (crm_levels - 1)
    interp = np.maximum(0.0, 1.0 - np.abs(position[:, None] - np.arange(levels)[None, :]))
    field_ids = np.arange(NV)
    parity = np.where(field_ids % 2 == 0, 1.0, -1.0)
    return interp, (0.8 + 0.05 * field_ids) * parity / np.sqrt(float(NV))


def dot(a, b, contract, precision=None):
    return lax.dot_general(
        a, b, ((contract[0:1], contract[1:2]), ((), ())),
        precision=precision, preferred_element_type=F32,
    )


def split(x):
    high = x.astype(BF16)
    return high, (x - high.astype(F32)).astype(BF16)


def pick(onehot, x, contract):
    high, low = split(x)
    return dot(onehot, high, contract) + dot(onehot, low, contract)


def iota(shape, dim):
    return lax.broadcasted_iota(jnp.int32, shape, dim)


def full(shape):
    return pl.BlockSpec(shape, lambda *_: (0,) * len(shape))


def edges_kernel(edge_ref, weight_ref, out_ref):
    parts = [
        dot(weight_ref[...], edge_ref[:, j, :], (1, 1), HIGHEST) for j in range(4)
    ]
    out_ref[...] = jnp.concatenate(parts, axis=1)


def route_kernel(peers, capacity, me_ref, routes_ref, branch_ref, neigh_ref, gcm_ref, weight_ref,
                 own_ref, pos_ref, base_ref, halo_map_ref):
    columns = routes_ref.shape[1]
    elems = columns // 4
    crm_levels = own_ref.shape[0]
    slots = peers * capacity
    half = capacity // 2
    me = me_ref[0]
    destination = routes_ref[...]
    named = iota((peers, columns), 0) == destination
    earlier = (iota((columns, columns), 0) < iota((columns, columns), 1)).astype(BF16)
    before = dot(named.astype(BF16), earlier, (1, 0))
    rank = jnp.sum(jnp.where(named, before, 0.0), axis=0, keepdims=True).astype(jnp.int32)
    upper = (rank >= half).astype(jnp.int32)
    position = upper * (slots // 2) + destination * half + rank - upper * half
    pos_ref[...] = position
    place = (iota((slots, columns), 0) == position).astype(BF16)

    target = jnp.concatenate([neigh_ref[j : j + 1, :] for j in range(4)], axis=1)
    owner = target // columns
    edge = target - owner * columns
    block = jnp.where(owner == me, 0, jnp.where(owner == (me ^ 1), 1, 2))
    source = block * columns + (edge % 4) * elems + edge // 4
    window = iota((3 * columns, columns), 0)
    chosen = (window == source).astype(F32) + (window == iota((3 * columns, columns), 1)).astype(F32)
    column = iota((columns, columns), 0)
    row = iota((columns, columns), 1)
    first = (column % 4) * elems + column // 4
    second = ((column + 1) % 4) * elems + column // 4
    pair = ((row == first) | (row == second)).astype(BF16)
    mapped = dot(pair, chosen.astype(BF16), (1, 1)).astype(BF16)
    halo_map_ref[...] = dot(place, mapped[:, columns:], (1, 0)).astype(BF16)

    own_high, own_low = split(own_ref[...])
    local = mapped[:, :columns]
    force = dot(weight_ref[...], gcm_ref[...], (1, 0), HIGHEST)
    force += 0.25 * (dot(own_high, local, (1, 1)) + dot(own_low, local, (1, 1)))
    code = (branch_ref[...] + 1).astype(F32)
    fields = jnp.concatenate(
        [force, code, jnp.zeros((HALF - crm_levels - 1, columns), F32)], axis=0
    )
    both = pick(place, fields, (1, 1))
    base_ref[...] = jnp.concatenate([both[: slots // 2], both[slots // 2 :]], axis=1)


def outgoing_kernel(base_ref, map_ref, pair_ref, other_ref, out_ref):
    crm_levels = pair_ref.shape[0]
    window = jnp.concatenate([pair_ref[...], other_ref[...]], axis=1)
    window = jnp.concatenate([window, jnp.zeros((HALF - crm_levels, window.shape[1]), F32)], axis=0)
    both = 0.25 * pick(map_ref[...], window, (1, 1))
    rows = out_ref.shape[0]
    out_ref[...] = base_ref[...] + jnp.concatenate([both[:rows], both[rows:]], axis=1)


def five_points(rows, z):
    row, up, down = rows[z], rows[max(z - 1, 0)], rows[min(z + 1, len(rows) - 1)]
    count = len(row)
    ring = [pltpu.roll(row[-1], 1, 0)] + row + [pltpu.roll(row[0], 7, 0)]
    pairs = [row[k] + row[k + 1] for k in range(0, count, 2)]
    return [
        (pairs[k // 2] + ring[k if k % 2 == 0 else k + 2]) + (up[k] + down[k]) for k in range(count)
    ]


def add_up(values):
    while len(values) > 1:
        values = [a + b for a, b in zip(values[::2], values[1::2])]
    return values[0]


def rows_of_sums(ref, crm_levels):
    return add_up([ref[pl.ds(s, crm_levels, stride=8), :] for s in range(8)])


def saturation(z, crm_levels):
    return 1.0 - z * (2.0 / (crm_levels - 1))


def levels_of(crm_levels):
    return iota((crm_levels, LANES), 0)


def shifted(x):
    return jnp.concatenate([x[:1], x[:-1]], axis=0) + jnp.concatenate([x[1:], x[-1:]], axis=0)


def before_kernel(state_ref, kept_ref, first_ref, linear_ref, sums_ref, part_ref, sems):
    blocks, _, crm_levels, width, _ = kept_ref.shape
    count = width // 8

    def copy(j):
        lanes = pl.ds(pl.multiple_of(j * LANES, LANES), LANES)
        return pltpu.make_async_copy(state_ref.at[:, :, :, lanes], kept_ref.at[j], sems.at[j])

    for j in range(blocks):
        copy(j).start()

    def block(j, _):
        copy(j).wait()
        dry = []
        fields = [[] for _ in range(STEPS + 1)]
        for i in range(crm_levels + STEPS):
            if i < crm_levels:
                heat = [kept_ref[j, 0, i, pl.ds(k, 8, stride=count), :] for k in range(count)]
                moist = [kept_ref[j, 1, i, pl.ds(k, 8, stride=count), :] for k in range(count)]
                dry.append([m - 0.3 * h for h, m in zip(heat, moist)])
                fields[0].append([(h + h) + m for h, m in zip(heat, moist)])
                part_ref[0, pl.ds(8 * i, 8), :] = add_up(dry[i])
                part_ref[1, pl.ds(8 * i, 8), :] = add_up(fields[0][i])
            z = i - 1
            if 0 <= z < crm_levels:
                for k, total in enumerate(five_points(dry, z)):
                    first_ref[j, z, k] = (0.2 * LOG2E) * total
            for t in range(1, STEPS + 1):
                z = i - t
                if 0 <= z < crm_levels:
                    fields[t].append(five_points(fields[t - 1], z))
            if 0 <= z < crm_levels:
                for k, total in enumerate(fields[STEPS][z]):
                    linear_ref[j, z, k] = (1.0 / 125.0) * total
        level = saturation(levels_of(crm_levels).astype(F32), crm_levels)
        dry_mean = rows_of_sums(part_ref.at[0], crm_levels) * (1.0 / width)
        sums_ref[j, 0] = LOG2E * (dry_mean - level)
        sums_ref[j, 1] = rows_of_sums(part_ref.at[1], crm_levels) * (1.0 / width)
        return 0

    lax.fori_loop(0, blocks, block, 0)


def lane_maps(rows, capacity):
    half = capacity // 2
    row = iota((rows, LANES), 0)
    slot = iota((rows, LANES), 1)
    rank = slot % capacity
    low = (row == (slot // capacity) * half + rank) & (rank < half)
    high = (row == (slot // capacity) * half + rank - half) & (rank >= half)
    return low.astype(BF16), high.astype(BF16)


def received(arrived, low, high):
    first, second = split(arrived)
    lower = dot(first, low, (0, 0)) + dot(second, low, (0, 0))
    upper = dot(first, high, (0, 0)) + dot(second, high, (0, 0))
    return lower[:HALF] + upper[HALF:]


def cloud_kernel(capacity, arrived_ref, first_ref, sums_ref, last_ref, row_ref, occupied_ref,
                 reply_ref, rain_ref, got_ref, push_ref, part_ref, field_ref):
    blocks, crm_levels, count = first_ref.shape[:3]
    cells = crm_levels * count * 8
    part = arrived_ref.shape[0] // blocks
    low, high = lane_maps(part, capacity)
    for j in range(blocks):
        got_ref[j] = received(arrived_ref[pl.ds(j * part, part), :], low, high)
    level = levels_of(crm_levels)
    edge = (0.4 / (crm_levels - 1)) * LOG2E
    bound = jnp.where(level == 0, -edge, 0.0) + jnp.where(level == crm_levels - 1, edge, 0.0)
    dried = LOG2E * saturation(level.astype(F32), crm_levels)

    def block(j, _):
        force = got_ref[j, :crm_levels, :]
        code = got_ref[j, crm_levels : crm_levels + 1, :]
        rate = 0.15 + 0.25 * (code == 2.0).astype(F32)
        lowered = jnp.broadcast_to((1.15 * LOG2E) * rate, (8, LANES))
        push = (-0.65 * LOG2E) * force
        push_ref[0] = push - dried
        push_ref[1] = push + bound

        def finish(acc):
            mean = jnp.sum(add_up(list(acc)), axis=0, keepdims=True) * (1.0 / cells)
            rain_ref[j] = jnp.where(code > 0.0, rate * mean, 0.0)
            return mean

        def pushed(step, z):
            return jnp.broadcast_to(push_ref[min(step, 1), pl.ds(z, 1), :], (8, LANES))

        fields = [[] for _ in range(STEPS)]
        acc = [jnp.zeros((8, LANES), F32) for _ in range(count)]
        for i in range(crm_levels + STEPS - 1):
            for t in range(STEPS):
                z = i - t
                if not 0 <= z < crm_levels:
                    continue
                push = pushed(t, z)
                if t == 0:
                    values = [first_ref[j, z, k] + push for k in range(count)]
                else:
                    values = [0.2 * total + push for total in five_points(fields[t - 1], z)]
                amounts = [jnp.log(1.0 + jnp.exp2(y)) for y in values]
                acc = [a + amount for a, amount in zip(acc, amounts)]
                values = [y - lowered * amount for y, amount in zip(values, amounts)]
                fields[t].append(values)
                if t == STEPS - 1:
                    for k in range(count):
                        last_ref[j, z, k] = values[k]
                    part_ref[pl.ds(8 * z, 8), :] = add_up(values)
        mean = finish(acc)

        @pl.when(jnp.min(mean) < SMALL_RAIN)
        def _():
            def condense(z, k, y, acc, store):
                e = jnp.exp2(y)
                amount = jnp.where(e < 2.0**-8, e * (1.0 - 0.5 * e), jnp.log(1.0 + e))
                store[z, k] = y - lowered * amount
                return acc + amount

            def first(z, acc):
                push = pushed(0, z)
                return tuple(
                    condense(z, k, first_ref[j, z, k] + push, acc[k], field_ref.at[0]) for k in range(count)
                )

            def later(source, target):
                def body(z, acc):
                    push = pushed(1, z)
                    at = (z, jnp.maximum(z - 1, 0), jnp.minimum(z + 1, crm_levels - 1))
                    row, up, down = [[source[y, k] for k in range(count)] for y in at]
                    totals = five_points([up, row, down], 1)
                    return tuple(
                        condense(z, k, 0.2 * totals[k] + push, acc[k], target) for k in range(count)
                    )
                return body

            acc = tuple(jnp.zeros((8, LANES), F32) for _ in range(count))
            acc = lax.fori_loop(0, crm_levels, first, acc)
            acc = lax.fori_loop(0, crm_levels, later(field_ref.at[0], field_ref.at[1]), acc)
            acc = lax.fori_loop(0, crm_levels, later(field_ref.at[1], last_ref.at[j]), acc)

            def totals(z, _):
                at = pl.ds(pl.multiple_of(8 * z, 8), 8)
                part_ref[at, :] = add_up([last_ref[j, z, k] for k in range(count)])
                return 0

            lax.fori_loop(0, crm_levels, totals, 0)
            finish(acc)

        dg = rows_of_sums(part_ref, crm_levels) * (1.0 / (count * 8)) - sums_ref[j, 0]
        start = sums_ref[j, 1]
        q, response = start, jnp.zeros_like(start)
        for _ in range(STEPS):
            q = 0.6 * q + 0.2 * shifted(q) + 0.5 * force
            response = 0.6 * response + 0.2 * shifted(response) + 0.5 * force
        row_ref[j] = response
        occupied_ref[j] = code
        answer = (0.7 / 2.3) * (q - start) - (3.0 / (2.3 * LOG2E)) * dg
        answer = jnp.concatenate([answer, jnp.zeros((HALF - crm_levels, LANES), F32)], axis=0)
        reply = jnp.concatenate([pick(low, answer, (1, 1)), pick(high, answer, (1, 1))], axis=1)
        reply_ref[pl.ds(pl.multiple_of(j * part, part), part), :] = reply
        return 0

    lax.fori_loop(0, blocks, block, 0)


def after_kernel(kept_ref, last_ref, linear_ref, row_ref, occupied_ref, out_ref, new_ref, sems):
    blocks, _, crm_levels, width, _ = kept_ref.shape
    count = width // 8

    def copy(j):
        lanes = pl.ds(pl.multiple_of(j * LANES, LANES), LANES)
        return pltpu.make_async_copy(new_ref.at[j], out_ref.at[:, :, :, lanes], sems.at[j])

    def block(j, _):
        occupied = jnp.broadcast_to(occupied_ref[j], (8, LANES)) > 0.0
        for z in range(crm_levels):
            row = jnp.broadcast_to(row_ref[j, pl.ds(z, 1), :], (8, LANES))
            for k in range(count):
                at = pl.ds(k, 8, stride=count)
                linear = linear_ref[j, z, k] + row
                dry = (1.0 / LOG2E) * last_ref[j, z, k] + saturation(z, crm_levels)
                heat = (1.0 / 2.3) * (linear - dry)
                moist = dry + 0.3 * heat
                new_ref[j, 0, z, at, :] = jnp.where(occupied, heat, kept_ref[j, 0, z, at, :])
                new_ref[j, 1, z, at, :] = jnp.where(occupied, moist, kept_ref[j, 1, z, at, :])
        copy(j).start()
        return 0

    lax.fori_loop(0, blocks, block, 0)
    for j in range(blocks):
        copy(j).wait()


def tendency_kernel(pos_ref, returned_ref, weight_ref, out_ref):
    rows = returned_ref.shape[0]
    columns = pos_ref.shape[1]
    place = (iota((2 * rows, columns), 0) == pos_ref[...]).astype(BF16)
    high, low = split(returned_ref[...])
    lower = dot(high, place[:rows], (0, 0)) + dot(low, place[:rows], (0, 0))
    upper = dot(high, place[rows:], (0, 0)) + dot(low, place[rows:], (0, 0))
    out_ref[...] = dot(weight_ref[...], lower[:HALF] + upper[HALF:], (1, 0), HIGHEST)


def call(kernel, out, scratch=(), cost=(0, 0, 0), vmem=32, **specs):
    return pl.pallas_call(
        kernel, out_shape=out, scratch_shapes=list(scratch),
        cost_estimate=pl.CostEstimate(flops=int(cost[0]), bytes_accessed=int(cost[1]), transcendentals=int(cost[2])),
        compiler_params=pltpu.CompilerParams(vmem_limit_bytes=vmem * 2**20), **specs,
    )


def from_hbm(*arrays):
    return [pltpu.with_memory_space_constraint(x, pltpu.HBM) for x in arrays]


def cloud_before(crm_state):
    _, crm_levels, width, slots = crm_state.shape
    blocks = slots // LANES
    cells = crm_levels * width * slots
    field = (blocks, crm_levels, width // 8, 8, LANES)
    return call(
        before_kernel,
        (
            pltpu.VMEM((blocks, 2, crm_levels, width, LANES), F32),
            pltpu.VMEM(field, F32),
            pltpu.VMEM(field, F32),
            pltpu.VMEM((blocks, 2, crm_levels, LANES), F32),
        ),
        [pltpu.VMEM((2, crm_levels * 8, LANES), F32), pltpu.SemaphoreType.DMA((blocks,))],
        (cells * 25, cells * 8, 0),
        in_specs=[pl.BlockSpec(memory_space=pltpu.HBM)],
        out_specs=[pl.BlockSpec(memory_space=pltpu.VMEM)] * 4,
    )(*from_hbm(crm_state))


def cloud_steps(capacity, arrived, first, sums):
    blocks, crm_levels, count = first.shape[:3]
    slots = blocks * LANES
    cells = crm_levels * count * 8 * slots
    return call(
        functools.partial(cloud_kernel, capacity),
        (
            pltpu.VMEM(first.shape, F32),
            pltpu.VMEM((blocks, crm_levels, LANES), F32),
            pltpu.VMEM((blocks, 1, LANES), F32),
            jax.ShapeDtypeStruct(arrived.shape, F32),
            jax.ShapeDtypeStruct((blocks, 1, LANES), F32),
        ),
        [
            pltpu.VMEM((blocks, HALF, LANES), F32),
            pltpu.VMEM((2, crm_levels, LANES), F32),
            pltpu.VMEM((crm_levels * 8, LANES), F32),
            pltpu.VMEM((2,) + first.shape[1:], F32),
        ],
        (cells * 30, cells * 8, cells * 6),
        in_specs=[pl.BlockSpec(memory_space=pltpu.VMEM)] * 3,
        out_specs=[pl.BlockSpec(memory_space=pltpu.VMEM)] * 5,
    )(arrived, first, sums)


def cloud_after(kept, last, linear, row, occupied):
    blocks, _, crm_levels, width, _ = kept.shape
    slots = blocks * LANES
    cells = crm_levels * width * slots
    return call(
        after_kernel,
        jax.ShapeDtypeStruct((2, crm_levels, width, slots), F32),
        [pltpu.VMEM(kept.shape, F32), pltpu.SemaphoreType.DMA((blocks,))],
        (cells * 10, cells * 8, 0),
        in_specs=[pl.BlockSpec(memory_space=pltpu.VMEM)] * 5,
        out_specs=pl.BlockSpec(memory_space=pltpu.HBM),
    )(kept, last, linear, row, occupied)


def on_device(gcm_state, edge_part, neighbours, branch, routes, crm_state):
    peers = lax.axis_size(AXES)
    me = lax.axis_index(AXES)
    columns, features = gcm_state.shape
    levels = features // NV
    _, crm_levels, width, slots = crm_state.shape
    capacity = slots // peers
    rows = slots // 2
    interp, mixing = tables(levels, crm_levels)
    weight = np.concatenate([mixing[k] * interp for k in range(NV)], axis=1).astype(np.float32)
    edge_weight = weight[:, : edge_part.shape[2]]
    back = np.zeros((features, HALF), np.float32)
    back[:, :crm_levels] = weight.T
    shape = jax.ShapeDtypeStruct

    own = call(edges_kernel, shape((crm_levels, columns), F32), cost=(1e7, 4e5, 0))(
        *from_hbm(edge_part, jnp.asarray(edge_weight))
    )
    pair = lax.ppermute(own, AXES, [(i, i ^ 1) for i in range(peers)])
    other = lax.ppermute(own, AXES, [(i, (((i + 1) ^ 1) - 1) % peers) for i in range(peers)])
    smem = pl.BlockSpec(memory_space=pltpu.SMEM)
    vmem = pl.BlockSpec(memory_space=pltpu.VMEM)
    position, base, halo_map = call(
        functools.partial(route_kernel, peers, capacity),
        (
            shape((1, columns), jnp.int32),
            shape((rows, LANES), F32),
            shape((slots, 2 * columns), BF16),
        ),
        cost=(2e9, 2e6, 0),
        in_specs=[smem] + [vmem] * 6,
        out_specs=[vmem] * 3,
    )(
        me.reshape(1),
        *from_hbm(routes.T, branch.reshape(1, -1), neighbours.T, gcm_state.T, jnp.asarray(weight)),
        own,
    )
    outgoing = call(outgoing_kernel, shape((rows, LANES), F32), cost=(2e8, 1e6, 0))(base, halo_map, pair, other)
    kept, first, linear, sums = cloud_before(crm_state)
    arrived = lax.all_to_all(outgoing.reshape(peers, capacity // 2, LANES), AXES, 0, 0, tiled=True)
    last, row, occupied, reply, rain = cloud_steps(capacity, arrived.reshape(rows, LANES), first, sums)
    returned = lax.all_to_all(reply.reshape(peers, capacity // 2, LANES), AXES, 0, 0, tiled=True)
    updated = cloud_after(kept, last, linear, row, occupied)
    tendency = call(tendency_kernel, shape((features, columns), F32), cost=(1e8, 1e6, 0))(
        position, returned.reshape(rows, LANES), *from_hbm(jnp.asarray(back))
    )
    return (tendency.T, updated, rain.reshape(1, slots))


def solution(mesh):
    in_specs = (
        P(AXES, None),
        P(AXES, None, None),
        P(AXES, None),
        P(AXES),
        P(AXES, None),
        P(None, None, None, AXES),
    )
    out_specs = (
        P(AXES, None),
        P(None, None, None, AXES),
        P(AXES, None),
    )
    return jax.shard_map(
        on_device, mesh=mesh, in_specs=in_specs, out_specs=out_specs, check_vma=False
    )
```

time: 58.3 us -> 54.6 us (0.937)
  local copies, waits for them, and re-layouts: 17.4 us -> 14.2 us
  Pallas kernels: 24 us -> 21.8 us
  starting transfers between devices: 15.5 us -> 17 us
    pallas_call x4, Pallas kernels: 20.6 us -> 16.5 us  [the longest x1 6.67 us: cloud_steps(): call(functools.partial(cloud_kernel, capacity), (pltpu.VMEM(first.shape,...]
    unnamed x28 -> x16, local copies, waits for them, and re-layouts: 17.4 us -> 14.2 us
    all_to_all x1, starting transfers between devices: 2.56 us -> 4.76 us  [on_device(): lax.all_to_all(outgoing.reshape(peers, capacity // 2, LANES), AXES, 0, 0,...]
    pallas_call x1, Pallas kernels: 1.8 us -> 2.77 us  [on_device(): call(tendency_kernel, shape((features, columns), F32), cost=(100000000.0,...]
    pallas_call x1, Pallas kernels: 0.44 us -> 1.4 us  [on_device(): call(edges_kernel, shape((crm_levels, columns), F32), cost=(10000000.0, 4...]
  transfers between devices with their start and end apart: 4 -> 4, of which waited for: 0 -> 1; matrix products, arithmetic and copies ran while one was open for 0% -> 0% of each run, Pallas kernels for 21% -> 18%
where the time goes in v2:
time: 54.6 us; the launch traced here: 54.2 us
  Pallas kernels  21.8 us (40%)
  starting transfers between devices  17 us (31%)
  local copies, waits for them, and re-layouts  14.2 us (26%)
  between operations  0.72 us (1%)
    unnamed x16, local copies, waits for them, and re-layouts  14.2 us
    pallas_call x1, Pallas kernels, cloud_steps(): call(functools.partial(cloud_kernel, capacity), (pltpu.VMEM(first.shape,...  6.67 us
    ppermute x1, starting transfers between devices, on_device(): lax.ppermute(own, AXES, [(i, ((i + 1 ^ 1) - 1) % peers) for i in range(pe...  6.44 us
    all_to_all x1, starting transfers between devices, on_device(): lax.all_to_all(reply.reshape(peers, capacity // 2, LANES), AXES, 0, 0, ti...  5.83 us
    all_to_all x1, starting transfers between devices, on_device(): lax.all_to_all(outgoing.reshape(peers, capacity // 2, LANES), AXES, 0, 0,...  4.76 us
    pallas_call x1, Pallas kernels, cloud_before(): call(before_kernel, (pltpu.VMEM((blocks, 2, crm_levels, width, LANES), F3...  4.05 us
    pallas_call x1, Pallas kernels, cloud_after(): call(after_kernel, jax.ShapeDtypeStruct((2, crm_levels, width, slots), F3...  3.05 us
    pallas_call x1, Pallas kernels, on_device(): call(tendency_kernel, shape((features, columns), F32), cost=(100000000.0,...  2.77 us
  transfers between devices with their start and end apart: 4, of which 1 were waited for; matrix products, arithmetic and copies ran while one was open for 0% of the time, Pallas kernels for 18%

profile of v2, /device:TPU:0, one launch (start us, length us, event | category | flops | bytes accessed | tf_op | source)
XLA Modules:
  0.0 54.2 jit_solution(3900284353483512544)
XLA Ops:
  0.6 1.4 %shard_map.112.own_ref = f32[48,256]{1,0:T(8,128)S(1)} custom-call(f32[64,4,144]{2,1,0:T(4,128)} %edge_ref.1, f32[48,144]{1,0:T(8,128)} %constant.17.clone.weight_ref), custom_call_target="tpu_custom_call" | custom-call | flops 10000000 | bytes 400000 | tf_op jit(solution)/shard_map/pallas_call | solution.py:440
  2.0 6.4 %collective-permute-start.1 = (f32[48,256]{1,0:T(8,128)S(1)}, f32[48,256]{1,0:T(8,128)S(1)}, u32[]{:S(2)}, u32[]{:S(2)}) collective-permute-start(f32[48,256]{1,0:T(8,128)S(1)} %shard_map.112.own_ref), channel_id=1, source_target_pairs={{0,31},{1,2},{2,1},{3,4},{4,3},{5,6},{6,5},{7,8},{8,7},{9,10},{10,... | collective-permute-start | bytes 147464 | tf_op jit(solution)/shard_map/ppermute | solution.py:444
  8.5 0.0 collective-permute-start
  8.5 2.7 %shard_map.113 = (s32[1,256]{1,0:T(1,128)S(1)}, f32[256,128]{1,0:T(8,128)S(1)}, bf16[512,512]{1,0:T(8,128)(2,1)S(1)}) custom-call(s32[1]{0:T(128)} %bitcast.me_ref, s32[1,256]{1,0:T(1,128)} %bitcast.16, s32[1,256]{1,0:T(1,128)} %bitcast.17, s32[4,64]{1,0:T(4,128)} %bitcast.15, f32[576,256]{1,0:T(8,128)} %bitcast.14, f32[48,576]{1,0:T(8,128)} %constant.18.clone.weight_ref, ...), custom_call_target="tpu_custom_call" | custom-call | flops 2000000000 | bytes 2000000 | tf_op jit(solution)/shard_map/pallas_call | solution.py:447
  11.2 0.0 collective-permute-done.1.other_ref
  11.2 0.0 collective-permute-done.pair_ref
  11.2 1.2 %shard_map.114 = f32[256,128]{1,0:T(8,128)} custom-call(f32[256,128]{1,0:T(8,128)S(1)} %get-tuple-element.16.base_ref, bf16[512,512]{1,0:T(8,128)(2,1)S(1)} %get-tuple-element.17.map_ref, f32[48,256]{1,0:T(8,128)S(1)} %collective-permute-done.pair_ref, f32[48,256]{1,0:T(8,128)S(1)} %collective-permute-done.1.other_ref), custom_call_target="tpu_custom_call" | custom-call | flops 200000000 | bytes 1000000 | tf_op jit(solution)/shard_map/pallas_call | solution.py:462
  12.4 4.8 %all-to-all-start = ((f32[32,8,128]{2,1,0:T(8,128)}), f32[32,8,128]{2,1,0:T(8,128)S(1)}, u32[]{:S(2)}, u32[]{:S(2)}) async-start(f32[32,8,128]{2,1,0:T(8,128)} %bitcast.5), calls=%async_computation | async-start | bytes 262144 | tf_op jit(solution)/shard_map/all_to_all | solution.py:464
  17.1 4.0 %shard_map.115 = (f32[4,2,48,32,128]{4,3,2,1,0:T(8,128)S(1)}, f32[4,48,4,8,128]{4,3,2,1,0:T(8,128)S(1)}, f32[4,48,4,8,128]{4,3,2,1,0:T(8,128)S(1)}, f32[4,2,48,128]{3,2,1,0:T(8,128)S(1)}) custom-call(f32[2,48,32,512]{3,2,1,0:T(8,128)} %state_ref.1), custom_call_target="tpu_custom_call" | custom-call | flops 19660800 | bytes 6291456 | tf_op jit(solution)/shard_map/pallas_call | solution.py:371
  21.2 0.0 copy-start
  21.2 2.7 %copy-done = f32[4,2,48,32,128]{4,3,2,1,0:T(8,128)} copy-done((f32[4,2,48,32,128]{4,3,2,1,0:T(8,128)}, f32[4,2,48,32,128]{4,3,2,1,0:T(8,128)S(1)}, u32[]{:S(2)}) %copy-start) | copy-done | bytes 6291480
  23.9 0.0 copy-start.4
  23.9 1.7 %copy-done.4 = f32[4,48,4,8,128]{4,3,2,1,0:T(8,128)} copy-done((f32[4,48,4,8,128]{4,3,2,1,0:T(8,128)}, f32[4,48,4,8,128]{4,3,2,1,0:T(8,128)S(1)}, u32[]{:S(2)}) %copy-start.4) | copy-done | bytes 3145752
  25.5 0.0 copy-start.6
  25.5 0.7 %copy-done.6 = f32[4,2,48,128]{3,2,1,0:T(8,128)} copy-done((f32[4,2,48,128]{3,2,1,0:T(8,128)}, f32[4,2,48,128]{3,2,1,0:T(8,128)S(1)}, u32[]{:S(2)}) %copy-start.6) | copy-done | bytes 196632
  26.2 0.0 all-to-all-done
  26.2 0.0 copy-start.5
  26.2 1.9 %copy-done.5 = f32[4,48,4,8,128]{4,3,2,1,0:T(8,128)S(1)} copy-done((f32[4,48,4,8,128]{4,3,2,1,0:T(8,128)S(1)}, f32[4,48,4,8,128]{4,3,2,1,0:T(8,128)}, u32[]{:S(2)}) %copy-start.5) | copy-done | bytes 3145752
  28.1 0.0 copy-start.7
  28.1 0.9 %copy-done.7 = f32[4,2,48,128]{3,2,1,0:T(8,128)S(1)} copy-done((f32[4,2,48,128]{3,2,1,0:T(8,128)S(1)}, f32[4,2,48,128]{3,2,1,0:T(8,128)}, u32[]{:S(2)}) %copy-start.7) | copy-done | bytes 196632
  29.0 6.7 %shard_map.116 = (f32[4,48,4,8,128]{4,3,2,1,0:T(8,128)S(1)}, f32[4,48,128]{2,1,0:T(8,128)S(1)}, f32[4,1,128]{2,1,0:T(1,128)S(1)}, f32[256,128]{1,0:T(8,128)}, f32[4,1,128]{2,1,0:T(1,128)}) custom-call(f32[256,128]{1,0:T(8,128)S(1)} %bitcast.12, f32[4,48,4,8,128]{4,3,2,1,0:T(8,128)S(1)} %copy-done.5, f32[4,2,48,128]{3,2,1,0:T(8,128)S(1)} %copy-done.7), custom_call_target="tpu_custom_call" | custom-call | flops 23592960 | bytes 6291456 | tf_op jit(solution)/shard_map/pallas_call | solution.py:390
  35.7 0.0 copy-start.2
  35.7 1.7 %copy-done.2 = f32[4,48,4,8,128]{4,3,2,1,0:T(8,128)} copy-done((f32[4,48,4,8,128]{4,3,2,1,0:T(8,128)}, f32[4,48,4,8,128]{4,3,2,1,0:T(8,128)S(1)}, u32[]{:S(2)}) %copy-start.2) | copy-done | bytes 3145752
  37.4 5.8 %all-to-all-start.1 = ((f32[32,8,128]{2,1,0:T(8,128)}), f32[32,8,128]{2,1,0:T(8,128)S(1)}, u32[]{:S(2)}, u32[]{:S(2)}) async-start(f32[32,8,128]{2,1,0:T(8,128)} %bitcast.7), calls=%async_computation.1 | async-start | bytes 262144 | tf_op jit(solution)/shard_map/all_to_all | solution.py:466
  43.2 0.0 copy-start.1
  43.2 2.8 %copy-done.1 = f32[4,2,48,32,128]{4,3,2,1,0:T(8,128)S(1)} copy-done((f32[4,2,48,32,128]{4,3,2,1,0:T(8,128)S(1)}, f32[4,2,48,32,128]{4,3,2,1,0:T(8,128)}, u32[]{:S(2)}) %copy-start.1) | copy-done | bytes 6291480
  46.0 0.0 copy-start.3
  46.0 1.9 %copy-done.3 = f32[4,48,4,8,128]{4,3,2,1,0:T(8,128)S(1)} copy-done((f32[4,48,4,8,128]{4,3,2,1,0:T(8,128)S(1)}, f32[4,48,4,8,128]{4,3,2,1,0:T(8,128)}, u32[]{:S(2)}) %copy-start.3) | copy-done | bytes 3145752
  47.9 3.0 %shard_map.118 = f32[2,48,32,512]{3,2,1,0:T(8,128)} custom-call(f32[4,2,48,32,128]{4,3,2,1,0:T(8,128)S(1)} %copy-done.1, f32[4,48,4,8,128]{4,3,2,1,0:T(8,128)S(1)} %copy-done.3, f32[4,48,4,8,128]{4,3,2,1,0:T(8,128)S(1)} %get-tuple-element.23.linear_ref, f32[4,48,128]{2,1,0:T(8,128)S(1)} %get-tuple-element.24.row_ref, ...), custom_call_target="tpu_custom_call" | custom-call | flops 7864320 | bytes 6291456 | tf_op jit(solution)/shard_map/pallas_call | solution.py:415
  50.9 0.5 all-to-all-done.1
  51.4 2.8 %shard_map.117 = f32[576,256]{1,0:T(8,128)} custom-call(s32[1,256]{1,0:T(1,128)S(1)} %get-tuple-element.15.pos_ref, f32[256,128]{1,0:T(8,128)S(1)} %bitcast.11, f32[576,64]{1,0:T(8,128)} %constant.19.clone.weight_ref), custom_call_target="tpu_custom_call" | custom-call | flops 100000000 | bytes 1000000 | tf_op jit(solution)/shard_map/pallas_call | solution.py:468
Async XLA Ops:
  2.0 9.1 %collective-permute-start.1 = (f32[48,256]{1,0:T(8,128)S(1)}, f32[48,256]{1,0:T(8,128)S(1)}, u32[]{:S(2)}, u32[]{:S(2)}) collective-permute-start(f32[48,256]{1,0:T(8,128)S(1)} %shard_map.112.own_ref), channel_id=1, source_target_pairs={{0,31},{1,2},{2,1},{3,4},{4,3},{5,6},{6,5},{7,8},{8,7},{9,10},{10,... | collective-permute-start | bytes 147464 | tf_op jit(solution)/shard_map/ppermute | solution.py:444
  8.5 2.7 %collective-permute-start = (f32[48,256]{1,0:T(8,128)S(1)}, f32[48,256]{1,0:T(8,128)S(1)}, u32[]{:S(2)}, u32[]{:S(2)}) collective-permute-start(f32[48,256]{1,0:T(8,128)S(1)} %shard_map.112.own_ref), channel_id=1, source_target_pairs={{0,1},{1,0},{2,3},{3,2},{4,5},{5,4},{6,7},{7,6},{8,9},{9,8},{10,11... | collective-permute-start | bytes 147464 | tf_op jit(solution)/shard_map/ppermute | solution.py:443
  12.4 13.9 %all-to-all-start = ((f32[32,8,128]{2,1,0:T(8,128)}), f32[32,8,128]{2,1,0:T(8,128)S(1)}, u32[]{:S(2)}, u32[]{:S(2)}) async-start(f32[32,8,128]{2,1,0:T(8,128)} %bitcast.5), calls=%async_computation | async-start | bytes 262144 | tf_op jit(solution)/shard_map/all_to_all | solution.py:464
  21.2 2.7 %copy-start = (f32[4,2,48,32,128]{4,3,2,1,0:T(8,128)}, f32[4,2,48,32,128]{4,3,2,1,0:T(8,128)S(1)}, u32[]{:S(2)}) copy-start(f32[4,2,48,32,128]{4,3,2,1,0:T(8,128)S(1)} %get-tuple-element.21.kept_ref) | copy-start | bytes 18874372
  23.9 1.7 %copy-start.4 = (f32[4,48,4,8,128]{4,3,2,1,0:T(8,128)}, f32[4,48,4,8,128]{4,3,2,1,0:T(8,128)S(1)}, u32[]{:S(2)}) copy-start(f32[4,48,4,8,128]{4,3,2,1,0:T(8,128)S(1)} %get-tuple-element.18.first_ref) | copy-start | bytes 9437188
  25.5 0.7 %copy-start.6 = (f32[4,2,48,128]{3,2,1,0:T(8,128)}, f32[4,2,48,128]{3,2,1,0:T(8,128)S(1)}, u32[]{:S(2)}) copy-start(f32[4,2,48,128]{3,2,1,0:T(8,128)S(1)} %get-tuple-element.19.sums_ref) | copy-start | bytes 589828
  26.2 1.9 %copy-start.5 = (f32[4,48,4,8,128]{4,3,2,1,0:T(8,128)S(1)}, f32[4,48,4,8,128]{4,3,2,1,0:T(8,128)}, u32[]{:S(2)}) copy-start(f32[4,48,4,8,128]{4,3,2,1,0:T(8,128)} %copy-done.4) | copy-start | bytes 9437188
  28.1 0.9 %copy-start.7 = (f32[4,2,48,128]{3,2,1,0:T(8,128)S(1)}, f32[4,2,48,128]{3,2,1,0:T(8,128)}, u32[]{:S(2)}) copy-start(f32[4,2,48,128]{3,2,1,0:T(8,128)} %copy-done.6) | copy-start | bytes 589828
  35.7 1.7 %copy-start.2 = (f32[4,48,4,8,128]{4,3,2,1,0:T(8,128)}, f32[4,48,4,8,128]{4,3,2,1,0:T(8,128)S(1)}, u32[]{:S(2)}) copy-start(f32[4,48,4,8,128]{4,3,2,1,0:T(8,128)S(1)} %get-tuple-element.22.last_ref) | copy-start | bytes 9437188
  37.4 14.1 %all-to-all-start.1 = ((f32[32,8,128]{2,1,0:T(8,128)}), f32[32,8,128]{2,1,0:T(8,128)S(1)}, u32[]{:S(2)}, u32[]{:S(2)}) async-start(f32[32,8,128]{2,1,0:T(8,128)} %bitcast.7), calls=%async_computation.1 | async-start | bytes 262144 | tf_op jit(solution)/shard_map/all_to_all | solution.py:466
  43.2 2.8 %copy-start.1 = (f32[4,2,48,32,128]{4,3,2,1,0:T(8,128)S(1)}, f32[4,2,48,32,128]{4,3,2,1,0:T(8,128)}, u32[]{:S(2)}) copy-start(f32[4,2,48,32,128]{4,3,2,1,0:T(8,128)} %copy-done) | copy-start | bytes 18874372
  46.0 1.9 %copy-start.3 = (f32[4,48,4,8,128]{4,3,2,1,0:T(8,128)S(1)}, f32[4,48,4,8,128]{4,3,2,1,0:T(8,128)}, u32[]{:S(2)}) copy-start(f32[4,48,4,8,128]{4,3,2,1,0:T(8,128)} %copy-done.2) | copy-start | bytes 9437188

commit v3 on v2

v3 whole, which is shorter than its diff:
```python
import functools

import jax
import jax.numpy as jnp
import numpy as np
from jax import lax
from jax.experimental import pallas as pl
from jax.experimental.pallas import tpu as pltpu
from jax.sharding import PartitionSpec as P

NV = 8
STEPS = 3
AXES = ("elem", "sub")
LANES = 128
HALF = 64
LOG2E = 1.4426950408889634
F32 = jnp.float32
BF16 = jnp.bfloat16
HIGHEST = lax.Precision.HIGHEST
SMALL_RAIN = 0.2


def mixing(k):
    return (0.8 + 0.05 * k) * (1.0 if k % 2 == 0 else -1.0) / float(np.sqrt(float(NV)))


def interp(z, level, crm_levels, levels):
    position = z.astype(F32) * ((levels - 1) / (crm_levels - 1))
    return jnp.maximum(0.0, 1.0 - jnp.abs(position - level.astype(F32)))


def dot(a, b, contract, precision=None):
    return lax.dot_general(
        a, b, ((contract[0:1], contract[1:2]), ((), ())),
        precision=precision, preferred_element_type=F32,
    )


def split(x):
    high = x.astype(BF16)
    return high, (x - high.astype(F32)).astype(BF16)


def both_halves(x):
    high, low = split(x)
    return jnp.concatenate([high, low], axis=0)


def slot_rows(onehot, fields):
    product = dot(onehot, both_halves(fields), (1, 1))
    product = product + pltpu.roll(product, HALF, 1)
    rows = product.shape[0] // 2
    return jnp.where(iota((rows, 2 * HALF), 1) < HALF, product[:rows], product[rows:])


def padded(fields):
    return jnp.concatenate([fields, jnp.zeros((HALF - fields.shape[0], fields.shape[1]), F32)], axis=0)


def iota(shape, dim):
    return lax.broadcasted_iota(jnp.int32, shape, dim)


def edges_kernel(edge_ref, out_ref):
    crm_levels = out_ref.shape[0]
    shape = (crm_levels, edge_ref.shape[2])
    levels = shape[1] // 2
    lane = iota(shape, 1)
    weight = jnp.where(
        lane < levels,
        mixing(0) * interp(iota(shape, 0), lane, crm_levels, levels),
        mixing(1) * interp(iota(shape, 0), lane - levels, crm_levels, levels),
    )
    parts = [dot(weight, edge_ref[:, j, :], (1, 1), HIGHEST) for j in range(4)]
    out_ref[...] = jnp.concatenate(parts, axis=1)


def route_kernel(peers, capacity, me_ref, routes_ref, branch_ref, neigh_ref, gcm_ref, own_ref,
                 pos_ref, base_ref, halo_map_ref):
    columns = routes_ref.shape[1]
    elems = columns // 4
    crm_levels = own_ref.shape[0]
    slots = peers * capacity
    half = capacity // 2
    me = me_ref[0]
    destination = routes_ref[...]
    named = iota((peers, columns), 0) == destination
    earlier = (iota((columns, columns), 0) < iota((columns, columns), 1)).astype(BF16)
    before = dot(named.astype(BF16), earlier, (1, 0))
    rank = jnp.sum(jnp.where(named, before, 0.0), axis=0, keepdims=True).astype(jnp.int32)
    upper = (rank >= half).astype(jnp.int32)
    position = upper * (slots // 2) + destination * half + rank - upper * half
    pos_ref[...] = position
    place = (iota((slots, columns), 0) == position).astype(BF16)

    target = jnp.concatenate([neigh_ref[j : j + 1, :] for j in range(4)], axis=1)
    owner = target // columns
    edge = target - owner * columns
    block = jnp.where(owner == me, 0, jnp.where(owner == (me ^ 1), 1, 2))
    source = block * columns + (edge % 4) * elems + edge // 4
    window = iota((3 * columns, columns), 0)
    chosen = (window == source).astype(F32) + (window == iota((3 * columns, columns), 1)).astype(F32)
    column = iota((columns, columns), 0)
    row = iota((columns, columns), 1)
    first = (column % 4) * elems + column // 4
    second = ((column + 1) % 4) * elems + column // 4
    pair = ((row == first) | (row == second)).astype(BF16)
    mapped = dot(pair, chosen.astype(BF16), (1, 1)).astype(BF16)
    halo_map_ref[...] = dot(place, mapped[:, columns:], (1, 0)).astype(BF16)

    own_high, own_low = split(own_ref[...])
    local = mapped[:, :columns]
    levels = gcm_ref.shape[0] // NV
    mixed = mixing(0) * gcm_ref[:levels, :]
    for k in range(1, NV):
        mixed += mixing(k) * gcm_ref[pl.ds(k * levels, levels), :]
    shape = (crm_levels, levels)
    force = dot(interp(iota(shape, 0), iota(shape, 1), crm_levels, levels), mixed, (1, 0), HIGHEST)
    force += 0.25 * (dot(own_high, local, (1, 1)) + dot(own_low, local, (1, 1)))
    code = (branch_ref[...] + 1).astype(F32)
    base_ref[...] = slot_rows(place, padded(jnp.concatenate([force, code], axis=0)))


def outgoing_kernel(base_ref, map_ref, pair_ref, other_ref, out_ref):
    window = jnp.concatenate([pair_ref[...], other_ref[...]], axis=1)
    out_ref[...] = base_ref[...] + 0.25 * slot_rows(map_ref[...], padded(window))


def five_points(rows, z):
    row, up, down = rows[z], rows[max(z - 1, 0)], rows[min(z + 1, len(rows) - 1)]
    count = len(row)
    ring = [pltpu.roll(row[-1], 1, 0)] + row + [pltpu.roll(row[0], 7, 0)]
    pairs = [row[k] + row[k + 1] for k in range(0, count, 2)]
    return [
        (pairs[k // 2] + ring[k if k % 2 == 0 else k + 2]) + (up[k] + down[k]) for k in range(count)
    ]


def add_up(values):
    while len(values) > 1:
        values = [a + b for a, b in zip(values[::2], values[1::2])]
    return values[0]


def rows_of_sums(ref, crm_levels):
    return add_up([ref[pl.ds(s, crm_levels, stride=8), :] for s in range(8)])


def saturation(z, crm_levels):
    return 1.0 - z * (2.0 / (crm_levels - 1))


def levels_of(crm_levels):
    return iota((crm_levels, LANES), 0)


def shifted(x):
    return jnp.concatenate([x[:1], x[:-1]], axis=0) + jnp.concatenate([x[1:], x[-1:]], axis=0)


def before_kernel(state_ref, first_ref, sums_ref, kept_ref, part_ref, sems):
    blocks, _, crm_levels, width, _ = kept_ref.shape
    count = width // 8

    def copy(j):
        lanes = pl.ds(pl.multiple_of(j * LANES, LANES), LANES)
        return pltpu.make_async_copy(state_ref.at[:, :, :, lanes], kept_ref.at[j], sems.at[j])

    for j in range(blocks):
        copy(j).start()

    def block(j, _):
        copy(j).wait()
        dry = []
        for i in range(crm_levels + 1):
            if i < crm_levels:
                heat = [kept_ref[j, 0, i, pl.ds(k, 8, stride=count), :] for k in range(count)]
                moist = [kept_ref[j, 1, i, pl.ds(k, 8, stride=count), :] for k in range(count)]
                dry.append([m - 0.3 * h for h, m in zip(heat, moist)])
                part_ref[0, pl.ds(8 * i, 8), :] = add_up(dry[i])
                part_ref[1, pl.ds(8 * i, 8), :] = add_up(heat)
            if i:
                for k, total in enumerate(five_points(dry, i - 1)):
                    first_ref[j, i - 1, k] = (0.2 * LOG2E) * total
        level = saturation(levels_of(crm_levels).astype(F32), crm_levels)
        dry_mean = rows_of_sums(part_ref.at[0], crm_levels) * (1.0 / width)
        start = dry_mean + rows_of_sums(part_ref.at[1], crm_levels) * (2.3 / width)
        q = start
        for _ in range(STEPS):
            q = 0.6 * q + 0.2 * shifted(q)
        sums_ref[j, 0] = LOG2E * (dry_mean - level)
        sums_ref[j, 1] = q - start
        return 0

    lax.fori_loop(0, blocks, block, 0)


def lane_maps(rows, capacity):
    half = capacity // 2
    row = iota((rows, LANES), 0)
    slot = iota((rows, LANES), 1)
    rank = slot % capacity
    low = (row == (slot // capacity) * half + rank) & (rank < half)
    high = (row == (slot // capacity) * half + rank - half) & (rank >= half)
    return low.astype(BF16), high.astype(BF16)


def cloud_kernel(capacity, arrived_ref, first_ref, sums_ref, last_ref, row_ref, occupied_ref,
                 reply_ref, rain_ref, push_ref, part_ref, field_ref):
    blocks, crm_levels, count = first_ref.shape[:3]
    width = count * 8
    part = arrived_ref.shape[0] // blocks
    low, high = lane_maps(part, capacity)
    level = levels_of(crm_levels)
    edge = (0.4 / (crm_levels - 1)) * LOG2E
    bound = jnp.where(level == 0, -edge, 0.0) + jnp.where(level == crm_levels - 1, edge, 0.0)
    dried = LOG2E * saturation(level.astype(F32), crm_levels)
    maps = jnp.concatenate([low, high], axis=1)
    maps = jnp.concatenate([maps, maps], axis=0)
    for j in range(blocks):
        got = dot(both_halves(arrived_ref[pl.ds(j * part, part), :]), maps, (0, 0))
        got = got[:HALF, :LANES] + got[HALF:, LANES:]
        push = (-0.65 * LOG2E) * got[:crm_levels]
        push_ref[j, 0] = push - dried
        push_ref[j, 1] = push + bound
        occupied_ref[j] = got[crm_levels : crm_levels + 1]
        response = jnp.zeros((crm_levels, LANES), F32)
        for _ in range(STEPS):
            response = 0.6 * response + 0.2 * shifted(response) + 0.5 * got[:crm_levels]
        row_ref[j] = response

    def rate_of(j):
        return 0.15 + 0.25 * (occupied_ref[j] == 2.0).astype(F32)

    def lowering(j):
        return jnp.broadcast_to((1.15 * LOG2E) * rate_of(j), (8, LANES))

    def pushed(j, step, z):
        return jnp.broadcast_to(push_ref[j, min(step, 1), pl.ds(z, 1), :], (8, LANES))

    def block(j, _):
        lowered = lowering(j)
        fields = [[] for _ in range(STEPS)]
        for i in range(crm_levels + STEPS - 1):
            for t in range(STEPS):
                z = i - t
                if not 0 <= z < crm_levels:
                    continue
                push = pushed(j, t, z)
                if t == 0:
                    values = [first_ref[j, z, k] + push for k in range(count)]
                else:
                    values = [0.2 * total + push for total in five_points(fields[t - 1], z)]
                values = [y - lowered * jnp.log(1.0 + jnp.exp2(y)) for y in values]
                fields[t].append(values)
                if t == STEPS - 1:
                    for k in range(count):
                        last_ref[j, z, k] = values[k]
                    part_ref[j, pl.ds(8 * z, 8), :] = add_up(values)
        return 0

    lax.fori_loop(0, blocks, block, 0)

    def again(j):
        lowered = lowering(j)

        def condense(z, k, y, acc, store):
            e = jnp.exp2(y)
            amount = jnp.where(e < 2.0**-8, e * (1.0 - 0.5 * e), jnp.log(1.0 + e))
            store[z, k] = y - lowered * amount
            return acc + amount

        def first(z, acc):
            push = pushed(j, 0, z)
            return tuple(
                condense(z, k, first_ref[j, z, k] + push, acc[k], field_ref.at[0]) for k in range(count)
            )

        def later(source, target):
            def body(z, acc):
                push = pushed(j, 1, z)
                at = (jnp.maximum(z - 1, 0), z, jnp.minimum(z + 1, crm_levels - 1))
                totals = five_points([[source[y, k] for k in range(count)] for y in at], 1)
                return tuple(
                    condense(z, k, 0.2 * totals[k] + push, acc[k], target) for k in range(count)
                )
            return body

        def totals(z, _):
            at = pl.ds(pl.multiple_of(8 * z, 8), 8)
            part_ref[j, at, :] = add_up([last_ref[j, z, k] for k in range(count)])
            return 0

        acc = tuple(jnp.zeros((8, LANES), F32) for _ in range(count))
        acc = lax.fori_loop(0, crm_levels, first, acc)
        acc = lax.fori_loop(0, crm_levels, later(field_ref.at[0], field_ref.at[1]), acc)
        acc = lax.fori_loop(0, crm_levels, later(field_ref.at[1], last_ref.at[j]), acc)
        lax.fori_loop(0, crm_levels, totals, 0)
        mean = jnp.sum(add_up(list(acc)), axis=0, keepdims=True) * (1.0 / (crm_levels * width))
        rain_ref[j] = jnp.where(occupied_ref[j] > 0.0, rate_of(j) * mean, 0.0)

    def change(j):
        return rows_of_sums(part_ref.at[j], crm_levels) * (1.0 / width) - sums_ref[j, 0]

    for j in range(blocks):
        budget = STEPS * (push_ref[j, 1] - bound) - change(j)
        rain = jnp.sum(budget, axis=0, keepdims=True) * (1.0 / (1.15 * LOG2E * crm_levels))
        occupied = occupied_ref[j] > 0.0
        rain_ref[j] = jnp.where(occupied, rain, 0.0)
        wettest = jnp.max(jnp.where(occupied, rain / rate_of(j), -2.0))

        @pl.when((wettest > -1.0) & (wettest < SMALL_RAIN))
        def _():
            again(j)

    turned = jnp.concatenate([low, high], axis=0)
    for j in range(blocks):
        answer = (0.7 / 2.3) * (sums_ref[j, 1] + row_ref[j]) - (3.0 / (2.3 * LOG2E)) * change(j)
        reply_ref[pl.ds(j * part, part), :] = slot_rows(turned, padded(answer))


def after_kernel(state_ref, last_ref, row_ref, occupied_ref, out_ref, kept_ref, new_ref, sems, done_sems):
    blocks, _, crm_levels, width, _ = kept_ref.shape
    count = width // 8

    def lanes(j):
        return pl.ds(pl.multiple_of(j * LANES, LANES), LANES)

    def load(j):
        return pltpu.make_async_copy(state_ref.at[:, :, :, lanes(j)], kept_ref.at[j], sems.at[j])

    def store(j):
        return pltpu.make_async_copy(new_ref.at[j], out_ref.at[:, :, :, lanes(j)], done_sems.at[j])

    for j in range(blocks):
        load(j).start()

    def block(j, _):
        occupied = jnp.broadcast_to(occupied_ref[j], (8, LANES)) > 0.0
        load(j).wait()
        fields = [[] for _ in range(STEPS + 1)]
        for i in range(crm_levels + STEPS):
            if i < crm_levels:
                heat = [kept_ref[j, 0, i, pl.ds(k, 8, stride=count), :] for k in range(count)]
                moist = [kept_ref[j, 1, i, pl.ds(k, 8, stride=count), :] for k in range(count)]
                fields[0].append([(h + h) + m for h, m in zip(heat, moist)])
            for t in range(1, STEPS + 1):
                z = i - t
                if 0 <= z < crm_levels:
                    fields[t].append(five_points(fields[t - 1], z))
            if not 0 <= z < crm_levels:
                continue
            row = jnp.broadcast_to(row_ref[j, pl.ds(z, 1), :], (8, LANES))
            for k, total in enumerate(fields[STEPS][z]):
                at = pl.ds(k, 8, stride=count)
                linear = (1.0 / 125.0) * total + row
                dry = (1.0 / LOG2E) * last_ref[j, z, k] + saturation(z, crm_levels)
                heat = (1.0 / 2.3) * (linear - dry)
                moist = dry + 0.3 * heat
                new_ref[j, 0, z, at, :] = jnp.where(occupied, heat, kept_ref[j, 0, z, at, :])
                new_ref[j, 1, z, at, :] = jnp.where(occupied, moist, kept_ref[j, 1, z, at, :])
        store(j).start()
        return 0

    lax.fori_loop(0, blocks, block, 0)
    for j in range(blocks):
        store(j).wait()


def tendency_kernel(crm_levels, pos_ref, returned_ref, out_ref):
    levels = out_ref.shape[0] // NV
    rows = returned_ref.shape[0]
    columns = pos_ref.shape[1]
    place = (iota((2 * rows, columns), 0) == pos_ref[...]).astype(BF16)
    high, low = split(returned_ref[...])
    lower = dot(high, place[:rows], (0, 0)) + dot(low, place[:rows], (0, 0))
    upper = dot(high, place[rows:], (0, 0)) + dot(low, place[rows:], (0, 0))
    answer = lower[:crm_levels] + upper[HALF : HALF + crm_levels]
    shape = (levels, crm_levels)
    spread = dot(interp(iota(shape, 1), iota(shape, 0), crm_levels, levels), answer, (1, 0), HIGHEST)
    for k in range(NV):
        out_ref[pl.ds(k * levels, levels), :] = mixing(k) * spread


def call(kernel, out, scratch=(), cost=(0, 0, 0), vmem=32, **specs):
    return pl.pallas_call(
        kernel, out_shape=out, scratch_shapes=list(scratch),
        cost_estimate=pl.CostEstimate(flops=int(cost[0]), bytes_accessed=int(cost[1]), transcendentals=int(cost[2])),
        compiler_params=pltpu.CompilerParams(vmem_limit_bytes=vmem * 2**20), **specs,
    )


def from_hbm(*arrays):
    return [pltpu.with_memory_space_constraint(x, pltpu.HBM) for x in arrays]


HBM = pl.BlockSpec(memory_space=pltpu.HBM)
VMEM = pl.BlockSpec(memory_space=pltpu.VMEM)


def cloud_before(crm_state):
    _, crm_levels, width, slots = crm_state.shape
    blocks = slots // LANES
    cells = crm_levels * width * slots
    return call(
        before_kernel,
        (
            pltpu.VMEM((blocks, crm_levels, width // 8, 8, LANES), F32),
            pltpu.VMEM((blocks, 2, crm_levels, LANES), F32),
        ),
        [
            pltpu.VMEM((blocks, 2, crm_levels, width, LANES), F32),
            pltpu.VMEM((2, crm_levels * 8, LANES), F32),
            pltpu.SemaphoreType.DMA((blocks,)),
        ],
        (cells * 25, cells * 8, 0),
        in_specs=[HBM],
        out_specs=[VMEM] * 2,
    )(*from_hbm(crm_state))


def cloud_steps(capacity, arrived, first, sums):
    blocks, crm_levels, count = first.shape[:3]
    slots = blocks * LANES
    cells = crm_levels * count * 8 * slots
    return call(
        functools.partial(cloud_kernel, capacity),
        (
            pltpu.VMEM(first.shape, F32),
            pltpu.VMEM((blocks, crm_levels, LANES), F32),
            pltpu.VMEM((blocks, 1, LANES), F32),
            jax.ShapeDtypeStruct(arrived.shape, F32),
            jax.ShapeDtypeStruct((blocks, 1, LANES), F32),
        ),
        [
            pltpu.VMEM((blocks, 2, crm_levels, LANES), F32),
            pltpu.VMEM((blocks, crm_levels * 8, LANES), F32),
            pltpu.VMEM((2,) + first.shape[1:], F32),
        ],
        (cells * 30, cells * 8, cells * 6),
        in_specs=[VMEM] * 3,
        out_specs=[VMEM] * 5,
    )(arrived, first, sums)


def cloud_after(crm_state, last, row, occupied):
    _, crm_levels, width, slots = crm_state.shape
    blocks = slots // LANES
    cells = crm_levels * width * slots
    return call(
        after_kernel,
        jax.ShapeDtypeStruct(crm_state.shape, F32),
        [pltpu.VMEM((blocks, 2, crm_levels, width, LANES), F32)] * 2
        + [pltpu.SemaphoreType.DMA((blocks,))] * 2,
        (cells * 10, cells * 8, 0),
        in_specs=[HBM] + [VMEM] * 3,
        out_specs=HBM,
    )(*from_hbm(crm_state), last, row, occupied)


def on_device(gcm_state, edge_part, neighbours, branch, routes, crm_state):
    peers = lax.axis_size(AXES)
    me = lax.axis_index(AXES)
    columns, features = gcm_state.shape
    _, crm_levels, _, slots = crm_state.shape
    capacity = slots // peers
    rows = slots // 2
    shape = jax.ShapeDtypeStruct

    own = call(edges_kernel, shape((crm_levels, columns), F32), cost=(1e7, 4e5, 0))(
        *from_hbm(edge_part)
    )
    pair = lax.ppermute(own, AXES, [(i, i ^ 1) for i in range(peers)])
    other = lax.ppermute(own, AXES, [(i, (((i + 1) ^ 1) - 1) % peers) for i in range(peers)])
    position, base, halo_map = call(
        functools.partial(route_kernel, peers, capacity),
        (
            shape((1, columns), jnp.int32),
            shape((rows, LANES), F32),
            shape((slots, 2 * columns), BF16),
        ),
        cost=(2e9, 2e6, 0),
        in_specs=[pl.BlockSpec(memory_space=pltpu.SMEM)] + [VMEM] * 5,
        out_specs=[VMEM] * 3,
    )(
        me.reshape(1),
        *from_hbm(routes.T, branch.reshape(1, -1), neighbours.T, gcm_state.T),
        own,
    )
    outgoing = call(outgoing_kernel, shape((rows, LANES), F32), cost=(2e8, 1e6, 0))(base, halo_map, pair, other)
    first, sums = cloud_before(crm_state)
    arrived = lax.all_to_all(outgoing.reshape(peers, capacity // 2, LANES), AXES, 0, 0, tiled=True)
    last, row, occupied, reply, rain = cloud_steps(capacity, arrived.reshape(rows, LANES), first, sums)
    returned = lax.all_to_all(reply.reshape(peers, capacity // 2, LANES), AXES, 0, 0, tiled=True)
    updated = cloud_after(crm_state, last, row, occupied)
    tendency = call(functools.partial(tendency_kernel, crm_levels), shape((features, columns), F32), cost=(1e8, 1e6, 0))(
        position, returned.reshape(rows, LANES)
    )
    return (tendency.T, updated, rain.reshape(1, slots))


def solution(mesh):
    in_specs = (
        P(AXES, None),
        P(AXES, None, None),
        P(AXES, None),
        P(AXES),
        P(AXES, None),
        P(None, None, None, AXES),
    )
    out_specs = (
        P(AXES, None),
        P(None, None, None, AXES),
        P(AXES, None),
    )
    return jax.shard_map(
        on_device, mesh=mesh, in_specs=in_specs, out_specs=out_specs, check_vma=False
    )
```

time: 54.6 us -> 47.4 us (0.87)
  local copies, waits for them, and re-layouts: 14.2 us -> 5.15 us
  waiting for transfers between devices: 0.5 us -> 5.8 us
  Pallas kernels: 21.8 us -> 19.9 us
  starting transfers between devices: 17 us -> 15.5 us
    unnamed x16 -> x8, local copies, waits for them, and re-layouts: 14.2 us -> 5.15 us
    all_to_all x1, waiting for transfers between devices: 0.01 us -> 2.66 us  [on_device(): lax.all_to_all(outgoing.reshape(peers, capacity // 2, LANES), AXES, 0, 0,...]
    all_to_all x1, starting transfers between devices: 5.83 us -> 3.18 us  [on_device(): lax.all_to_all(reply.reshape(peers, capacity // 2, LANES), AXES, 0, 0, ti...]
    all_to_all x1, waiting for transfers between devices: 0.5 us -> 3.13 us  [on_device(): lax.all_to_all(reply.reshape(peers, capacity // 2, LANES), AXES, 0, 0, ti...]
    pallas_call x1, Pallas kernels: 6.67 us -> 5.51 us  [cloud_steps(): call(functools.partial(cloud_kernel, capacity), (pltpu.VMEM(first.shape,...]
  transfers between devices with their start and end apart: 4 -> 4, of which waited for: 1 -> 2; matrix products, arithmetic and copies ran while one was open for 0% -> 0% of each run, Pallas kernels for 18% -> 22%
where the time goes in v3:
time: 47.4 us; the launch traced here: 47 us
  Pallas kernels  19.9 us (42%)
  starting transfers between devices  15.5 us (33%)
  waiting for transfers between devices  5.8 us (12%)
  local copies, waits for them, and re-layouts  5.15 us (11%)
  between operations  0.71 us (1%)
    ppermute x1, starting transfers between devices, on_device(): lax.ppermute(own, AXES, [(i, ((i + 1 ^ 1) - 1) % peers) for i in range(pe...  6.59 us
    pallas_call x1, Pallas kernels, cloud_steps(): call(functools.partial(cloud_kernel, capacity), (pltpu.VMEM(first.shape,...  5.51 us
    all_to_all x1, starting transfers between devices, on_device(): lax.all_to_all(outgoing.reshape(peers, capacity // 2, LANES), AXES, 0, 0,...  5.2 us
    unnamed x8, local copies, waits for them, and re-layouts  5.15 us
    pallas_call x1, Pallas kernels, cloud_after(): call(after_kernel, jax.ShapeDtypeStruct(crm_state.shape, F32), [pltpu.VME...  5.09 us
    pallas_call x1, Pallas kernels, cloud_before(): call(before_kernel, (pltpu.VMEM((blocks, crm_levels, width // 8, 8, LANES...  3.22 us
    all_to_all x1, starting transfers between devices, on_device(): lax.all_to_all(reply.reshape(peers, capacity // 2, LANES), AXES, 0, 0, ti...  3.18 us
    all_to_all x1, waiting for transfers between devices, on_device(): lax.all_to_all(reply.reshape(peers, capacity // 2, LANES), AXES, 0, 0, ti...  3.13 us
  transfers between devices with their start and end apart: 4, of which 2 were waited for; matrix products, arithmetic and copies ran while one was open for 0% of the time, Pallas kernels for 22%

profile of v3, /device:TPU:0, one launch (start us, length us, event | category | flops | bytes accessed | tf_op | source)
XLA Modules:
  0.0 47.0 jit_solution(5885018904757534926)
XLA Ops:
  0.6 1.4 %shard_map.85.own_ref = f32[48,256]{1,0:T(8,128)S(1)} custom-call(f32[64,4,144]{2,1,0:T(4,128)} %edge_ref.1), custom_call_target="tpu_custom_call" | custom-call | flops 10000000 | bytes 400000 | tf_op jit(solution)/shard_map/pallas_call | solution.py:470
  2.1 0.5 %collective-permute-start = (f32[48,256]{1,0:T(8,128)S(1)}, f32[48,256]{1,0:T(8,128)S(1)}, u32[]{:S(2)}, u32[]{:S(2)}) collective-permute-start(f32[48,256]{1,0:T(8,128)S(1)} %shard_map.85.own_ref), channel_id=1, source_target_pairs={{0,1},{1,0},{2,3},{3,2},{4,5},{5,4},{6,7},{7,6},{8,9},{9,8},{10,11... | collective-permute-start | bytes 147464 | tf_op jit(solution)/shard_map/ppermute | solution.py:473
  2.6 6.6 %collective-permute-start.1 = (f32[48,256]{1,0:T(8,128)S(1)}, f32[48,256]{1,0:T(8,128)S(1)}, u32[]{:S(2)}, u32[]{:S(2)}) collective-permute-start(f32[48,256]{1,0:T(8,128)S(1)} %shard_map.85.own_ref), channel_id=1, source_target_pairs={{0,31},{1,2},{2,1},{3,4},{4,3},{5,6},{6,5},{7,8},{8,7},{9,10},{10,... | collective-permute-start | bytes 147464 | tf_op jit(solution)/shard_map/ppermute | solution.py:474
  9.2 2.2 %shard_map.86 = (s32[1,256]{1,0:T(1,128)S(1)}, f32[256,128]{1,0:T(8,128)S(1)}, bf16[512,512]{1,0:T(8,128)(2,1)S(1)}) custom-call(s32[1]{0:T(128)} %bitcast.me_ref, s32[1,256]{1,0:T(1,128)} %bitcast.16, s32[1,256]{1,0:T(1,128)} %bitcast.17, s32[4,64]{1,0:T(4,128)} %bitcast.15, f32[576,256]{1,0:T(8,128)} %bitcast.14, f32[48,256]{1,0:T(8,128)S(1)} %shard_map.85.own_ref), custom_call_target="tpu_custom_call" | custom-call | flops 2000000000 | bytes 2000000 | tf_op jit(solution)/shard_map/pallas_call | solution.py:475
  11.4 0.0 collective-permute-done.pair_ref
  11.4 0.0 collective-permute-done.1.other_ref
  11.4 1.0 %shard_map.87 = f32[256,128]{1,0:T(8,128)} custom-call(f32[256,128]{1,0:T(8,128)S(1)} %get-tuple-element.14.base_ref, bf16[512,512]{1,0:T(8,128)(2,1)S(1)} %get-tuple-element.15.map_ref, f32[48,256]{1,0:T(8,128)S(1)} %collective-permute-done.pair_ref, f32[48,256]{1,0:T(8,128)S(1)} %collective-permute-done.1.other_ref), custom_call_target="tpu_custom_call" | custom-call | flops 200000000 | bytes 1000000 | tf_op jit(solution)/shard_map/pallas_call | solution.py:490
  12.5 5.2 %all-to-all-start = ((f32[32,8,128]{2,1,0:T(8,128)}), f32[32,8,128]{2,1,0:T(8,128)S(1)}, u32[]{:S(2)}, u32[]{:S(2)}) async-start(f32[32,8,128]{2,1,0:T(8,128)} %bitcast.5), calls=%async_computation | async-start | bytes 262144 | tf_op jit(solution)/shard_map/all_to_all | solution.py:492
  17.7 3.2 %shard_map.88 = (f32[4,48,4,8,128]{4,3,2,1,0:T(8,128)S(1)}, f32[4,2,48,128]{3,2,1,0:T(8,128)S(1)}) custom-call(f32[2,48,32,512]{3,2,1,0:T(8,128)} %state_ref.3), custom_call_target="tpu_custom_call" | custom-call | flops 19660800 | bytes 6291456 | tf_op jit(solution)/shard_map/pallas_call | solution.py:405
  20.9 0.0 copy-start
  20.9 1.7 %copy-done = f32[4,48,4,8,128]{4,3,2,1,0:T(8,128)} copy-done((f32[4,48,4,8,128]{4,3,2,1,0:T(8,128)}, f32[4,48,4,8,128]{4,3,2,1,0:T(8,128)S(1)}, u32[]{:S(2)}) %copy-start) | copy-done | bytes 3145752
  22.6 0.0 copy-start.2
  22.6 0.7 %copy-done.2 = f32[4,2,48,128]{3,2,1,0:T(8,128)} copy-done((f32[4,2,48,128]{3,2,1,0:T(8,128)}, f32[4,2,48,128]{3,2,1,0:T(8,128)S(1)}, u32[]{:S(2)}) %copy-start.2) | copy-done | bytes 196632
  23.2 2.7 %all-to-all-done = f32[32,8,128]{2,1,0:T(8,128)S(1)} async-done(((f32[32,8,128]{2,1,0:T(8,128)}), f32[32,8,128]{2,1,0:T(8,128)S(1)}, u32[]{:S(2)}, u32[]{:S(2)}) %all-to-all-start) | async-done | bytes 131104 | tf_op jit(solution)/shard_map/all_to_all | solution.py:492
  25.9 0.0 copy-start.1
  25.9 1.9 %copy-done.1 = f32[4,48,4,8,128]{4,3,2,1,0:T(8,128)S(1)} copy-done((f32[4,48,4,8,128]{4,3,2,1,0:T(8,128)S(1)}, f32[4,48,4,8,128]{4,3,2,1,0:T(8,128)}, u32[]{:S(2)}) %copy-start.1) | copy-done | bytes 3145752
  27.8 0.0 copy-start.3
  27.8 0.9 %copy-done.3 = f32[4,2,48,128]{3,2,1,0:T(8,128)S(1)} copy-done((f32[4,2,48,128]{3,2,1,0:T(8,128)S(1)}, f32[4,2,48,128]{3,2,1,0:T(8,128)}, u32[]{:S(2)}) %copy-start.3) | copy-done | bytes 196632
  28.7 5.5 %shard_map.89 = (f32[4,48,4,8,128]{4,3,2,1,0:T(8,128)S(1)}, f32[4,48,128]{2,1,0:T(8,128)S(1)}, f32[4,1,128]{2,1,0:T(1,128)S(1)}, f32[256,128]{1,0:T(8,128)}, f32[4,1,128]{2,1,0:T(1,128)}) custom-call(f32[256,128]{1,0:T(8,128)S(1)} %bitcast.12, f32[4,48,4,8,128]{4,3,2,1,0:T(8,128)S(1)} %copy-done.1, f32[4,2,48,128]{3,2,1,0:T(8,128)S(1)} %copy-done.3), custom_call_target="tpu_custom_call" | custom-call | flops 23592960 | bytes 6291456 | tf_op jit(solution)/shard_map/pallas_call | solution.py:426
  34.2 3.2 %all-to-all-start.1 = ((f32[32,8,128]{2,1,0:T(8,128)}), f32[32,8,128]{2,1,0:T(8,128)S(1)}, u32[]{:S(2)}, u32[]{:S(2)}) async-start(f32[32,8,128]{2,1,0:T(8,128)} %bitcast.7), calls=%async_computation.1 | async-start | bytes 262144 | tf_op jit(solution)/shard_map/all_to_all | solution.py:494
  37.4 5.1 %shard_map.91 = f32[2,48,32,512]{3,2,1,0:T(8,128)} custom-call(f32[2,48,32,512]{3,2,1,0:T(8,128)} %state_ref.3, f32[4,48,4,8,128]{4,3,2,1,0:T(8,128)S(1)} %get-tuple-element.19.last_ref, f32[4,48,128]{2,1,0:T(8,128)S(1)} %get-tuple-element.20.row_ref, f32[4,1,128]{2,1,0:T(1,128)S(1)} %get-tuple-element.21.occupied_ref), custom_call_target="tpu_custom_call" | custom-call | flops 7864320 | bytes 6291456 | tf_op jit(solution)/shard_map/pallas_call | solution.py:450
  42.5 3.1 %all-to-all-done.1 = f32[32,8,128]{2,1,0:T(8,128)S(1)} async-done(((f32[32,8,128]{2,1,0:T(8,128)}), f32[32,8,128]{2,1,0:T(8,128)S(1)}, u32[]{:S(2)}, u32[]{:S(2)}) %all-to-all-start.1) | async-done | bytes 131104 | tf_op jit(solution)/shard_map/all_to_all | solution.py:494
  45.6 1.4 %shard_map.90 = f32[576,256]{1,0:T(8,128)} custom-call(s32[1,256]{1,0:T(1,128)S(1)} %get-tuple-element.13.pos_ref, f32[256,128]{1,0:T(8,128)S(1)} %bitcast.11), custom_call_target="tpu_custom_call" | custom-call | flops 100000000 | bytes 1000000 | tf_op jit(solution)/shard_map/pallas_call | solution.py:496
Async XLA Ops:
  2.1 9.4 %collective-permute-start = (f32[48,256]{1,0:T(8,128)S(1)}, f32[48,256]{1,0:T(8,128)S(1)}, u32[]{:S(2)}, u32[]{:S(2)}) collective-permute-start(f32[48,256]{1,0:T(8,128)S(1)} %shard_map.85.own_ref), channel_id=1, source_target_pairs={{0,1},{1,0},{2,3},{3,2},{4,5},{5,4},{6,7},{7,6},{8,9},{9,8},{10,11... | collective-permute-start | bytes 147464 | tf_op jit(solution)/shard_map/ppermute | solution.py:473
  2.6 8.9 %collective-permute-start.1 = (f32[48,256]{1,0:T(8,128)S(1)}, f32[48,256]{1,0:T(8,128)S(1)}, u32[]{:S(2)}, u32[]{:S(2)}) collective-permute-start(f32[48,256]{1,0:T(8,128)S(1)} %shard_map.85.own_ref), channel_id=1, source_target_pairs={{0,31},{1,2},{2,1},{3,4},{4,3},{5,6},{6,5},{7,8},{8,7},{9,10},{10,... | collective-permute-start | bytes 147464 | tf_op jit(solution)/shard_map/ppermute | solution.py:474
  12.5 13.4 %all-to-all-start = ((f32[32,8,128]{2,1,0:T(8,128)}), f32[32,8,128]{2,1,0:T(8,128)S(1)}, u32[]{:S(2)}, u32[]{:S(2)}) async-start(f32[32,8,128]{2,1,0:T(8,128)} %bitcast.5), calls=%async_computation | async-start | bytes 262144 | tf_op jit(solution)/shard_map/all_to_all | solution.py:492
  20.9 1.7 %copy-start = (f32[4,48,4,8,128]{4,3,2,1,0:T(8,128)}, f32[4,48,4,8,128]{4,3,2,1,0:T(8,128)S(1)}, u32[]{:S(2)}) copy-start(f32[4,48,4,8,128]{4,3,2,1,0:T(8,128)S(1)} %get-tuple-element.16.first_ref) | copy-start | bytes 9437188
  22.6 0.7 %copy-start.2 = (f32[4,2,48,128]{3,2,1,0:T(8,128)}, f32[4,2,48,128]{3,2,1,0:T(8,128)S(1)}, u32[]{:S(2)}) copy-start(f32[4,2,48,128]{3,2,1,0:T(8,128)S(1)} %get-tuple-element.17.sums_ref) | copy-start | bytes 589828
  25.9 1.9 %copy-start.1 = (f32[4,48,4,8,128]{4,3,2,1,0:T(8,128)S(1)}, f32[4,48,4,8,128]{4,3,2,1,0:T(8,128)}, u32[]{:S(2)}) copy-start(f32[4,48,4,8,128]{4,3,2,1,0:T(8,128)} %copy-done) | copy-start | bytes 9437188
  27.8 0.9 %copy-start.3 = (f32[4,2,48,128]{3,2,1,0:T(8,128)S(1)}, f32[4,2,48,128]{3,2,1,0:T(8,128)}, u32[]{:S(2)}) copy-start(f32[4,2,48,128]{3,2,1,0:T(8,128)} %copy-done.2) | copy-start | bytes 589828
  34.2 11.4 %all-to-all-start.1 = ((f32[32,8,128]{2,1,0:T(8,128)}), f32[32,8,128]{2,1,0:T(8,128)S(1)}, u32[]{:S(2)}, u32[]{:S(2)}) async-start(f32[32,8,128]{2,1,0:T(8,128)} %bitcast.7), calls=%async_computation.1 | async-start | bytes 262144 | tf_op jit(solution)/shard_map/all_to_all | solution.py:494

commit v4 on v3

v4 whole, which is shorter than its diff:
```python
import functools

import jax
import jax.numpy as jnp
import numpy as np
from jax import lax
from jax.experimental import pallas as pl
from jax.experimental.pallas import tpu as pltpu
from jax.sharding import PartitionSpec as P

NV = 8
STEPS = 3
AXES = ("elem", "sub")
LANES = 128
HALF = 64
LOG2E = 1.4426950408889634
F32 = jnp.float32
BF16 = jnp.bfloat16
HIGHEST = lax.Precision.HIGHEST
SMALL_RAIN = 0.2


def mixing(k):
    return (0.8 + 0.05 * k) * (1.0 if k % 2 == 0 else -1.0) / float(np.sqrt(float(NV)))


def interp(z, level, crm_levels, levels):
    position = z.astype(F32) * ((levels - 1) / (crm_levels - 1))
    return jnp.maximum(0.0, 1.0 - jnp.abs(position - level.astype(F32)))


def dot(a, b, contract, precision=None):
    return lax.dot_general(
        a, b, ((contract[0:1], contract[1:2]), ((), ())),
        precision=precision, preferred_element_type=F32,
    )


def split(x):
    high = x.astype(BF16)
    return high, (x - high.astype(F32)).astype(BF16)


def both_halves(x):
    high, low = split(x)
    return jnp.concatenate([high, low], axis=0)


def slot_rows(onehot, fields):
    product = dot(onehot, both_halves(fields), (1, 1))
    product = product + pltpu.roll(product, HALF, 1)
    rows = product.shape[0] // 2
    return jnp.where(iota((rows, 2 * HALF), 1) < HALF, product[:rows], product[rows:])


def padded(fields):
    return jnp.concatenate([fields, jnp.zeros((HALF - fields.shape[0], fields.shape[1]), F32)], axis=0)


def iota(shape, dim):
    return lax.broadcasted_iota(jnp.int32, shape, dim)


def edges_kernel(edge_ref, out_ref):
    crm_levels = out_ref.shape[0]
    shape = (crm_levels, edge_ref.shape[2])
    levels = shape[1] // 2
    lane = iota(shape, 1)
    weight = jnp.where(
        lane < levels,
        mixing(0) * interp(iota(shape, 0), lane, crm_levels, levels),
        mixing(1) * interp(iota(shape, 0), lane - levels, crm_levels, levels),
    )
    out_ref[...] = dot(weight, edge_ref[...].reshape(-1, shape[1]), (1, 1), HIGHEST)


def route_kernel(peers, capacity, me_ref, routes_ref, branch_ref, neigh_ref, gcm_ref, own_ref, pair_ref,
                 pos_ref, base_ref, halo_map_ref):
    columns = routes_ref.shape[1]
    elems = columns // 4
    crm_levels = own_ref.shape[0]
    slots = peers * capacity
    half = capacity // 2
    me = me_ref[0]
    destination = routes_ref[...]
    named = iota((peers, columns), 0) == destination
    earlier = (iota((columns, columns), 0) < iota((columns, columns), 1)).astype(BF16)
    before = dot(named.astype(BF16), earlier, (1, 0))
    rank = jnp.sum(jnp.where(named, before, 0.0), axis=0, keepdims=True).astype(jnp.int32)
    upper = (rank >= half).astype(jnp.int32)
    position = upper * (slots // 2) + destination * half + rank - upper * half
    pos_ref[...] = position
    place = (iota((slots, columns), 0) == position).astype(BF16)

    target = jnp.concatenate([neigh_ref[j : j + 1, :] for j in range(4)], axis=1)
    owner = target // columns
    edge = target - owner * columns
    block = jnp.where(owner == me, 0, jnp.where(owner == (me ^ 1), 1, 2))
    source = block * columns + edge
    window = iota((3 * columns, columns), 0)
    local = iota((1, columns), 1)
    local = 4 * (local % elems) + local // elems
    chosen = (window == source).astype(F32) + (window == local).astype(F32)
    column = iota((columns, columns), 0)
    row = iota((columns, columns), 1)
    first = (column % 4) * elems + column // 4
    second = ((column + 1) % 4) * elems + column // 4
    pair = ((row == first) | (row == second)).astype(BF16)
    mapped = dot(pair, chosen.astype(BF16), (1, 1)).astype(BF16)
    halo_map_ref[...] = dot(place, mapped[:, 2 * columns :], (1, 0)).astype(BF16)

    near = jnp.concatenate([own_ref[...], pair_ref[...]], axis=1)
    levels = gcm_ref.shape[0] // NV
    mixed = mixing(0) * gcm_ref[:levels, :]
    for k in range(1, NV):
        mixed += mixing(k) * gcm_ref[pl.ds(k * levels, levels), :]
    shape = (crm_levels, levels)
    force = dot(interp(iota(shape, 0), iota(shape, 1), crm_levels, levels), mixed, (1, 0), HIGHEST)
    for part in split(near):
        force += 0.25 * dot(part, mapped[:, : 2 * columns], (1, 1))
    code = (branch_ref[...] + 1).astype(F32)
    base_ref[...] = slot_rows(place, padded(jnp.concatenate([force, code], axis=0)))


def outgoing_kernel(base_ref, map_ref, other_ref, out_ref):
    out_ref[...] = base_ref[...] + 0.25 * slot_rows(map_ref[...], padded(other_ref[...]))


class Field:
    def __init__(self, total):
        self.total, self.rows, self.diagonals = total, [], []

    def five(self, z):
        while len(self.diagonals) < z + 2:
            at = len(self.diagonals)
            below, here = self.rows[max(at - 1, 0)], self.rows[min(at, self.total - 1)]
            right = here[1:] + [pltpu.roll(here[0], 7, 0)]
            self.diagonals.append([a + b for a, b in zip(below, right)])
        low, high = self.diagonals[z], self.diagonals[z + 1]
        high = [pltpu.roll(high[-1], 1, 0)] + high[:-1]
        return [row + (a + b) for row, a, b in zip(self.rows[z], low, high)]


def five_points(row, up, down):
    left = [pltpu.roll(row[-1], 1, 0)] + row[:-1]
    right = row[1:] + [pltpu.roll(row[0], 7, 0)]
    return [(a + b + c) + (d + e) for a, b, c, d, e in zip(row, left, right, up, down)]


def add_up(values):
    while len(values) > 1:
        values = [a + b for a, b in zip(values[::2], values[1::2])]
    return values[0]


def rows_of_sums(ref, crm_levels):
    return add_up([ref[pl.ds(s, crm_levels, stride=8), :] for s in range(8)])


def saturation(z, crm_levels):
    return 1.0 - z * (2.0 / (crm_levels - 1))


def levels_of(crm_levels):
    return iota((crm_levels, LANES), 0)


def shifted(x):
    return jnp.concatenate([x[:1], x[:-1]], axis=0) + jnp.concatenate([x[1:], x[-1:]], axis=0)


def before_kernel(state_ref, first_ref, sums_ref, kept_ref, part_ref, kept_sums_ref, new_ref, sems, done_sems):
    blocks, _, crm_levels, width, _ = kept_ref.shape
    count = width // 8

    def copy(j):
        lanes = pl.ds(pl.multiple_of(j * LANES, LANES), LANES)
        return pltpu.make_async_copy(state_ref.at[:, :, :, lanes], kept_ref.at[j], sems.at[j])

    def done(j):
        return pltpu.make_async_copy(new_ref.at[j], first_ref.at[j], done_sems.at[j])

    for j in range(blocks):
        copy(j).start()

    def block(j, _):
        copy(j).wait()
        dry = Field(crm_levels)
        for i in range(crm_levels + 1):
            if i < crm_levels:
                heat = [kept_ref[j, 0, i, pl.ds(k, 8, stride=count), :] for k in range(count)]
                moist = [kept_ref[j, 1, i, pl.ds(k, 8, stride=count), :] for k in range(count)]
                dry.rows.append([m - 0.3 * h for h, m in zip(heat, moist)])
                part_ref[0, pl.ds(8 * i, 8), :] = add_up(dry.rows[i])
                part_ref[1, pl.ds(8 * i, 8), :] = add_up(heat)
            if i:
                for k, total in enumerate(dry.five(i - 1)):
                    new_ref[j, i - 1, k] = (0.2 * LOG2E) * total
        done(j).start()
        level = saturation(levels_of(crm_levels).astype(F32), crm_levels)
        dry_mean = rows_of_sums(part_ref.at[0], crm_levels) * (1.0 / width)
        start = dry_mean + rows_of_sums(part_ref.at[1], crm_levels) * (2.3 / width)
        q = start
        for _ in range(STEPS):
            q = 0.6 * q + 0.2 * shifted(q)
        kept_sums_ref[j, 0] = LOG2E * (dry_mean - level)
        kept_sums_ref[j, 1] = q - start
        return 0

    lax.fori_loop(0, blocks, block, 0)
    sums = pltpu.make_async_copy(kept_sums_ref, sums_ref, done_sems.at[blocks])
    sums.start()
    for j in range(blocks):
        done(j).wait()
    sums.wait()


def lane_maps(rows, capacity):
    half = capacity // 2
    row = iota((rows, LANES), 0)
    slot = iota((rows, LANES), 1)
    rank = slot % capacity
    low = (row == (slot // capacity) * half + rank) & (rank < half)
    high = (row == (slot // capacity) * half + rank - half) & (rank >= half)
    return low.astype(BF16), high.astype(BF16)


def bounds(crm_levels):
    level = levels_of(crm_levels)
    edge = (0.4 / (crm_levels - 1)) * LOG2E
    return jnp.where(level == 0, -edge, 0.0) + jnp.where(level == crm_levels - 1, edge, 0.0)


def dried(crm_levels):
    return LOG2E * saturation(levels_of(crm_levels).astype(F32), crm_levels)


def respond(force):
    q = jnp.zeros_like(force)
    for _ in range(STEPS):
        q = 0.6 * q + 0.2 * shifted(q) + 0.5 * force
    return q


def rate_of(code):
    return 0.15 + 0.25 * (code == 2.0).astype(F32)


def cloud_kernel(capacity, arrived_ref, far_ref, far_sums_ref, last_ref, force_ref, code_ref, rain_ref,
                 reply_ref, push_ref, part_ref, sums_ref, first_ref, sems):
    blocks, crm_levels, count = last_ref.shape[:3]
    width = count * 8
    part = arrived_ref.shape[0] // blocks

    def load(j):
        return pltpu.make_async_copy(far_ref.at[j], first_ref.at[j], sems.at[j])

    load_sums = pltpu.make_async_copy(far_sums_ref, sums_ref, sems.at[blocks])
    for j in range(blocks):
        load(j).start()
    load_sums.start()
    low, high = lane_maps(part, capacity)
    maps = jnp.concatenate([low, high], axis=1)
    maps = jnp.concatenate([maps, maps], axis=0)
    for j in range(blocks):
        got = dot(both_halves(arrived_ref[pl.ds(j * part, part), :]), maps, (0, 0))
        got = got[:HALF, :LANES] + got[HALF:, LANES:]
        push = (-0.65 * LOG2E) * got[:crm_levels]
        push_ref[j, 0] = push - dried(crm_levels)
        push_ref[j, 1] = push + bounds(crm_levels)
        force_ref[j] = got[:crm_levels]
        code_ref[j] = got[crm_levels : crm_levels + 1]

    def block(j, _):
        load(j).wait()
        lowered = jnp.broadcast_to((1.15 * LOG2E) * rate_of(code_ref[j]), (8, LANES))
        fields = [Field(crm_levels) for _ in range(STEPS)]
        for i in range(crm_levels + STEPS - 1):
            for t in range(STEPS):
                z = i - t
                if not 0 <= z < crm_levels:
                    continue
                push = jnp.broadcast_to(push_ref[j, min(t, 1), pl.ds(z, 1), :], (8, LANES))
                if t == 0:
                    values = [first_ref[j, z, k] + push for k in range(count)]
                else:
                    values = [0.2 * total + push for total in fields[t - 1].five(z)]
                values = [y - lowered * jnp.log(1.0 + jnp.exp2(y)) for y in values]
                fields[t].rows.append(values)
                if t == STEPS - 1:
                    for k in range(count):
                        last_ref[j, z, k] = values[k]
                    part_ref[j, pl.ds(8 * z, 8), :] = add_up(values)
        return 0

    lax.fori_loop(0, blocks, block, 0)
    load_sums.wait()
    turned = jnp.concatenate([low, high], axis=0)
    for j in range(blocks):
        dg = rows_of_sums(part_ref.at[j], crm_levels) * (1.0 / width) - sums_ref[j, 0]
        answer = (0.7 / 2.3) * (sums_ref[j, 1] + respond(force_ref[j])) - (3.0 / (2.3 * LOG2E)) * dg
        reply_ref[pl.ds(j * part, part), :] = slot_rows(turned, padded(answer))
        budget = (-0.65 * LOG2E * STEPS) * force_ref[j] - dg
        rain = jnp.sum(budget, axis=0, keepdims=True) * (1.0 / (1.15 * LOG2E * crm_levels))
        rain_ref[j] = jnp.where(code_ref[j] > 0.0, rain, 0.0)


def after_kernel(state_ref, last_ref, force_ref, code_ref, guess_ref, out_ref, rain_ref,
                 kept_ref, new_ref, row_ref, push_ref, field_ref, sems, done_sems):
    blocks, _, crm_levels, width, _ = kept_ref.shape
    count = width // 8
    pieces = sems.shape[1]
    piece = crm_levels // pieces

    def lanes(j):
        return pl.ds(pl.multiple_of(j * LANES, LANES), LANES)

    def load(j, p):
        at = pl.ds(p * piece, piece)
        return pltpu.make_async_copy(
            state_ref.at[:, at, :, lanes(j)], kept_ref.at[j, :, at, :, :], sems.at[j, p]
        )

    def store(j, p):
        at = pl.ds(p * piece, piece)
        return pltpu.make_async_copy(
            new_ref.at[j, :, at, :, :], out_ref.at[:, at, :, lanes(j)], done_sems.at[j, p]
        )

    for j in range(blocks):
        for p in range(pieces):
            load(j, p).start()
    rain_ref[...] = guess_ref[...]
    for j in range(blocks):
        row_ref[j] = respond(force_ref[j])
    rows = [guess_ref[j] / rate_of(code_ref[j]) for j in range(blocks)]
    marks = [jnp.where(code_ref[j] > 0.0, row, -2.0) for j, row in enumerate(rows)]
    wettest = [jnp.max(mark, axis=1, keepdims=True) for mark in marks]
    dry = [((w > -1.0) & (w < SMALL_RAIN)).astype(jnp.int32) for w in wettest]
    some_dry = jnp.max(functools.reduce(jnp.maximum, dry)) > 0

    def block(j, _):
        occupied = jnp.broadcast_to(code_ref[j], (8, LANES)) > 0.0
        fields = [Field(crm_levels) for _ in range(STEPS + 1)]
        for i in range(crm_levels + STEPS):
            if i < crm_levels:
                if i % piece == 0:
                    load(j, i // piece).wait()
                heat = [kept_ref[j, 0, i, pl.ds(k, 8, stride=count), :] for k in range(count)]
                moist = [kept_ref[j, 1, i, pl.ds(k, 8, stride=count), :] for k in range(count)]
                fields[0].rows.append([(h + h) + m for h, m in zip(heat, moist)])
            for t in range(1, STEPS + 1):
                z = i - t
                if 0 <= z < crm_levels:
                    fields[t].rows.append(fields[t - 1].five(z))
            if not 0 <= z < crm_levels:
                continue
            row = jnp.broadcast_to(row_ref[j, pl.ds(z, 1), :], (8, LANES))
            for k, total in enumerate(fields[STEPS].rows[z]):
                at = pl.ds(k, 8, stride=count)
                linear = (1.0 / 125.0) * total + row
                dry = (1.0 / LOG2E) * last_ref[j, z, k] + saturation(z, crm_levels)
                heat = (1.0 / 2.3) * (linear - dry)
                moist = dry + 0.3 * heat
                new_ref[j, 0, z, at, :] = jnp.where(occupied, heat, kept_ref[j, 0, z, at, :])
                new_ref[j, 1, z, at, :] = jnp.where(occupied, moist, kept_ref[j, 1, z, at, :])
            if z % piece == piece - 1:
                store(j, z // piece).start()
        return 0

    lax.fori_loop(0, blocks, block, 0)

    def again(j, _):
        rate = rate_of(code_ref[j])
        lowered = jnp.broadcast_to((1.15 * LOG2E) * rate, (8, LANES))
        push = (-0.65 * LOG2E) * force_ref[j]
        push_ref[0] = push - dried(crm_levels)
        push_ref[1] = push + bounds(crm_levels)

        def condense(y, acc):
            e = jnp.exp2(y)
            amount = jnp.where(e < 2.0**-8, e * (1.0 - 0.5 * e), jnp.log(1.0 + e))
            return y - lowered * amount, acc + amount

        def start(z, _):
            for k in range(count):
                at = pl.ds(k, 8, stride=count)
                field_ref[0, z, k] = LOG2E * (kept_ref[j, 1, z, at, :] - 0.3 * kept_ref[j, 0, z, at, :])
            return 0

        def step(source, target, which):
            def body(z, acc):
                push = jnp.broadcast_to(push_ref[which, pl.ds(z, 1), :], (8, LANES))
                at = (z, jnp.maximum(z - 1, 0), jnp.minimum(z + 1, crm_levels - 1))
                totals = five_points(*[[field_ref[source, y, k] for k in range(count)] for y in at])
                new = []
                for k in range(count):
                    field_ref[target, z, k], total = condense(0.2 * totals[k] + push, acc[k])
                    new.append(total)
                return tuple(new)
            return body

        acc = tuple(jnp.zeros((8, LANES), F32) for _ in range(count))
        lax.fori_loop(0, crm_levels, start, 0)
        for t in range(STEPS):
            acc = lax.fori_loop(0, crm_levels, step(t % 2, (t + 1) % 2, min(t, 1)), acc)
        mean = jnp.sum(add_up(list(acc)), axis=0, keepdims=True) * (1.0 / (crm_levels * width))
        rain_ref[j] = jnp.where(code_ref[j] > 0.0, rate * mean, 0.0)
        return 0

    @pl.when(some_dry)
    def _():
        lax.fori_loop(0, blocks, again, 0)

    for j in range(blocks):
        for p in range(pieces):
            store(j, p).wait()


def tendency_kernel(crm_levels, pos_ref, returned_ref, out_ref, new_ref, sems):
    levels = out_ref.shape[0] // NV
    rows = returned_ref.shape[0]
    columns = pos_ref.shape[1]
    place = (iota((2 * rows, columns), 0) == pos_ref[...]).astype(BF16)
    high, low = split(returned_ref[...])
    lower = dot(high, place[:rows], (0, 0)) + dot(low, place[:rows], (0, 0))
    upper = dot(high, place[rows:], (0, 0)) + dot(low, place[rows:], (0, 0))
    answer = lower[:crm_levels] + upper[HALF : HALF + crm_levels]
    shape = (levels, crm_levels)
    spread = dot(interp(iota(shape, 1), iota(shape, 0), crm_levels, levels), answer, (1, 0), HIGHEST)
    copies = []
    for k in range(NV):
        new_ref[k] = mixing(k) * spread
        copies.append(
            pltpu.make_async_copy(new_ref.at[k], out_ref.at[pl.ds(k * levels, levels), :], sems.at[k])
        )
        copies[k].start()
    for copy in copies:
        copy.wait()


def call(kernel, out, scratch=(), cost=(0, 0, 0), vmem=32, **specs):
    return pl.pallas_call(
        kernel, out_shape=out, scratch_shapes=list(scratch),
        cost_estimate=pl.CostEstimate(flops=int(cost[0]), bytes_accessed=int(cost[1]), transcendentals=int(cost[2])),
        compiler_params=pltpu.CompilerParams(vmem_limit_bytes=vmem * 2**20), **specs,
    )


def from_hbm(*arrays):
    return [pltpu.with_memory_space_constraint(x, pltpu.HBM) for x in arrays]


HBM = pl.BlockSpec(memory_space=pltpu.HBM)
VMEM = pl.BlockSpec(memory_space=pltpu.VMEM)


def cloud_before(crm_state):
    _, crm_levels, width, slots = crm_state.shape
    blocks = slots // LANES
    cells = crm_levels * width * slots
    field = (blocks, crm_levels, width // 8, 8, LANES)
    sums = (blocks, 2, crm_levels, LANES)
    return call(
        before_kernel,
        (pltpu.HBM(field, F32), pltpu.HBM(sums, F32)),
        [
            pltpu.VMEM((blocks, 2, crm_levels, width, LANES), F32),
            pltpu.VMEM((2, crm_levels * 8, LANES), F32),
            pltpu.VMEM(sums, F32),
            pltpu.VMEM(field, F32),
            pltpu.SemaphoreType.DMA((blocks,)),
            pltpu.SemaphoreType.DMA((blocks + 1,)),
        ],
        (cells * 25, cells * 8, 0),
        in_specs=[HBM],
        out_specs=[HBM] * 2,
    )(*from_hbm(crm_state))


def cloud_steps(capacity, arrived, first, sums):
    blocks, _, crm_levels, _ = sums.shape
    slots = blocks * LANES
    cells = crm_levels * first.shape[2] * 8 * slots
    return call(
        functools.partial(cloud_kernel, capacity),
        (
            pltpu.VMEM(first.shape, F32),
            pltpu.VMEM((blocks, crm_levels, LANES), F32),
            pltpu.VMEM((blocks, 1, LANES), F32),
            pltpu.VMEM((blocks, 1, LANES), F32),
            jax.ShapeDtypeStruct(arrived.shape, F32),
        ),
        [
            pltpu.VMEM(sums.shape, F32),
            pltpu.VMEM((blocks, crm_levels * 8, LANES), F32),
            pltpu.VMEM(sums.shape, F32),
            pltpu.VMEM(first.shape, F32),
            pltpu.SemaphoreType.DMA((blocks + 1,)),
        ],
        (cells * 30, cells * 8, cells * 6),
        in_specs=[VMEM, HBM, HBM],
        out_specs=[VMEM] * 5,
    )(arrived, *from_hbm(first, sums))


def cloud_after(crm_state, last, force, code, rain):
    _, crm_levels, width, slots = crm_state.shape
    blocks = slots // LANES
    pieces = 1
    cells = crm_levels * width * slots
    return call(
        after_kernel,
        (jax.ShapeDtypeStruct(crm_state.shape, F32), jax.ShapeDtypeStruct((blocks, 1, LANES), F32)),
        [pltpu.VMEM((blocks, 2, crm_levels, width, LANES), F32)] * 2
        + [
            pltpu.VMEM((blocks, crm_levels, LANES), F32),
            pltpu.VMEM((2, crm_levels, LANES), F32),
            pltpu.VMEM((2,) + last.shape[1:], F32),
        ]
        + [pltpu.SemaphoreType.DMA((blocks, pieces))] * 2,
        (cells * 10, cells * 8, 0),
        in_specs=[HBM] + [VMEM] * 4,
        out_specs=[HBM, VMEM],
    )(*from_hbm(crm_state), last, force, code, rain)


def on_device(gcm_state, edge_part, neighbours, branch, routes, crm_state):
    peers = lax.axis_size(AXES)
    me = lax.axis_index(AXES)
    columns, features = gcm_state.shape
    _, crm_levels, _, slots = crm_state.shape
    capacity = slots // peers
    rows = slots // 2
    shape = jax.ShapeDtypeStruct

    own = call(edges_kernel, shape((crm_levels, columns), F32), cost=(1e7, 4e5, 0))(
        *from_hbm(edge_part)
    )
    other = lax.ppermute(own, AXES, [(i, (((i + 1) ^ 1) - 1) % peers) for i in range(peers)])
    pair = lax.ppermute(own, AXES, [(i, i ^ 1) for i in range(peers)])
    position, base, halo_map = call(
        functools.partial(route_kernel, peers, capacity),
        (
            shape((1, columns), jnp.int32),
            shape((rows, LANES), F32),
            shape((slots, columns), BF16),
        ),
        cost=(2e9, 2e6, 0),
        in_specs=[pl.BlockSpec(memory_space=pltpu.SMEM)] + [VMEM] * 6,
        out_specs=[VMEM] * 3,
    )(
        me.reshape(1),
        *from_hbm(routes.T, branch.reshape(1, -1), neighbours.T, gcm_state.T),
        own,
        pair,
    )
    outgoing = call(outgoing_kernel, shape((rows, LANES), F32), cost=(2e8, 1e6, 0))(base, halo_map, other)
    first, sums = cloud_before(crm_state)
    arrived = lax.all_to_all(outgoing.reshape(peers, capacity // 2, LANES), AXES, 0, 0, tiled=True)
    last, force, code, rain, reply = cloud_steps(capacity, arrived.reshape(rows, LANES), first, sums)
    returned = lax.all_to_all(reply.reshape(peers, capacity // 2, LANES), AXES, 0, 0, tiled=True)
    updated, rain = cloud_after(crm_state, last, force, code, rain)
    levels = features // NV
    tendency = call(
        functools.partial(tendency_kernel, crm_levels),
        shape((features, columns), F32),
        [pltpu.VMEM((NV, levels, columns), F32), pltpu.SemaphoreType.DMA((NV,))],
        (1e8, 1e6, 0),
        in_specs=[VMEM] * 2,
        out_specs=HBM,
    )(position, returned.reshape(rows, LANES))
    return (tendency.T, updated, rain.reshape(1, slots))


def solution(mesh):
    in_specs = (
        P(AXES, None),
        P(AXES, None, None),
        P(AXES, None),
        P(AXES),
        P(AXES, None),
        P(None, None, None, AXES),
    )
    out_specs = (
        P(AXES, None),
        P(None, None, None, AXES),
        P(AXES, None),
    )
    return jax.shard_map(
        on_device, mesh=mesh, in_specs=in_specs, out_specs=out_specs, check_vma=False
    )
```

time: 47.4 us -> 43.9 us (0.926)
  local copies, waits for them, and re-layouts: 5.15 us -> 0 us
  Pallas kernels: 19.9 us -> 21.8 us
  starting transfers between devices: 15.5 us -> 14.9 us
    unnamed x8 -> x0, local copies, waits for them, and re-layouts: 5.15 us -> none
    pallas_call x2, Pallas kernels: 8.31 us -> 10.2 us  [the longest x1 5.55 us: cloud_after(): call(after_kernel, (jax.ShapeDtypeStruct(crm_state.shape, F32), jax.Shape...]
    all_to_all x1, waiting for transfers between devices: 2.66 us -> 3.57 us  [on_device(): lax.all_to_all(outgoing.reshape(peers, capacity // 2, LANES), AXES, 0, 0,...]
    all_to_all x1, starting transfers between devices: 3.18 us -> 2.57 us  [on_device(): lax.all_to_all(reply.reshape(peers, capacity // 2, LANES), AXES, 0, 0, ti...]
  transfers between devices with their start and end apart: 4 -> 4, of which waited for: 2 -> 2; matrix products, arithmetic and copies ran while one was open for 0% -> 0% of each run, Pallas kernels for 22% -> 29%
where the time goes in v4:
time: 43.9 us; the launch traced here: 43.6 us
  Pallas kernels  21.8 us (50%)
  starting transfers between devices  14.9 us (34%)
  waiting for transfers between devices  6.25 us (14%)
  between operations  0.7 us (2%)
    ppermute x1, starting transfers between devices, on_device(): lax.ppermute(own, AXES, [(i, ((i + 1 ^ 1) - 1) % peers) for i in range(pe...  6.59 us
    pallas_call x1, Pallas kernels, cloud_steps(): call(functools.partial(cloud_kernel, capacity), (pltpu.VMEM(first.shape,...  5.66 us
    pallas_call x1, Pallas kernels, cloud_after(): call(after_kernel, (jax.ShapeDtypeStruct(crm_state.shape, F32), jax.Shape...  5.55 us
    all_to_all x1, starting transfers between devices, on_device(): lax.all_to_all(outgoing.reshape(peers, capacity // 2, LANES), AXES, 0, 0,...  5.21 us
    pallas_call x1, Pallas kernels, cloud_before(): call(before_kernel, (pltpu.HBM(field, F32), pltpu.HBM(sums, F32)), [pltpu...  4.65 us
    all_to_all x1, waiting for transfers between devices, on_device(): lax.all_to_all(outgoing.reshape(peers, capacity // 2, LANES), AXES, 0, 0,...  3.57 us
    all_to_all x1, waiting for transfers between devices, on_device(): lax.all_to_all(reply.reshape(peers, capacity // 2, LANES), AXES, 0, 0, ti...  2.67 us
    all_to_all x1, starting transfers between devices, on_device(): lax.all_to_all(reply.reshape(peers, capacity // 2, LANES), AXES, 0, 0, ti...  2.57 us
  transfers between devices with their start and end apart: 4, of which 2 were waited for; matrix products, arithmetic and copies ran while one was open for 0% of the time, Pallas kernels for 29%

profile of v4, /device:TPU:0, one launch (start us, length us, event | category | flops | bytes accessed | tf_op | source)
XLA Modules:
  0.0 43.6 jit_solution(15074230179380111385)
XLA Ops:
  0.6 1.3 %shard_map.85.own_ref = f32[48,256]{1,0:T(8,128)S(1)} custom-call(f32[64,4,144]{2,1,0:T(4,128)} %edge_ref.1), custom_call_target="tpu_custom_call" | custom-call | flops 10000000 | bytes 400000 | tf_op jit(solution)/shard_map/pallas_call | solution.py:537
  1.9 0.5 %collective-permute-start = (f32[48,256]{1,0:T(8,128)S(1)}, f32[48,256]{1,0:T(8,128)S(1)}, u32[]{:S(2)}, u32[]{:S(2)}) collective-permute-start(f32[48,256]{1,0:T(8,128)S(1)} %shard_map.85.own_ref), channel_id=1, source_target_pairs={{0,1},{1,0},{2,3},{3,2},{4,5},{5,4},{6,7},{7,6},{8,9},{9,8},{10,11... | collective-permute-start | bytes 147464 | tf_op jit(solution)/shard_map/ppermute | solution.py:541
  2.4 6.6 %collective-permute-start.1 = (f32[48,256]{1,0:T(8,128)S(1)}, f32[48,256]{1,0:T(8,128)S(1)}, u32[]{:S(2)}, u32[]{:S(2)}) collective-permute-start(f32[48,256]{1,0:T(8,128)S(1)} %shard_map.85.own_ref), channel_id=1, source_target_pairs={{0,31},{1,2},{2,1},{3,4},{4,3},{5,6},{6,5},{7,8},{8,7},{9,10},{10,... | collective-permute-start | bytes 147464 | tf_op jit(solution)/shard_map/ppermute | solution.py:540
  9.0 0.0 collective-permute-done.pair_ref
  9.0 2.2 %shard_map.86 = (s32[1,256]{1,0:T(1,128)S(1)}, f32[256,128]{1,0:T(8,128)S(1)}, bf16[512,256]{1,0:T(8,128)(2,1)S(1)}) custom-call(s32[1]{0:T(128)} %bitcast.me_ref, s32[1,256]{1,0:T(1,128)} %bitcast.17, s32[1,256]{1,0:T(1,128)} %bitcast.18, s32[4,64]{1,0:T(4,128)} %bitcast.15, f32[576,256]{1,0:T(8,128)} %bitcast.14, f32[48,256]{1,0:T(8,128)S(1)} %shard_map.85.own_ref, ...), custom_call_target="tpu_custom_call" | custom-call | flops 2000000000 | bytes 2000000 | tf_op jit(solution)/shard_map/pallas_call | solution.py:542
  11.3 0.0 collective-permute-done.1.other_ref
  11.3 0.9 %shard_map.87 = f32[256,128]{1,0:T(8,128)} custom-call(f32[256,128]{1,0:T(8,128)S(1)} %get-tuple-element.16.base_ref, bf16[512,256]{1,0:T(8,128)(2,1)S(1)} %get-tuple-element.17.map_ref, f32[48,256]{1,0:T(8,128)S(1)} %collective-permute-done.1.other_ref), custom_call_target="tpu_custom_call" | custom-call | flops 200000000 | bytes 1000000 | tf_op jit(solution)/shard_map/pallas_call | solution.py:558
  12.3 5.2 %all-to-all-start = ((f32[32,8,128]{2,1,0:T(8,128)}), f32[32,8,128]{2,1,0:T(8,128)S(1)}, u32[]{:S(2)}, u32[]{:S(2)}) async-start(f32[32,8,128]{2,1,0:T(8,128)} %bitcast.5), calls=%async_computation | async-start | bytes 262144 | tf_op jit(solution)/shard_map/all_to_all | solution.py:560
  17.5 4.6 %shard_map.88 = (f32[4,48,4,8,128]{4,3,2,1,0:T(8,128)}, f32[4,2,48,128]{3,2,1,0:T(8,128)}) custom-call(f32[2,48,32,512]{3,2,1,0:T(8,128)} %state_ref.3), custom_call_target="tpu_custom_call" | custom-call | flops 19660800 | bytes 6291456 | tf_op jit(solution)/shard_map/pallas_call | solution.py:464
  22.1 3.6 %all-to-all-done = f32[32,8,128]{2,1,0:T(8,128)S(1)} async-done(((f32[32,8,128]{2,1,0:T(8,128)}), f32[32,8,128]{2,1,0:T(8,128)S(1)}, u32[]{:S(2)}, u32[]{:S(2)}) %all-to-all-start) | async-done | bytes 131104 | tf_op jit(solution)/shard_map/all_to_all | solution.py:560
  25.7 5.7 %shard_map.89 = (f32[4,48,4,8,128]{4,3,2,1,0:T(8,128)S(1)}, f32[4,48,128]{2,1,0:T(8,128)S(1)}, f32[4,1,128]{2,1,0:T(1,128)S(1)}, f32[4,1,128]{2,1,0:T(1,128)S(1)}, f32[256,128]{1,0:T(8,128)}) custom-call(f32[256,128]{1,0:T(8,128)S(1)} %bitcast.12, f32[4,48,4,8,128]{4,3,2,1,0:T(8,128)} %get-tuple-element.18.far_ref, ...), custom_call_target="tpu_custom_call" | custom-call | flops 23592960 | bytes 6291456 | tf_op jit(solution)/shard_map/pallas_call | solution.py:485
  31.4 2.6 %all-to-all-start.1 = ((f32[32,8,128]{2,1,0:T(8,128)}), f32[32,8,128]{2,1,0:T(8,128)S(1)}, u32[]{:S(2)}, u32[]{:S(2)}) async-start(f32[32,8,128]{2,1,0:T(8,128)} %bitcast.7), calls=%async_computation.1 | async-start | bytes 262144 | tf_op jit(solution)/shard_map/all_to_all | solution.py:562
  34.0 5.6 %shard_map.91 = (f32[2,48,32,512]{3,2,1,0:T(8,128)}, f32[4,1,128]{2,1,0:T(1,128)}) custom-call(f32[2,48,32,512]{3,2,1,0:T(8,128)} %state_ref.3, f32[4,48,4,8,128]{4,3,2,1,0:T(8,128)S(1)} %get-tuple-element.21.last_ref, f32[4,48,128]{2,1,0:T(8,128)S(1)} %get-tuple-element.22.force_ref, f32[4,1,128]{2,1,0:T(1,128)S(1)} %get-tuple-element.23.code_ref, ...), custom_call_target="tpu_custom_call" | custom-call | flops 7864320 | bytes 6291456 | tf_op jit(solution)/shard_map/pallas_call | solution.py:512
  39.5 2.7 %all-to-all-done.1 = f32[32,8,128]{2,1,0:T(8,128)S(1)} async-done(((f32[32,8,128]{2,1,0:T(8,128)}), f32[32,8,128]{2,1,0:T(8,128)S(1)}, u32[]{:S(2)}, u32[]{:S(2)}) %all-to-all-start.1) | async-done | bytes 131104 | tf_op jit(solution)/shard_map/all_to_all | solution.py:562
  42.2 1.4 %shard_map.90 = f32[576,256]{1,0:T(8,128)} custom-call(s32[1,256]{1,0:T(1,128)S(1)} %get-tuple-element.15.pos_ref, f32[256,128]{1,0:T(8,128)S(1)} %bitcast.11), custom_call_target="tpu_custom_call" | custom-call | flops 100000000 | bytes 1000000 | tf_op jit(solution)/shard_map/pallas_call | solution.py:565
Async XLA Ops:
  1.9 7.1 %collective-permute-start = (f32[48,256]{1,0:T(8,128)S(1)}, f32[48,256]{1,0:T(8,128)S(1)}, u32[]{:S(2)}, u32[]{:S(2)}) collective-permute-start(f32[48,256]{1,0:T(8,128)S(1)} %shard_map.85.own_ref), channel_id=1, source_target_pairs={{0,1},{1,0},{2,3},{3,2},{4,5},{5,4},{6,7},{7,6},{8,9},{9,8},{10,11... | collective-permute-start | bytes 147464 | tf_op jit(solution)/shard_map/ppermute | solution.py:541
  2.4 8.9 %collective-permute-start.1 = (f32[48,256]{1,0:T(8,128)S(1)}, f32[48,256]{1,0:T(8,128)S(1)}, u32[]{:S(2)}, u32[]{:S(2)}) collective-permute-start(f32[48,256]{1,0:T(8,128)S(1)} %shard_map.85.own_ref), channel_id=1, source_target_pairs={{0,31},{1,2},{2,1},{3,4},{4,3},{5,6},{6,5},{7,8},{8,7},{9,10},{10,... | collective-permute-start | bytes 147464 | tf_op jit(solution)/shard_map/ppermute | solution.py:540
  12.3 13.4 %all-to-all-start = ((f32[32,8,128]{2,1,0:T(8,128)}), f32[32,8,128]{2,1,0:T(8,128)S(1)}, u32[]{:S(2)}, u32[]{:S(2)}) async-start(f32[32,8,128]{2,1,0:T(8,128)} %bitcast.5), calls=%async_computation | async-start | bytes 262144 | tf_op jit(solution)/shard_map/all_to_all | solution.py:560
  31.4 10.8 %all-to-all-start.1 = ((f32[32,8,128]{2,1,0:T(8,128)}), f32[32,8,128]{2,1,0:T(8,128)S(1)}, u32[]{:S(2)}, u32[]{:S(2)}) async-start(f32[32,8,128]{2,1,0:T(8,128)} %bitcast.7), calls=%async_computation.1 | async-start | bytes 262144 | tf_op jit(solution)/shard_map/all_to_all | solution.py:562

commit v5 on v4

--- a/solution.py
+++ b/solution.py
@@ -74,7 +74,7 @@
     out_ref[...] = dot(weight, edge_ref[...].reshape(-1, shape[1]), (1, 1), HIGHEST)
 
 
-def route_kernel(peers, capacity, me_ref, routes_ref, branch_ref, neigh_ref, gcm_ref, own_ref, pair_ref,
+def route_kernel(peers, capacity, me_ref, routes_ref, branch_ref, neigh_ref, gcm_ref, own_ref,
                  pos_ref, base_ref, halo_map_ref):
     columns = routes_ref.shape[1]
     elems = columns // 4
@@ -107,23 +107,23 @@
     second = ((column + 1) % 4) * elems + column // 4
     pair = ((row == first) | (row == second)).astype(BF16)
     mapped = dot(pair, chosen.astype(BF16), (1, 1)).astype(BF16)
-    halo_map_ref[...] = dot(place, mapped[:, 2 * columns :], (1, 0)).astype(BF16)
-
-    near = jnp.concatenate([own_ref[...], pair_ref[...]], axis=1)
+    halo_map_ref[...] = dot(place, mapped[:, columns:], (1, 0)).astype(BF16)
+
     levels = gcm_ref.shape[0] // NV
     mixed = mixing(0) * gcm_ref[:levels, :]
     for k in range(1, NV):
         mixed += mixing(k) * gcm_ref[pl.ds(k * levels, levels), :]
     shape = (crm_levels, levels)
     force = dot(interp(iota(shape, 0), iota(shape, 1), crm_levels, levels), mixed, (1, 0), HIGHEST)
-    for part in split(near):
-        force += 0.25 * dot(part, mapped[:, : 2 * columns], (1, 1))
+    for part in split(own_ref[...]):
+        force += 0.25 * dot(part, mapped[:, :columns], (1, 1))
     code = (branch_ref[...] + 1).astype(F32)
     base_ref[...] = slot_rows(place, padded(jnp.concatenate([force, code], axis=0)))
 
 
-def outgoing_kernel(base_ref, map_ref, other_ref, out_ref):
-    out_ref[...] = base_ref[...] + 0.25 * slot_rows(map_ref[...], padded(other_ref[...]))
+def outgoing_kernel(base_ref, map_ref, other_ref, pair_ref, _, out_ref):
+    window = jnp.concatenate([pair_ref[...], other_ref[...]], axis=1)
+    out_ref[...] = base_ref[...] + 0.25 * slot_rows(map_ref[...], padded(window))
 
 
 class Field:
@@ -169,12 +169,12 @@
     return jnp.concatenate([x[:1], x[:-1]], axis=0) + jnp.concatenate([x[1:], x[-1:]], axis=0)
 
 
-def before_kernel(state_ref, first_ref, sums_ref, kept_ref, part_ref, kept_sums_ref, new_ref, sems, done_sems):
+def before_kernel(start, state_ref, first_ref, sums_ref, kept_ref, part_ref, kept_sums_ref, new_ref, sems, done_sems):
     blocks, _, crm_levels, width, _ = kept_ref.shape
     count = width // 8
 
     def copy(j):
-        lanes = pl.ds(pl.multiple_of(j * LANES, LANES), LANES)
+        lanes = pl.ds(pl.multiple_of((start + j) * LANES, LANES), LANES)
         return pltpu.make_async_copy(state_ref.at[:, :, :, lanes], kept_ref.at[j], sems.at[j])
 
     def done(j):
@@ -246,19 +246,25 @@
     return 0.15 + 0.25 * (code == 2.0).astype(F32)
 
 
-def cloud_kernel(capacity, arrived_ref, far_ref, far_sums_ref, last_ref, force_ref, code_ref, rain_ref,
+def cloud_kernel(capacity, arrived_ref, near_ref, near_sums_ref, far_ref, far_sums_ref, last_ref, force_ref, code_ref, rain_ref,
                  reply_ref, push_ref, part_ref, sums_ref, first_ref, sems):
     blocks, crm_levels, count = last_ref.shape[:3]
+    near = near_ref.shape[0]
     width = count * 8
     part = arrived_ref.shape[0] // blocks
 
     def load(j):
-        return pltpu.make_async_copy(far_ref.at[j], first_ref.at[j], sems.at[j])
-
-    load_sums = pltpu.make_async_copy(far_sums_ref, sums_ref, sems.at[blocks])
+        source = near_ref.at[j] if j < near else far_ref.at[j - near]
+        return pltpu.make_async_copy(source, first_ref.at[j], sems.at[j])
+
+    load_sums = [
+        pltpu.make_async_copy(near_sums_ref, sums_ref.at[pl.ds(0, near)], sems.at[blocks]),
+        pltpu.make_async_copy(far_sums_ref, sums_ref.at[pl.ds(near, blocks - near)], sems.at[blocks + 1]),
+    ]
     for j in range(blocks):
         load(j).start()
-    load_sums.start()
+    for copy in load_sums:
+        copy.start()
     low, high = lane_maps(part, capacity)
     maps = jnp.concatenate([low, high], axis=1)
     maps = jnp.concatenate([maps, maps], axis=0)
@@ -272,7 +278,7 @@
         code_ref[j] = got[crm_levels : crm_levels + 1]
 
     def block(j, _):
-        load(j).wait()
+        pltpu.make_async_copy(far_ref.at[0], first_ref.at[j], sems.at[j]).wait()
         lowered = jnp.broadcast_to((1.15 * LOG2E) * rate_of(code_ref[j]), (8, LANES))
         fields = [Field(crm_levels) for _ in range(STEPS)]
         for i in range(crm_levels + STEPS - 1):
@@ -294,7 +300,8 @@
         return 0
 
     lax.fori_loop(0, blocks, block, 0)
-    load_sums.wait()
+    for copy in load_sums:
+        copy.wait()
     turned = jnp.concatenate([low, high], axis=0)
     for j in range(blocks):
         dg = rows_of_sums(part_ref.at[j], crm_levels) * (1.0 / width) - sums_ref[j, 0]
@@ -455,14 +462,13 @@
 VMEM = pl.BlockSpec(memory_space=pltpu.VMEM)
 
 
-def cloud_before(crm_state):
-    _, crm_levels, width, slots = crm_state.shape
-    blocks = slots // LANES
-    cells = crm_levels * width * slots
+def cloud_before(crm_state, start, blocks):
+    _, crm_levels, width, _ = crm_state.shape
+    cells = crm_levels * width * blocks * LANES
     field = (blocks, crm_levels, width // 8, 8, LANES)
     sums = (blocks, 2, crm_levels, LANES)
     return call(
-        before_kernel,
+        functools.partial(before_kernel, start),
         (pltpu.HBM(field, F32), pltpu.HBM(sums, F32)),
         [
             pltpu.VMEM((blocks, 2, crm_levels, width, LANES), F32),
@@ -478,30 +484,31 @@
     )(*from_hbm(crm_state))
 
 
-def cloud_steps(capacity, arrived, first, sums):
-    blocks, _, crm_levels, _ = sums.shape
-    slots = blocks * LANES
-    cells = crm_levels * first.shape[2] * 8 * slots
+def cloud_steps(capacity, arrived, near, near_sums, far, far_sums):
+    blocks = near.shape[0] + far.shape[0]
+    crm_levels, count = far.shape[1:3]
+    cells = crm_levels * count * 8 * blocks * LANES
+    sums = (blocks,) + far_sums.shape[1:]
     return call(
         functools.partial(cloud_kernel, capacity),
         (
-            pltpu.VMEM(first.shape, F32),
+            pltpu.VMEM((blocks,) + far.shape[1:], F32),
             pltpu.VMEM((blocks, crm_levels, LANES), F32),
             pltpu.VMEM((blocks, 1, LANES), F32),
             pltpu.VMEM((blocks, 1, LANES), F32),
             jax.ShapeDtypeStruct(arrived.shape, F32),
         ),
         [
-            pltpu.VMEM(sums.shape, F32),
+            pltpu.VMEM(sums, F32),
             pltpu.VMEM((blocks, crm_levels * 8, LANES), F32),
-            pltpu.VMEM(sums.shape, F32),
-            pltpu.VMEM(first.shape, F32),
-            pltpu.SemaphoreType.DMA((blocks + 1,)),
+            pltpu.VMEM(sums, F32),
+            pltpu.VMEM((blocks,) + far.shape[1:], F32),
+            pltpu.SemaphoreType.DMA((blocks + 2,)),
         ],
         (cells * 30, cells * 8, cells * 6),
-        in_specs=[VMEM, HBM, HBM],
+        in_specs=[VMEM] + [HBM] * 4,
         out_specs=[VMEM] * 5,
-    )(arrived, *from_hbm(first, sums))
+    )(arrived, *from_hbm(near, near_sums, far, far_sums))
 
 
 def cloud_after(crm_state, last, force, code, rain):
@@ -544,21 +551,26 @@
         (
             shape((1, columns), jnp.int32),
             shape((rows, LANES), F32),
-            shape((slots, columns), BF16),
+            shape((slots, 2 * columns), BF16),
         ),
         cost=(2e9, 2e6, 0),
-        in_specs=[pl.BlockSpec(memory_space=pltpu.SMEM)] + [VMEM] * 6,
+        in_specs=[pl.BlockSpec(memory_space=pltpu.SMEM)] + [VMEM] * 5,
         out_specs=[VMEM] * 3,
     )(
         me.reshape(1),
         *from_hbm(routes.T, branch.reshape(1, -1), neighbours.T, gcm_state.T),
         own,
-        pair,
-    )
-    outgoing = call(outgoing_kernel, shape((rows, LANES), F32), cost=(2e8, 1e6, 0))(base, halo_map, other)
-    first, sums = cloud_before(crm_state)
+    )
+    near, near_sums = cloud_before(crm_state, 0, 1)
+    outgoing = call(
+        outgoing_kernel, shape((rows, LANES), F32), cost=(2e8, 1e6, 0),
+        in_specs=[VMEM] * 4 + [HBM], out_specs=VMEM,
+    )(base, halo_map, other, pair, *from_hbm(near))
+    far, far_sums = cloud_before(crm_state, 1, slots // LANES - 1)
     arrived = lax.all_to_all(outgoing.reshape(peers, capacity // 2, LANES), AXES, 0, 0, tiled=True)
-    last, force, code, rain, reply = cloud_steps(capacity, arrived.reshape(rows, LANES), first, sums)
+    last, force, code, rain, reply = cloud_steps(
+        capacity, arrived.reshape(rows, LANES), near, near_sums, far, far_sums
+    )
     returned = lax.all_to_all(reply.reshape(peers, capacity // 2, LANES), AXES, 0, 0, tiled=True)
     updated, rain = cloud_after(crm_state, last, force, code, rain)
     levels = features // NV

time: 43.9 us -> 43.3 us (0.986)
  starting transfers between devices: 14.9 us -> 11.6 us
  Pallas kernels: 21.8 us -> 23.4 us
  waiting for transfers between devices: 6.25 us -> 7.32 us
    all_to_all x1, starting transfers between devices: 5.21 us -> 2.58 us  [on_device(): lax.all_to_all(outgoing.reshape(peers, capacity // 2, LANES), AXES, 0, 0,...]
    pallas_call x2 -> x3, Pallas kernels: 10.3 us -> 11.8 us  [the longest x2 6.13 us: cloud_before(): call(functools.partial(before_kernel, start), (pltpu.HBM(field, F32), plt...]
    all_to_all x1, waiting for transfers between devices: 3.57 us -> 4.64 us  [on_device(): lax.all_to_all(outgoing.reshape(peers, capacity // 2, LANES), AXES, 0, 0,...]
    ppermute x1, starting transfers between devices: 0.52 us -> 0.01 us  [on_device(): pair = lax.ppermute(own, AXES, [(i, i ^ 1) for i in range(peers)])]
  transfers between devices with their start and end apart: 4 -> 4, of which waited for: 2 -> 2; matrix products, arithmetic and copies ran while one was open for 0% -> 0% of each run, Pallas kernels for 29% -> 33%
where the time goes in v5:
time: 43.3 us; the launch traced here: 43 us
  Pallas kernels  23.4 us (54%)
  starting transfers between devices  11.6 us (27%)
  waiting for transfers between devices  7.32 us (17%)
  between operations  0.71 us (2%)
    ppermute x1, starting transfers between devices, on_device(): lax.ppermute(own, AXES, [(i, ((i + 1 ^ 1) - 1) % peers) for i in range(pe...  6.44 us
    pallas_call x2, Pallas kernels, cloud_before(): call(functools.partial(before_kernel, start), (pltpu.HBM(field, F32), plt...  6.13 us
    pallas_call x1, Pallas kernels, cloud_steps(): call(functools.partial(cloud_kernel, capacity), (pltpu.VMEM((blocks,) + f...  5.68 us
    pallas_call x1, Pallas kernels, cloud_after(): call(after_kernel, (jax.ShapeDtypeStruct(crm_state.shape, F32), jax.Shape...  5.55 us
    all_to_all x1, waiting for transfers between devices, on_device(): lax.all_to_all(outgoing.reshape(peers, capacity // 2, LANES), AXES, 0, 0,...  4.64 us
    all_to_all x1, waiting for transfers between devices, on_device(): lax.all_to_all(reply.reshape(peers, capacity // 2, LANES), AXES, 0, 0, ti...  2.67 us
    all_to_all x1, starting transfers between devices, on_device(): lax.all_to_all(outgoing.reshape(peers, capacity // 2, LANES), AXES, 0, 0,...  2.58 us
    all_to_all x1, starting transfers between devices, on_device(): lax.all_to_all(reply.reshape(peers, capacity // 2, LANES), AXES, 0, 0, ti...  2.57 us
  transfers between devices with their start and end apart: 4, of which 2 were waited for; matrix products, arithmetic and copies ran while one was open for 0% of the time, Pallas kernels for 33%

profile of v5, /device:TPU:0, one launch (start us, length us, event | category | flops | bytes accessed | tf_op | source)
XLA Modules:
  0.0 43.0 jit_solution(4280440173454569881)
XLA Ops:
  0.6 1.3 %shard_map.85.own_ref = f32[48,256]{1,0:T(8,128)S(1)} custom-call(f32[64,4,144]{2,1,0:T(4,128)} %edge_ref.1), custom_call_target="tpu_custom_call" | custom-call | flops 10000000 | bytes 400000 | tf_op jit(solution)/shard_map/pallas_call | solution.py:544
  1.9 6.4 %collective-permute-start = (f32[48,256]{1,0:T(8,128)S(1)}, f32[48,256]{1,0:T(8,128)S(1)}, u32[]{:S(2)}, u32[]{:S(2)}) collective-permute-start(f32[48,256]{1,0:T(8,128)S(1)} %shard_map.85.own_ref), channel_id=1, source_target_pairs={{0,31},{1,2},{2,1},{3,4},{4,3},{5,6},{6,5},{7,8},{8,7},{9,10},{10,... | collective-permute-start | bytes 147464 | tf_op jit(solution)/shard_map/ppermute | solution.py:547
  8.4 0.0 collective-permute-start.1
  8.4 2.3 %shard_map.86 = (s32[1,256]{1,0:T(1,128)S(1)}, f32[256,128]{1,0:T(8,128)S(1)}, bf16[512,512]{1,0:T(8,128)(2,1)S(1)}) custom-call(s32[1]{0:T(128)} %bitcast.me_ref, s32[1,256]{1,0:T(1,128)} %bitcast.17, s32[1,256]{1,0:T(1,128)} %bitcast.18, s32[4,64]{1,0:T(4,128)} %bitcast.15, f32[576,256]{1,0:T(8,128)} %bitcast.14, f32[48,256]{1,0:T(8,128)S(1)} %shard_map.85.own_ref), custom_call_target="tpu_custom_call" | custom-call | flops 2000000000 | bytes 2000000 | tf_op jit(solution)/shard_map/pallas_call | solution.py:549
  10.7 2.5 %shard_map.87 = (f32[1,48,4,8,128]{4,3,2,1,0:T(8,128)}, f32[1,2,48,128]{3,2,1,0:T(8,128)}) custom-call(f32[2,48,32,512]{3,2,1,0:T(8,128)} %state_ref.5), custom_call_target="tpu_custom_call" | custom-call | flops 4915200 | bytes 1572864 | tf_op jit(solution)/shard_map/pallas_call | solution.py:470
  13.2 0.0 collective-permute-done.other_ref
  13.3 0.0 collective-permute-done.1.pair_ref
  13.3 1.0 %shard_map.88 = f32[256,128]{1,0:T(8,128)} custom-call(f32[256,128]{1,0:T(8,128)S(1)} %get-tuple-element.18.base_ref, bf16[512,512]{1,0:T(8,128)(2,1)S(1)} %get-tuple-element.19.map_ref, f32[48,256]{1,0:T(8,128)S(1)} %collective-permute-done.other_ref, f32[48,256]{1,0:T(8,128)S(1)} %collective-permute-done.1.pair_ref, ...), custom_call_target="tpu_custom_call" | custom-call | flops 200000000 | bytes 1000000 | tf_op jit(solution)/shard_map/pallas_call | solution.py:565
  14.3 2.6 %all-to-all-start = ((f32[32,8,128]{2,1,0:T(8,128)}), f32[32,8,128]{2,1,0:T(8,128)S(1)}, u32[]{:S(2)}, u32[]{:S(2)}) async-start(f32[32,8,128]{2,1,0:T(8,128)} %bitcast.5), calls=%async_computation | async-start | bytes 262144 | tf_op jit(solution)/shard_map/all_to_all | solution.py:570
  16.9 3.6 %shard_map.89 = (f32[3,48,4,8,128]{4,3,2,1,0:T(8,128)}, f32[3,2,48,128]{3,2,1,0:T(8,128)}) custom-call(f32[2,48,32,512]{3,2,1,0:T(8,128)} %state_ref.5), custom_call_target="tpu_custom_call" | custom-call | flops 14745600 | bytes 4718592 | tf_op jit(solution)/shard_map/pallas_call | solution.py:470
  20.5 4.6 %all-to-all-done = f32[32,8,128]{2,1,0:T(8,128)S(1)} async-done(((f32[32,8,128]{2,1,0:T(8,128)}), f32[32,8,128]{2,1,0:T(8,128)S(1)}, u32[]{:S(2)}, u32[]{:S(2)}) %all-to-all-start) | async-done | bytes 131104 | tf_op jit(solution)/shard_map/all_to_all | solution.py:570
  25.1 5.7 %shard_map.90 = (f32[4,48,4,8,128]{4,3,2,1,0:T(8,128)S(1)}, f32[4,48,128]{2,1,0:T(8,128)S(1)}, f32[4,1,128]{2,1,0:T(1,128)S(1)}, f32[4,1,128]{2,1,0:T(1,128)S(1)}, f32[256,128]{1,0:T(8,128)}) custom-call(f32[256,128]{1,0:T(8,128)S(1)} %bitcast.12, f32[1,48,4,8,128]{4,3,2,1,0:T(8,128)} %get-tuple-element.20._.near_ref, ...), custom_call_target="tpu_custom_call" | custom-call | flops 23592960 | bytes 6291456 | tf_op jit(solution)/shard_map/pallas_call | solution.py:492
  30.8 2.6 %all-to-all-start.1 = ((f32[32,8,128]{2,1,0:T(8,128)}), f32[32,8,128]{2,1,0:T(8,128)S(1)}, u32[]{:S(2)}, u32[]{:S(2)}) async-start(f32[32,8,128]{2,1,0:T(8,128)} %bitcast.7), calls=%async_computation.1 | async-start | bytes 262144 | tf_op jit(solution)/shard_map/all_to_all | solution.py:574
  33.4 5.6 %shard_map.92 = (f32[2,48,32,512]{3,2,1,0:T(8,128)}, f32[4,1,128]{2,1,0:T(1,128)}) custom-call(f32[2,48,32,512]{3,2,1,0:T(8,128)} %state_ref.5, f32[4,48,4,8,128]{4,3,2,1,0:T(8,128)S(1)} %get-tuple-element.25.last_ref, f32[4,48,128]{2,1,0:T(8,128)S(1)} %get-tuple-element.26.force_ref, f32[4,1,128]{2,1,0:T(1,128)S(1)} %get-tuple-element.27.code_ref, ...), custom_call_target="tpu_custom_call" | custom-call | flops 7864320 | bytes 6291456 | tf_op jit(solution)/shard_map/pallas_call | solution.py:519
  39.0 2.7 %all-to-all-done.1 = f32[32,8,128]{2,1,0:T(8,128)S(1)} async-done(((f32[32,8,128]{2,1,0:T(8,128)}), f32[32,8,128]{2,1,0:T(8,128)S(1)}, u32[]{:S(2)}, u32[]{:S(2)}) %all-to-all-start.1) | async-done | bytes 131104 | tf_op jit(solution)/shard_map/all_to_all | solution.py:574
  41.6 1.4 %shard_map.91 = f32[576,256]{1,0:T(8,128)} custom-call(s32[1,256]{1,0:T(1,128)S(1)} %get-tuple-element.17.pos_ref, f32[256,128]{1,0:T(8,128)S(1)} %bitcast.11), custom_call_target="tpu_custom_call" | custom-call | flops 100000000 | bytes 1000000 | tf_op jit(solution)/shard_map/pallas_call | solution.py:577
Async XLA Ops:
  1.9 11.3 %collective-permute-start = (f32[48,256]{1,0:T(8,128)S(1)}, f32[48,256]{1,0:T(8,128)S(1)}, u32[]{:S(2)}, u32[]{:S(2)}) collective-permute-start(f32[48,256]{1,0:T(8,128)S(1)} %shard_map.85.own_ref), channel_id=1, source_target_pairs={{0,31},{1,2},{2,1},{3,4},{4,3},{5,6},{6,5},{7,8},{8,7},{9,10},{10,... | collective-permute-start | bytes 147464 | tf_op jit(solution)/shard_map/ppermute | solution.py:547
  8.4 4.9 %collective-permute-start.1 = (f32[48,256]{1,0:T(8,128)S(1)}, f32[48,256]{1,0:T(8,128)S(1)}, u32[]{:S(2)}, u32[]{:S(2)}) collective-permute-start(f32[48,256]{1,0:T(8,128)S(1)} %shard_map.85.own_ref), channel_id=1, source_target_pairs={{0,1},{1,0},{2,3},{3,2},{4,5},{5,4},{6,7},{7,6},{8,9},{9,8},{10,11... | collective-permute-start | bytes 147464 | tf_op jit(solution)/shard_map/ppermute | solution.py:548
  14.3 10.8 %all-to-all-start = ((f32[32,8,128]{2,1,0:T(8,128)}), f32[32,8,128]{2,1,0:T(8,128)S(1)}, u32[]{:S(2)}, u32[]{:S(2)}) async-start(f32[32,8,128]{2,1,0:T(8,128)} %bitcast.5), calls=%async_computation | async-start | bytes 262144 | tf_op jit(solution)/shard_map/all_to_all | solution.py:570
  30.8 10.8 %all-to-all-start.1 = ((f32[32,8,128]{2,1,0:T(8,128)}), f32[32,8,128]{2,1,0:T(8,128)S(1)}, u32[]{:S(2)}, u32[]{:S(2)}) async-start(f32[32,8,128]{2,1,0:T(8,128)} %bitcast.7), calls=%async_computation.1 | async-start | bytes 262144 | tf_op jit(solution)/shard_map/all_to_all | solution.py:574

commit v6 on v5

--- a/solution.py
+++ b/solution.py
@@ -16,7 +16,6 @@
 LOG2E = 1.4426950408889634
 F32 = jnp.float32
 BF16 = jnp.bfloat16
-HIGHEST = lax.Precision.HIGHEST
 SMALL_RAIN = 0.2
 
 
@@ -29,16 +28,24 @@
     return jnp.maximum(0.0, 1.0 - jnp.abs(position - level.astype(F32)))
 
 
-def dot(a, b, contract, precision=None):
+def dot(a, b, contract):
     return lax.dot_general(
         a, b, ((contract[0:1], contract[1:2]), ((), ())),
-        precision=precision, preferred_element_type=F32,
+        preferred_element_type=F32,
     )
 
 
 def split(x):
     high = x.astype(BF16)
     return high, (x - high.astype(F32)).astype(BF16)
+
+
+def dot_in_three(a, b, contract):
+    high, low = split(b)
+    parts = both_halves(a)
+    rows = a.shape[0]
+    first = dot(parts, high, contract)
+    return first[:rows] + first[rows:] + dot(parts[:rows], low, contract)
 
 
 def both_halves(x):
@@ -71,7 +78,7 @@
         mixing(0) * interp(iota(shape, 0), lane, crm_levels, levels),
         mixing(1) * interp(iota(shape, 0), lane - levels, crm_levels, levels),
     )
-    out_ref[...] = dot(weight, edge_ref[...].reshape(-1, shape[1]), (1, 1), HIGHEST)
+    out_ref[...] = dot_in_three(weight, edge_ref[...].reshape(-1, shape[1]), (1, 1))
 
 
 def route_kernel(peers, capacity, me_ref, routes_ref, branch_ref, neigh_ref, gcm_ref, own_ref,
@@ -114,7 +121,7 @@
     for k in range(1, NV):
         mixed += mixing(k) * gcm_ref[pl.ds(k * levels, levels), :]
     shape = (crm_levels, levels)
-    force = dot(interp(iota(shape, 0), iota(shape, 1), crm_levels, levels), mixed, (1, 0), HIGHEST)
+    force = dot_in_three(interp(iota(shape, 0), iota(shape, 1), crm_levels, levels), mixed, (1, 0))
     for part in split(own_ref[...]):
         force += 0.25 * dot(part, mapped[:, :columns], (1, 1))
     code = (branch_ref[...] + 1).astype(F32)
@@ -429,15 +436,19 @@
     rows = returned_ref.shape[0]
     columns = pos_ref.shape[1]
     place = (iota((2 * rows, columns), 0) == pos_ref[...]).astype(BF16)
-    high, low = split(returned_ref[...])
-    lower = dot(high, place[:rows], (0, 0)) + dot(low, place[:rows], (0, 0))
-    upper = dot(high, place[rows:], (0, 0)) + dot(low, place[rows:], (0, 0))
-    answer = lower[:crm_levels] + upper[HALF : HALF + crm_levels]
-    shape = (levels, crm_levels)
-    spread = dot(interp(iota(shape, 1), iota(shape, 0), crm_levels, levels), answer, (1, 0), HIGHEST)
+    shape = (levels, 2 * HALF)
+    lane, level = iota(shape, 1), iota(shape, 0)
+    table = [
+        jnp.where((lane >= at) & (lane < at + crm_levels), interp(lane - at, level, crm_levels, levels), 0.0)
+        for at in (0, HALF)
+    ]
+    spread = dot_in_three(jnp.concatenate(table, axis=0), returned_ref[...], (1, 1))
+    parts = both_halves(jnp.concatenate([spread[:levels], spread[levels:]], axis=1))
+    answer = dot(parts, place, (1, 0))
+    answer = answer[:levels] + answer[levels:]
     copies = []
     for k in range(NV):
-        new_ref[k] = mixing(k) * spread
+        new_ref[k] = mixing(k) * answer
         copies.append(
             pltpu.make_async_copy(new_ref.at[k], out_ref.at[pl.ds(k * levels, levels), :], sems.at[k])
         )

time: 43.3 us -> 43.1 us (level)
  no operation moved by 1% of the time
where the time goes in v6:
time: 43.1 us; the launch traced here: 42.8 us
  Pallas kernels  23.2 us (54%)
  starting transfers between devices  11.6 us (27%)
  waiting for transfers between devices  7.32 us (17%)
  between operations  0.71 us (2%)
    ppermute x1, starting transfers between devices, on_device(): lax.ppermute(own, AXES, [(i, ((i + 1 ^ 1) - 1) % peers) for i in range(pe...  6.44 us
    pallas_call x2, Pallas kernels, cloud_before(): call(functools.partial(before_kernel, start), (pltpu.HBM(field, F32), plt...  6.13 us
    pallas_call x1, Pallas kernels, cloud_steps(): call(functools.partial(cloud_kernel, capacity), (pltpu.VMEM((blocks,) + f...  5.68 us
    pallas_call x1, Pallas kernels, cloud_after(): call(after_kernel, (jax.ShapeDtypeStruct(crm_state.shape, F32), jax.Shape...  5.55 us
    all_to_all x1, waiting for transfers between devices, on_device(): lax.all_to_all(outgoing.reshape(peers, capacity // 2, LANES), AXES, 0, 0,...  4.64 us
    all_to_all x1, waiting for transfers between devices, on_device(): lax.all_to_all(reply.reshape(peers, capacity // 2, LANES), AXES, 0, 0, ti...  2.67 us
    all_to_all x1, starting transfers between devices, on_device(): lax.all_to_all(outgoing.reshape(peers, capacity // 2, LANES), AXES, 0, 0,...  2.6 us
    all_to_all x1, starting transfers between devices, on_device(): lax.all_to_all(reply.reshape(peers, capacity // 2, LANES), AXES, 0, 0, ti...  2.57 us
  transfers between devices with their start and end apart: 4, of which 2 were waited for; matrix products, arithmetic and copies ran while one was open for 0% of the time, Pallas kernels for 33%

profile of v6, /device:TPU:0, one launch (start us, length us, event | category | flops | bytes accessed | tf_op | source)
XLA Modules:
  0.0 42.8 jit_solution(2409612294653941817)
XLA Ops:
  0.6 1.2 %shard_map.85.own_ref = f32[48,256]{1,0:T(8,128)S(1)} custom-call(f32[64,4,144]{2,1,0:T(4,128)} %edge_ref.1), custom_call_target="tpu_custom_call" | custom-call | flops 10000000 | bytes 400000 | tf_op jit(solution)/shard_map/pallas_call | solution.py:555
  1.8 6.4 %collective-permute-start = (f32[48,256]{1,0:T(8,128)S(1)}, f32[48,256]{1,0:T(8,128)S(1)}, u32[]{:S(2)}, u32[]{:S(2)}) collective-permute-start(f32[48,256]{1,0:T(8,128)S(1)} %shard_map.85.own_ref), channel_id=1, source_target_pairs={{0,31},{1,2},{2,1},{3,4},{4,3},{5,6},{6,5},{7,8},{8,7},{9,10},{10,... | collective-permute-start | bytes 147464 | tf_op jit(solution)/shard_map/ppermute | solution.py:558
  8.2 0.0 collective-permute-start.1
  8.2 2.3 %shard_map.86 = (s32[1,256]{1,0:T(1,128)S(1)}, f32[256,128]{1,0:T(8,128)S(1)}, bf16[512,512]{1,0:T(8,128)(2,1)S(1)}) custom-call(s32[1]{0:T(128)} %bitcast.me_ref, s32[1,256]{1,0:T(1,128)} %bitcast.17, s32[1,256]{1,0:T(1,128)} %bitcast.18, s32[4,64]{1,0:T(4,128)} %bitcast.15, f32[576,256]{1,0:T(8,128)} %bitcast.14, f32[48,256]{1,0:T(8,128)S(1)} %shard_map.85.own_ref), custom_call_target="tpu_custom_call" | custom-call | flops 2000000000 | bytes 2000000 | tf_op jit(solution)/shard_map/pallas_call | solution.py:560
  10.5 2.5 %shard_map.87 = (f32[1,48,4,8,128]{4,3,2,1,0:T(8,128)}, f32[1,2,48,128]{3,2,1,0:T(8,128)}) custom-call(f32[2,48,32,512]{3,2,1,0:T(8,128)} %state_ref.5), custom_call_target="tpu_custom_call" | custom-call | flops 4915200 | bytes 1572864 | tf_op jit(solution)/shard_map/pallas_call | solution.py:481
  13.1 0.0 collective-permute-done.other_ref
  13.1 0.0 collective-permute-done.1.pair_ref
  13.1 1.0 %shard_map.88 = f32[256,128]{1,0:T(8,128)} custom-call(f32[256,128]{1,0:T(8,128)S(1)} %get-tuple-element.18.base_ref, bf16[512,512]{1,0:T(8,128)(2,1)S(1)} %get-tuple-element.19.map_ref, f32[48,256]{1,0:T(8,128)S(1)} %collective-permute-done.other_ref, f32[48,256]{1,0:T(8,128)S(1)} %collective-permute-done.1.pair_ref, ...), custom_call_target="tpu_custom_call" | custom-call | flops 200000000 | bytes 1000000 | tf_op jit(solution)/shard_map/pallas_call | solution.py:576
  14.1 2.6 %all-to-all-start = ((f32[32,8,128]{2,1,0:T(8,128)}), f32[32,8,128]{2,1,0:T(8,128)S(1)}, u32[]{:S(2)}, u32[]{:S(2)}) async-start(f32[32,8,128]{2,1,0:T(8,128)} %bitcast.5), calls=%async_computation | async-start | bytes 262144 | tf_op jit(solution)/shard_map/all_to_all | solution.py:581
  16.8 3.6 %shard_map.89 = (f32[3,48,4,8,128]{4,3,2,1,0:T(8,128)}, f32[3,2,48,128]{3,2,1,0:T(8,128)}) custom-call(f32[2,48,32,512]{3,2,1,0:T(8,128)} %state_ref.5), custom_call_target="tpu_custom_call" | custom-call | flops 14745600 | bytes 4718592 | tf_op jit(solution)/shard_map/pallas_call | solution.py:481
  20.3 4.6 %all-to-all-done = f32[32,8,128]{2,1,0:T(8,128)S(1)} async-done(((f32[32,8,128]{2,1,0:T(8,128)}), f32[32,8,128]{2,1,0:T(8,128)S(1)}, u32[]{:S(2)}, u32[]{:S(2)}) %all-to-all-start) | async-done | bytes 131104 | tf_op jit(solution)/shard_map/all_to_all | solution.py:581
  25.0 5.7 %shard_map.90 = (f32[4,48,4,8,128]{4,3,2,1,0:T(8,128)S(1)}, f32[4,48,128]{2,1,0:T(8,128)S(1)}, f32[4,1,128]{2,1,0:T(1,128)S(1)}, f32[4,1,128]{2,1,0:T(1,128)S(1)}, f32[256,128]{1,0:T(8,128)}) custom-call(f32[256,128]{1,0:T(8,128)S(1)} %bitcast.12, f32[1,48,4,8,128]{4,3,2,1,0:T(8,128)} %get-tuple-element.20._.near_ref, ...), custom_call_target="tpu_custom_call" | custom-call | flops 23592960 | bytes 6291456 | tf_op jit(solution)/shard_map/pallas_call | solution.py:503
  30.7 2.6 %all-to-all-start.1 = ((f32[32,8,128]{2,1,0:T(8,128)}), f32[32,8,128]{2,1,0:T(8,128)S(1)}, u32[]{:S(2)}, u32[]{:S(2)}) async-start(f32[32,8,128]{2,1,0:T(8,128)} %bitcast.7), calls=%async_computation.1 | async-start | bytes 262144 | tf_op jit(solution)/shard_map/all_to_all | solution.py:585
  33.3 5.6 %shard_map.92 = (f32[2,48,32,512]{3,2,1,0:T(8,128)}, f32[4,1,128]{2,1,0:T(1,128)}) custom-call(f32[2,48,32,512]{3,2,1,0:T(8,128)} %state_ref.5, f32[4,48,4,8,128]{4,3,2,1,0:T(8,128)S(1)} %get-tuple-element.25.last_ref, f32[4,48,128]{2,1,0:T(8,128)S(1)} %get-tuple-element.26.force_ref, f32[4,1,128]{2,1,0:T(1,128)S(1)} %get-tuple-element.27.code_ref, ...), custom_call_target="tpu_custom_call" | custom-call | flops 7864320 | bytes 6291456 | tf_op jit(solution)/shard_map/pallas_call | solution.py:530
  38.8 2.7 %all-to-all-done.1 = f32[32,8,128]{2,1,0:T(8,128)S(1)} async-done(((f32[32,8,128]{2,1,0:T(8,128)}), f32[32,8,128]{2,1,0:T(8,128)S(1)}, u32[]{:S(2)}, u32[]{:S(2)}) %all-to-all-start.1) | async-done | bytes 131104 | tf_op jit(solution)/shard_map/all_to_all | solution.py:585
  41.5 1.3 %shard_map.91 = f32[576,256]{1,0:T(8,128)} custom-call(s32[1,256]{1,0:T(1,128)S(1)} %get-tuple-element.17.pos_ref, f32[256,128]{1,0:T(8,128)S(1)} %bitcast.11), custom_call_target="tpu_custom_call" | custom-call | flops 100000000 | bytes 1000000 | tf_op jit(solution)/shard_map/pallas_call | solution.py:588
Async XLA Ops:
  1.8 11.3 %collective-permute-start = (f32[48,256]{1,0:T(8,128)S(1)}, f32[48,256]{1,0:T(8,128)S(1)}, u32[]{:S(2)}, u32[]{:S(2)}) collective-permute-start(f32[48,256]{1,0:T(8,128)S(1)} %shard_map.85.own_ref), channel_id=1, source_target_pairs={{0,31},{1,2},{2,1},{3,4},{4,3},{5,6},{6,5},{7,8},{8,7},{9,10},{10,... | collective-permute-start | bytes 147464 | tf_op jit(solution)/shard_map/ppermute | solution.py:558
  8.2 4.9 %collective-permute-start.1 = (f32[48,256]{1,0:T(8,128)S(1)}, f32[48,256]{1,0:T(8,128)S(1)}, u32[]{:S(2)}, u32[]{:S(2)}) collective-permute-start(f32[48,256]{1,0:T(8,128)S(1)} %shard_map.85.own_ref), channel_id=1, source_target_pairs={{0,1},{1,0},{2,3},{3,2},{4,5},{5,4},{6,7},{7,6},{8,9},{9,8},{10,11... | collective-permute-start | bytes 147464 | tf_op jit(solution)/shard_map/ppermute | solution.py:559
  14.1 10.8 %all-to-all-start = ((f32[32,8,128]{2,1,0:T(8,128)}), f32[32,8,128]{2,1,0:T(8,128)S(1)}, u32[]{:S(2)}, u32[]{:S(2)}) async-start(f32[32,8,128]{2,1,0:T(8,128)} %bitcast.5), calls=%async_computation | async-start | bytes 262144 | tf_op jit(solution)/shard_map/all_to_all | solution.py:581
  30.7 10.8 %all-to-all-start.1 = ((f32[32,8,128]{2,1,0:T(8,128)}), f32[32,8,128]{2,1,0:T(8,128)S(1)}, u32[]{:S(2)}, u32[]{:S(2)}) async-start(f32[32,8,128]{2,1,0:T(8,128)} %bitcast.7), calls=%async_computation.1 | async-start | bytes 262144 | tf_op jit(solution)/shard_map/all_to_all | solution.py:585

commit v7 on v6

--- a/solution.py
+++ b/solution.py
@@ -81,8 +81,56 @@
     out_ref[...] = dot_in_three(weight, edge_ref[...].reshape(-1, shape[1]), (1, 1))
 
 
-def route_kernel(peers, capacity, me_ref, routes_ref, branch_ref, neigh_ref, gcm_ref, own_ref,
-                 pos_ref, base_ref, halo_map_ref):
+def outgoing_kernel(base_ref, map_ref, other_ref, pair_ref, out_ref):
+    window = jnp.concatenate([pair_ref[...], other_ref[...]], axis=1)
+    out_ref[...] = base_ref[...] + 0.25 * slot_rows(map_ref[...], padded(window))
+
+
+class Field:
+    def __init__(self, total):
+        self.total, self.rows, self.diagonals = total, [], []
+
+    def five(self, z):
+        while len(self.diagonals) < z + 2:
+            at = len(self.diagonals)
+            below, here = self.rows[max(at - 1, 0)], self.rows[min(at, self.total - 1)]
+            right = here[1:] + [pltpu.roll(here[0], 7, 0)]
+            self.diagonals.append([a + b for a, b in zip(below, right)])
+        low, high = self.diagonals[z], self.diagonals[z + 1]
+        high = [pltpu.roll(high[-1], 1, 0)] + high[:-1]
+        return [row + (a + b) for row, a, b in zip(self.rows[z], low, high)]
+
+
+def five_points(row, up, down):
+    left = [pltpu.roll(row[-1], 1, 0)] + row[:-1]
+    right = row[1:] + [pltpu.roll(row[0], 7, 0)]
+    return [(a + b + c) + (d + e) for a, b, c, d, e in zip(row, left, right, up, down)]
+
+
+def add_up(values):
+    while len(values) > 1:
+        values = [a + b for a, b in zip(values[::2], values[1::2])]
+    return values[0]
+
+
+def rows_of_sums(ref, crm_levels):
+    return add_up([ref[pl.ds(s, crm_levels, stride=8), :] for s in range(8)])
+
+
+def saturation(z, crm_levels):
+    return 1.0 - z * (2.0 / (crm_levels - 1))
+
+
+def levels_of(crm_levels):
+    return iota((crm_levels, LANES), 0)
+
+
+def shifted(x):
+    return jnp.concatenate([x[:1], x[:-1]], axis=0) + jnp.concatenate([x[1:], x[-1:]], axis=0)
+
+
+def route(peers, capacity, me_ref, routes_ref, branch_ref, neigh_ref, gcm_ref, own_ref,
+          pos_ref, base_ref, halo_map_ref):
     columns = routes_ref.shape[1]
     elems = columns // 4
     crm_levels = own_ref.shape[0]
@@ -128,67 +176,28 @@
     base_ref[...] = slot_rows(place, padded(jnp.concatenate([force, code], axis=0)))
 
 
-def outgoing_kernel(base_ref, map_ref, other_ref, pair_ref, _, out_ref):
-    window = jnp.concatenate([pair_ref[...], other_ref[...]], axis=1)
-    out_ref[...] = base_ref[...] + 0.25 * slot_rows(map_ref[...], padded(window))
-
-
-class Field:
-    def __init__(self, total):
-        self.total, self.rows, self.diagonals = total, [], []
-
-    def five(self, z):
-        while len(self.diagonals) < z + 2:
-            at = len(self.diagonals)
-            below, here = self.rows[max(at - 1, 0)], self.rows[min(at, self.total - 1)]
-            right = here[1:] + [pltpu.roll(here[0], 7, 0)]
-            self.diagonals.append([a + b for a, b in zip(below, right)])
-        low, high = self.diagonals[z], self.diagonals[z + 1]
-        high = [pltpu.roll(high[-1], 1, 0)] + high[:-1]
-        return [row + (a + b) for row, a, b in zip(self.rows[z], low, high)]
-
-
-def five_points(row, up, down):
-    left = [pltpu.roll(row[-1], 1, 0)] + row[:-1]
-    right = row[1:] + [pltpu.roll(row[0], 7, 0)]
-    return [(a + b + c) + (d + e) for a, b, c, d, e in zip(row, left, right, up, down)]
-
-
-def add_up(values):
-    while len(values) > 1:
-        values = [a + b for a, b in zip(values[::2], values[1::2])]
-    return values[0]
-
-
-def rows_of_sums(ref, crm_levels):
-    return add_up([ref[pl.ds(s, crm_levels, stride=8), :] for s in range(8)])
-
-
-def saturation(z, crm_levels):
-    return 1.0 - z * (2.0 / (crm_levels - 1))
-
-
-def levels_of(crm_levels):
-    return iota((crm_levels, LANES), 0)
-
-
-def shifted(x):
-    return jnp.concatenate([x[:1], x[:-1]], axis=0) + jnp.concatenate([x[1:], x[-1:]], axis=0)
-
-
-def before_kernel(start, state_ref, first_ref, sums_ref, kept_ref, part_ref, kept_sums_ref, new_ref, sems, done_sems):
+def before_kernel(peers, capacity, me_ref, routes_ref, branch_ref, neigh_ref, gcm_ref, own_ref, state_ref,
+                  pos_ref, base_ref, halo_map_ref, first_ref, sums_ref,
+                  near_routes_ref, near_branch_ref, near_neigh_ref, near_gcm_ref, kept_ref, part_ref, sems):
     blocks, _, crm_levels, width, _ = kept_ref.shape
     count = width // 8
 
     def copy(j):
-        lanes = pl.ds(pl.multiple_of((start + j) * LANES, LANES), LANES)
+        lanes = pl.ds(pl.multiple_of(j * LANES, LANES), LANES)
         return pltpu.make_async_copy(state_ref.at[:, :, :, lanes], kept_ref.at[j], sems.at[j])
 
-    def done(j):
-        return pltpu.make_async_copy(new_ref.at[j], first_ref.at[j], done_sems.at[j])
-
+    near = (near_routes_ref, near_branch_ref, near_neigh_ref, near_gcm_ref)
+    loads = [
+        pltpu.make_async_copy(far_ref, near_ref, sems.at[blocks + i])
+        for i, (far_ref, near_ref) in enumerate(zip((routes_ref, branch_ref, neigh_ref, gcm_ref), near))
+    ]
+    for load in loads:
+        load.start()
     for j in range(blocks):
         copy(j).start()
+    for load in loads:
+        load.wait()
+    route(peers, capacity, me_ref, *near, own_ref, pos_ref, base_ref, halo_map_ref)
 
     def block(j, _):
         copy(j).wait()
@@ -202,24 +211,18 @@
                 part_ref[1, pl.ds(8 * i, 8), :] = add_up(heat)
             if i:
                 for k, total in enumerate(dry.five(i - 1)):
-                    new_ref[j, i - 1, k] = (0.2 * LOG2E) * total
-        done(j).start()
+                    first_ref[j, i - 1, k] = (0.2 * LOG2E) * total
         level = saturation(levels_of(crm_levels).astype(F32), crm_levels)
         dry_mean = rows_of_sums(part_ref.at[0], crm_levels) * (1.0 / width)
         start = dry_mean + rows_of_sums(part_ref.at[1], crm_levels) * (2.3 / width)
         q = start
         for _ in range(STEPS):
             q = 0.6 * q + 0.2 * shifted(q)
-        kept_sums_ref[j, 0] = LOG2E * (dry_mean - level)
-        kept_sums_ref[j, 1] = q - start
+        sums_ref[j, 0] = LOG2E * (dry_mean - level)
+        sums_ref[j, 1] = q - start
         return 0
 
     lax.fori_loop(0, blocks, block, 0)
-    sums = pltpu.make_async_copy(kept_sums_ref, sums_ref, done_sems.at[blocks])
-    sums.start()
-    for j in range(blocks):
-        done(j).wait()
-    sums.wait()
 
 
 def lane_maps(rows, capacity):
@@ -253,25 +256,11 @@
     return 0.15 + 0.25 * (code == 2.0).astype(F32)
 
 
-def cloud_kernel(capacity, arrived_ref, near_ref, near_sums_ref, far_ref, far_sums_ref, last_ref, force_ref, code_ref, rain_ref,
-                 reply_ref, push_ref, part_ref, sums_ref, first_ref, sems):
+def cloud_kernel(capacity, arrived_ref, first_ref, sums_ref, last_ref, force_ref, code_ref, rain_ref,
+                 reply_ref, push_ref, part_ref):
     blocks, crm_levels, count = last_ref.shape[:3]
-    near = near_ref.shape[0]
     width = count * 8
     part = arrived_ref.shape[0] // blocks
-
-    def load(j):
-        source = near_ref.at[j] if j < near else far_ref.at[j - near]
-        return pltpu.make_async_copy(source, first_ref.at[j], sems.at[j])
-
-    load_sums = [
-        pltpu.make_async_copy(near_sums_ref, sums_ref.at[pl.ds(0, near)], sems.at[blocks]),
-        pltpu.make_async_copy(far_sums_ref, sums_ref.at[pl.ds(near, blocks - near)], sems.at[blocks + 1]),
-    ]
-    for j in range(blocks):
-        load(j).start()
-    for copy in load_sums:
-        copy.start()
     low, high = lane_maps(part, capacity)
     maps = jnp.concatenate([low, high], axis=1)
     maps = jnp.concatenate([maps, maps], axis=0)
@@ -285,7 +274,6 @@
         code_ref[j] = got[crm_levels : crm_levels + 1]
 
     def block(j, _):
-        pltpu.make_async_copy(far_ref.at[0], first_ref.at[j], sems.at[j]).wait()
         lowered = jnp.broadcast_to((1.15 * LOG2E) * rate_of(code_ref[j]), (8, LANES))
         fields = [Field(crm_levels) for _ in range(STEPS)]
         for i in range(crm_levels + STEPS - 1):
@@ -307,8 +295,6 @@
         return 0
 
     lax.fori_loop(0, blocks, block, 0)
-    for copy in load_sums:
-        copy.wait()
     turned = jnp.concatenate([low, high], axis=0)
     for j in range(blocks):
         dg = rows_of_sums(part_ref.at[j], crm_levels) * (1.0 / width) - sums_ref[j, 0]
@@ -473,53 +459,57 @@
 VMEM = pl.BlockSpec(memory_space=pltpu.VMEM)
 
 
-def cloud_before(crm_state, start, blocks):
-    _, crm_levels, width, _ = crm_state.shape
-    cells = crm_levels * width * blocks * LANES
-    field = (blocks, crm_levels, width // 8, 8, LANES)
-    sums = (blocks, 2, crm_levels, LANES)
+def before(peers, capacity, me, routes, branch, neighbours, gcm_state, own, crm_state):
+    _, crm_levels, width, slots = crm_state.shape
+    columns = routes.shape[0]
+    blocks = slots // LANES
+    cells = crm_levels * width * slots
     return call(
-        functools.partial(before_kernel, start),
-        (pltpu.HBM(field, F32), pltpu.HBM(sums, F32)),
+        functools.partial(before_kernel, peers, capacity),
+        (
+            pltpu.VMEM((1, columns), jnp.int32),
+            pltpu.VMEM((slots // 2, LANES), F32),
+            pltpu.VMEM((slots, 2 * columns), BF16),
+            pltpu.VMEM((blocks, crm_levels, width // 8, 8, LANES), F32),
+            pltpu.VMEM((blocks, 2, crm_levels, LANES), F32),
+        ),
         [
+            pltpu.VMEM((1, columns), jnp.int32),
+            pltpu.VMEM((1, columns), jnp.int32),
+            pltpu.VMEM((4, columns // 4), jnp.int32),
+            pltpu.VMEM(gcm_state.shape[::-1], F32),
             pltpu.VMEM((blocks, 2, crm_levels, width, LANES), F32),
             pltpu.VMEM((2, crm_levels * 8, LANES), F32),
-            pltpu.VMEM(sums, F32),
-            pltpu.VMEM(field, F32),
-            pltpu.SemaphoreType.DMA((blocks,)),
-            pltpu.SemaphoreType.DMA((blocks + 1,)),
+            pltpu.SemaphoreType.DMA((blocks + 4,)),
         ],
-        (cells * 25, cells * 8, 0),
-        in_specs=[HBM],
-        out_specs=[HBM] * 2,
-    )(*from_hbm(crm_state))
-
-
-def cloud_steps(capacity, arrived, near, near_sums, far, far_sums):
-    blocks = near.shape[0] + far.shape[0]
-    crm_levels, count = far.shape[1:3]
+        (cells * 25 + 2e9, cells * 8 + 2e6, 0),
+        in_specs=[pl.BlockSpec(memory_space=pltpu.SMEM)] + [HBM] * 4 + [VMEM, HBM],
+        out_specs=[VMEM] * 5,
+    )(
+        me.reshape(1),
+        *from_hbm(routes.T, branch.reshape(1, -1), neighbours.T, gcm_state.T),
+        own,
+        *from_hbm(crm_state),
+    )
+
+
+def cloud_steps(capacity, arrived, first, sums):
+    blocks, crm_levels, count = first.shape[:3]
     cells = crm_levels * count * 8 * blocks * LANES
-    sums = (blocks,) + far_sums.shape[1:]
     return call(
         functools.partial(cloud_kernel, capacity),
         (
-            pltpu.VMEM((blocks,) + far.shape[1:], F32),
+            pltpu.VMEM(first.shape, F32),
             pltpu.VMEM((blocks, crm_levels, LANES), F32),
             pltpu.VMEM((blocks, 1, LANES), F32),
             pltpu.VMEM((blocks, 1, LANES), F32),
             jax.ShapeDtypeStruct(arrived.shape, F32),
         ),
-        [
-            pltpu.VMEM(sums, F32),
-            pltpu.VMEM((blocks, crm_levels * 8, LANES), F32),
-            pltpu.VMEM(sums, F32),
-            pltpu.VMEM((blocks,) + far.shape[1:], F32),
-            pltpu.SemaphoreType.DMA((blocks + 2,)),
-        ],
+        [pltpu.VMEM(sums.shape, F32), pltpu.VMEM((blocks, crm_levels * 8, LANES), F32)],
         (cells * 30, cells * 8, cells * 6),
-        in_specs=[VMEM] + [HBM] * 4,
+        in_specs=[VMEM] * 3,
         out_specs=[VMEM] * 5,
-    )(arrived, *from_hbm(near, near_sums, far, far_sums))
+    )(arrived, first, sums)
 
 
 def cloud_after(crm_state, last, force, code, rain):
@@ -557,31 +547,12 @@
     )
     other = lax.ppermute(own, AXES, [(i, (((i + 1) ^ 1) - 1) % peers) for i in range(peers)])
     pair = lax.ppermute(own, AXES, [(i, i ^ 1) for i in range(peers)])
-    position, base, halo_map = call(
-        functools.partial(route_kernel, peers, capacity),
-        (
-            shape((1, columns), jnp.int32),
-            shape((rows, LANES), F32),
-            shape((slots, 2 * columns), BF16),
-        ),
-        cost=(2e9, 2e6, 0),
-        in_specs=[pl.BlockSpec(memory_space=pltpu.SMEM)] + [VMEM] * 5,
-        out_specs=[VMEM] * 3,
-    )(
-        me.reshape(1),
-        *from_hbm(routes.T, branch.reshape(1, -1), neighbours.T, gcm_state.T),
-        own,
-    )
-    near, near_sums = cloud_before(crm_state, 0, 1)
-    outgoing = call(
-        outgoing_kernel, shape((rows, LANES), F32), cost=(2e8, 1e6, 0),
-        in_specs=[VMEM] * 4 + [HBM], out_specs=VMEM,
-    )(base, halo_map, other, pair, *from_hbm(near))
-    far, far_sums = cloud_before(crm_state, 1, slots // LANES - 1)
+    position, base, halo_map, first, sums = before(
+        peers, capacity, me, routes, branch, neighbours, gcm_state, own, crm_state
+    )
+    outgoing = call(outgoing_kernel, shape((rows, LANES), F32), cost=(2e8, 1e6, 0))(base, halo_map, other, pair)
     arrived = lax.all_to_all(outgoing.reshape(peers, capacity // 2, LANES), AXES, 0, 0, tiled=True)
-    last, force, code, rain, reply = cloud_steps(
-        capacity, arrived.reshape(rows, LANES), near, near_sums, far, far_sums
-    )
+    last, force, code, rain, reply = cloud_steps(capacity, arrived.reshape(rows, LANES), first, sums)
     returned = lax.all_to_all(reply.reshape(peers, capacity // 2, LANES), AXES, 0, 0, tiled=True)
     updated, rain = cloud_after(crm_state, last, force, code, rain)
     levels = features // NV

time: 43.1 us -> 41.2 us (0.956)
  blocking collectives: 0 us -> 11.9 us
  Pallas kernels: 23.2 us -> 16.7 us
  waiting for transfers between devices: 7.32 us -> 2.68 us
  starting transfers between devices: 11.6 us -> 9.01 us
    all_to_all x0 -> x1, blocking collectives: none -> 11.9 us  [on_device(): lax.all_to_all(outgoing.reshape(peers, capacity // 2, LANES), AXES, 0, 0,...]
    pallas_call x4 -> x2, Pallas kernels: 14.1 us -> 8.31 us  [the longest x1 4.73 us: cloud_steps(): call(functools.partial(cloud_kernel, capacity), (pltpu.VMEM(first.shape,...]
    all_to_all x1 -> x0, waiting for transfers between devices: 4.64 us -> none  [on_device(): lax.all_to_all(outgoing.reshape(peers, capacity // 2, LANES), AXES, 0, 0,...]
    all_to_all x1 -> x0, starting transfers between devices: 2.6 us -> none  [on_device(): lax.all_to_all(outgoing.reshape(peers, capacity // 2, LANES), AXES, 0, 0,...]
    pallas_call x1, Pallas kernels: 1.04 us -> 0.36 us  [on_device(): call(outgoing_kernel, shape((rows, LANES), F32), cost=(200000000.0, 10000...]
  transfers between devices with their start and end apart: 4 -> 3, of which waited for: 2 -> 1; matrix products, arithmetic and copies ran while one was open for 0% -> 0% of each run, Pallas kernels for 33% -> 22%
where the time goes in v7:
time: 41.2 us; the launch traced here: 41 us
  Pallas kernels  16.7 us (41%)
  blocking collectives  11.9 us (29%)
  starting transfers between devices  9.01 us (22%)
  waiting for transfers between devices  2.68 us (7%)
  between operations  0.69 us (2%)
    all_to_all x1, blocking collectives, on_device(): lax.all_to_all(outgoing.reshape(peers, capacity // 2, LANES), AXES, 0, 0,...  11.9 us
    ppermute x1, starting transfers between devices, on_device(): lax.ppermute(own, AXES, [(i, ((i + 1 ^ 1) - 1) % peers) for i in range(pe...  6.44 us
    pallas_call x1, Pallas kernels, cloud_after(): call(after_kernel, (jax.ShapeDtypeStruct(crm_state.shape, F32), jax.Shape...  5.55 us
    pallas_call x1, Pallas kernels, cloud_steps(): call(functools.partial(cloud_kernel, capacity), (pltpu.VMEM(first.shape,...  4.73 us
    pallas_call x1, Pallas kernels, before(): call(functools.partial(before_kernel, peers, capacity), (pltpu.VMEM((1, c...  3.58 us
    all_to_all x1, waiting for transfers between devices, on_device(): lax.all_to_all(reply.reshape(peers, capacity // 2, LANES), AXES, 0, 0, ti...  2.67 us
    all_to_all x1, starting transfers between devices, on_device(): lax.all_to_all(reply.reshape(peers, capacity // 2, LANES), AXES, 0, 0, ti...  2.58 us
    pallas_call x1, Pallas kernels, on_device(): call(functools.partial(tendency_kernel, crm_levels), shape((features, col...  1.31 us
  transfers between devices with their start and end apart: 3, of which 1 were waited for; matrix products, arithmetic and copies ran while one was open for 0% of the time, Pallas kernels for 22%

profile of v7, /device:TPU:0, one launch (start us, length us, event | category | flops | bytes accessed | tf_op | source)
XLA Modules:
  0.0 41.0 jit_solution(9099131265151247358)
XLA Ops:
  0.6 1.2 %shard_map.85.own_ref = f32[48,256]{1,0:T(8,128)S(1)} custom-call(f32[64,4,144]{2,1,0:T(4,128)} %edge_ref.1), custom_call_target="tpu_custom_call" | custom-call | flops 10000000 | bytes 400000 | tf_op jit(solution)/shard_map/pallas_call | solution.py:545
  1.8 6.4 %collective-permute-start = (f32[48,256]{1,0:T(8,128)S(1)}, f32[48,256]{1,0:T(8,128)S(1)}, u32[]{:S(2)}, u32[]{:S(2)}) collective-permute-start(f32[48,256]{1,0:T(8,128)S(1)} %shard_map.85.own_ref), channel_id=1, source_target_pairs={{0,31},{1,2},{2,1},{3,4},{4,3},{5,6},{6,5},{7,8},{8,7},{9,10},{10,... | collective-permute-start | bytes 147464 | tf_op jit(solution)/shard_map/ppermute | solution.py:548
  8.2 0.0 collective-permute-start.1
  8.2 3.6 %shard_map.86 = (s32[1,256]{1,0:T(1,128)S(1)}, f32[256,128]{1,0:T(8,128)S(1)}, bf16[512,512]{1,0:T(8,128)(2,1)S(1)}, f32[4,48,4,8,128]{4,3,2,1,0:T(8,128)S(1)}, f32[4,2,48,128]{3,2,1,0:T(8,128)S(1)}) custom-call(s32[1]{0:T(128)} %bitcast.me_ref, s32[1,256]{1,0:T(1,128)} %bitcast.18, s32[1,256]{1,0:T(1,128)} %bitcast.19, s32[4,64]{1,0:T(4,128)} %bitcast.16, ...), custom_call_target="tpu_custom_call" | custom-call | flops 2019660800 | bytes 8291456 | tf_op jit(solution)/shard_map/pallas_call | solution.py:467
  11.8 0.0 collective-permute-done.other_ref
  11.8 0.0 collective-permute-done.1.pair_ref
  11.8 0.4 shard_map.87
  12.2 11.9 %all_to_all.10 = f32[32,8,128]{2,1,0:T(8,128)S(1)} all-to-all(f32[32,8,128]{2,1,0:T(8,128)S(1)} %bitcast.11), channel_id=1, replica_groups=mesh['elem'=8,'sub'=4] {'elem','sub'}, dimensions={0} | all-to-all | bytes 262144 | tf_op jit(solution)/shard_map/all_to_all | solution.py:554
  24.1 4.7 %shard_map.88 = (f32[4,48,4,8,128]{4,3,2,1,0:T(8,128)S(1)}, f32[4,48,128]{2,1,0:T(8,128)S(1)}, f32[4,1,128]{2,1,0:T(1,128)S(1)}, f32[4,1,128]{2,1,0:T(1,128)S(1)}, f32[256,128]{1,0:T(8,128)}) custom-call(f32[256,128]{1,0:T(8,128)S(1)} %bitcast.13, f32[4,48,4,8,128]{4,3,2,1,0:T(8,128)S(1)} %get-tuple-element.18.first_ref, ...), custom_call_target="tpu_custom_call" | custom-call | flops 23592960 | bytes 6291456 | tf_op jit(solution)/shard_map/pallas_call | solution.py:499
  28.8 2.6 %all-to-all-start.1 = ((f32[32,8,128]{2,1,0:T(8,128)}), f32[32,8,128]{2,1,0:T(8,128)S(1)}, u32[]{:S(2)}, u32[]{:S(2)}) async-start(f32[32,8,128]{2,1,0:T(8,128)} %bitcast.7), calls=%async_computation.1 | async-start | bytes 262144 | tf_op jit(solution)/shard_map/all_to_all | solution.py:556
  31.4 5.6 %shard_map.90 = (f32[2,48,32,512]{3,2,1,0:T(8,128)}, f32[4,1,128]{2,1,0:T(1,128)}) custom-call(f32[2,48,32,512]{3,2,1,0:T(8,128)} %state_ref.3, f32[4,48,4,8,128]{4,3,2,1,0:T(8,128)S(1)} %get-tuple-element.21.last_ref, f32[4,48,128]{2,1,0:T(8,128)S(1)} %get-tuple-element.22.force_ref, f32[4,1,128]{2,1,0:T(1,128)S(1)} %get-tuple-element.23.code_ref, ...), custom_call_target="tpu_custom_call" | custom-call | flops 7864320 | bytes 6291456 | tf_op jit(solution)/shard_map/pallas_call | solution.py:520
  37.0 2.7 %all-to-all-done.1 = f32[32,8,128]{2,1,0:T(8,128)S(1)} async-done(((f32[32,8,128]{2,1,0:T(8,128)}), f32[32,8,128]{2,1,0:T(8,128)S(1)}, u32[]{:S(2)}, u32[]{:S(2)}) %all-to-all-start.1) | async-done | bytes 131104 | tf_op jit(solution)/shard_map/all_to_all | solution.py:556
  39.7 1.3 %shard_map.89 = f32[576,256]{1,0:T(8,128)} custom-call(s32[1,256]{1,0:T(1,128)S(1)} %get-tuple-element.15.pos_ref, f32[256,128]{1,0:T(8,128)S(1)} %bitcast.12), custom_call_target="tpu_custom_call" | custom-call | flops 100000000 | bytes 1000000 | tf_op jit(solution)/shard_map/pallas_call | solution.py:559
Async XLA Ops:
  1.8 10.0 %collective-permute-start = (f32[48,256]{1,0:T(8,128)S(1)}, f32[48,256]{1,0:T(8,128)S(1)}, u32[]{:S(2)}, u32[]{:S(2)}) collective-permute-start(f32[48,256]{1,0:T(8,128)S(1)} %shard_map.85.own_ref), channel_id=1, source_target_pairs={{0,31},{1,2},{2,1},{3,4},{4,3},{5,6},{6,5},{7,8},{8,7},{9,10},{10,... | collective-permute-start | bytes 147464 | tf_op jit(solution)/shard_map/ppermute | solution.py:548
  8.2 3.6 %collective-permute-start.1 = (f32[48,256]{1,0:T(8,128)S(1)}, f32[48,256]{1,0:T(8,128)S(1)}, u32[]{:S(2)}, u32[]{:S(2)}) collective-permute-start(f32[48,256]{1,0:T(8,128)S(1)} %shard_map.85.own_ref), channel_id=1, source_target_pairs={{0,1},{1,0},{2,3},{3,2},{4,5},{5,4},{6,7},{7,6},{8,9},{9,8},{10,11... | collective-permute-start | bytes 147464 | tf_op jit(solution)/shard_map/ppermute | solution.py:549
  28.8 10.8 %all-to-all-start.1 = ((f32[32,8,128]{2,1,0:T(8,128)}), f32[32,8,128]{2,1,0:T(8,128)S(1)}, u32[]{:S(2)}, u32[]{:S(2)}) async-start(f32[32,8,128]{2,1,0:T(8,128)} %bitcast.7), calls=%async_computation.1 | async-start | bytes 262144 | tf_op jit(solution)/shard_map/all_to_all | solution.py:556

commit v8 on v7

--- a/solution.py
+++ b/solution.py
@@ -49,8 +49,8 @@
 
 
 def both_halves(x):
-    high, low = split(x)
-    return jnp.concatenate([high, low], axis=0)
+    high = x.astype(BF16).astype(F32)
+    return jnp.concatenate([high, x - high], axis=0).astype(BF16)
 
 
 def slot_rows(onehot, fields):

time: 41.2 us -> 41.2 us (level)
  no operation moved by 1% of the time
where the time goes in v8:
time: 41.2 us; the launch traced here: 41 us
  Pallas kernels  16.7 us (41%)
  blocking collectives  11.9 us (29%)
  starting transfers between devices  9.01 us (22%)
  waiting for transfers between devices  2.68 us (7%)
  between operations  0.69 us (2%)
    all_to_all x1, blocking collectives, on_device(): lax.all_to_all(outgoing.reshape(peers, capacity // 2, LANES), AXES, 0, 0,...  11.9 us
    ppermute x1, starting transfers between devices, on_device(): lax.ppermute(own, AXES, [(i, ((i + 1 ^ 1) - 1) % peers) for i in range(pe...  6.44 us
    pallas_call x1, Pallas kernels, cloud_after(): call(after_kernel, (jax.ShapeDtypeStruct(crm_state.shape, F32), jax.Shape...  5.55 us
    pallas_call x1, Pallas kernels, cloud_steps(): call(functools.partial(cloud_kernel, capacity), (pltpu.VMEM(first.shape,...  4.73 us
    pallas_call x1, Pallas kernels, before(): call(functools.partial(before_kernel, peers, capacity), (pltpu.VMEM((1, c...  3.58 us
    all_to_all x1, waiting for transfers between devices, on_device(): lax.all_to_all(reply.reshape(peers, capacity // 2, LANES), AXES, 0, 0, ti...  2.67 us
    all_to_all x1, starting transfers between devices, on_device(): lax.all_to_all(reply.reshape(peers, capacity // 2, LANES), AXES, 0, 0, ti...  2.58 us
    pallas_call x1, Pallas kernels, on_device(): call(functools.partial(tendency_kernel, crm_levels), shape((features, col...  1.31 us
  transfers between devices with their start and end apart: 3, of which 1 were waited for; matrix products, arithmetic and copies ran while one was open for 0% of the time, Pallas kernels for 22%

profile of v8, /device:TPU:0, one launch (start us, length us, event | category | flops | bytes accessed | tf_op | source)
XLA Modules:
  0.0 41.0 jit_solution(8361433908615468790)
XLA Ops:
  0.6 1.2 %shard_map.85.own_ref = f32[48,256]{1,0:T(8,128)S(1)} custom-call(f32[64,4,144]{2,1,0:T(4,128)} %edge_ref.1), custom_call_target="tpu_custom_call" | custom-call | flops 10000000 | bytes 400000 | tf_op jit(solution)/shard_map/pallas_call | solution.py:545
  1.8 6.4 %collective-permute-start = (f32[48,256]{1,0:T(8,128)S(1)}, f32[48,256]{1,0:T(8,128)S(1)}, u32[]{:S(2)}, u32[]{:S(2)}) collective-permute-start(f32[48,256]{1,0:T(8,128)S(1)} %shard_map.85.own_ref), channel_id=1, source_target_pairs={{0,31},{1,2},{2,1},{3,4},{4,3},{5,6},{6,5},{7,8},{8,7},{9,10},{10,... | collective-permute-start | bytes 147464 | tf_op jit(solution)/shard_map/ppermute | solution.py:548
  8.2 0.0 collective-permute-start.1
  8.2 3.6 %shard_map.86 = (s32[1,256]{1,0:T(1,128)S(1)}, f32[256,128]{1,0:T(8,128)S(1)}, bf16[512,512]{1,0:T(8,128)(2,1)S(1)}, f32[4,48,4,8,128]{4,3,2,1,0:T(8,128)S(1)}, f32[4,2,48,128]{3,2,1,0:T(8,128)S(1)}) custom-call(s32[1]{0:T(128)} %bitcast.me_ref, s32[1,256]{1,0:T(1,128)} %bitcast.18, s32[1,256]{1,0:T(1,128)} %bitcast.19, s32[4,64]{1,0:T(4,128)} %bitcast.16, ...), custom_call_target="tpu_custom_call" | custom-call | flops 2019660800 | bytes 8291456 | tf_op jit(solution)/shard_map/pallas_call | solution.py:467
  11.8 0.0 collective-permute-done.other_ref
  11.8 0.0 collective-permute-done.1.pair_ref
  11.8 0.4 shard_map.87
  12.2 11.9 %all_to_all.10 = f32[32,8,128]{2,1,0:T(8,128)S(1)} all-to-all(f32[32,8,128]{2,1,0:T(8,128)S(1)} %bitcast.11), channel_id=1, replica_groups=mesh['elem'=8,'sub'=4] {'elem','sub'}, dimensions={0} | all-to-all | bytes 262144 | tf_op jit(solution)/shard_map/all_to_all | solution.py:554
  24.1 4.7 %shard_map.88 = (f32[4,48,4,8,128]{4,3,2,1,0:T(8,128)S(1)}, f32[4,48,128]{2,1,0:T(8,128)S(1)}, f32[4,1,128]{2,1,0:T(1,128)S(1)}, f32[4,1,128]{2,1,0:T(1,128)S(1)}, f32[256,128]{1,0:T(8,128)}) custom-call(f32[256,128]{1,0:T(8,128)S(1)} %bitcast.13, f32[4,48,4,8,128]{4,3,2,1,0:T(8,128)S(1)} %get-tuple-element.18.first_ref, ...), custom_call_target="tpu_custom_call" | custom-call | flops 23592960 | bytes 6291456 | tf_op jit(solution)/shard_map/pallas_call | solution.py:499
  28.8 2.6 %all-to-all-start.1 = ((f32[32,8,128]{2,1,0:T(8,128)}), f32[32,8,128]{2,1,0:T(8,128)S(1)}, u32[]{:S(2)}, u32[]{:S(2)}) async-start(f32[32,8,128]{2,1,0:T(8,128)} %bitcast.7), calls=%async_computation.1 | async-start | bytes 262144 | tf_op jit(solution)/shard_map/all_to_all | solution.py:556
  31.4 5.6 %shard_map.90 = (f32[2,48,32,512]{3,2,1,0:T(8,128)}, f32[4,1,128]{2,1,0:T(1,128)}) custom-call(f32[2,48,32,512]{3,2,1,0:T(8,128)} %state_ref.3, f32[4,48,4,8,128]{4,3,2,1,0:T(8,128)S(1)} %get-tuple-element.21.last_ref, f32[4,48,128]{2,1,0:T(8,128)S(1)} %get-tuple-element.22.force_ref, f32[4,1,128]{2,1,0:T(1,128)S(1)} %get-tuple-element.23.code_ref, ...), custom_call_target="tpu_custom_call" | custom-call | flops 7864320 | bytes 6291456 | tf_op jit(solution)/shard_map/pallas_call | solution.py:520
  37.0 2.7 %all-to-all-done.1 = f32[32,8,128]{2,1,0:T(8,128)S(1)} async-done(((f32[32,8,128]{2,1,0:T(8,128)}), f32[32,8,128]{2,1,0:T(8,128)S(1)}, u32[]{:S(2)}, u32[]{:S(2)}) %all-to-all-start.1) | async-done | bytes 131104 | tf_op jit(solution)/shard_map/all_to_all | solution.py:556
  39.7 1.3 %shard_map.89 = f32[576,256]{1,0:T(8,128)} custom-call(s32[1,256]{1,0:T(1,128)S(1)} %get-tuple-element.15.pos_ref, f32[256,128]{1,0:T(8,128)S(1)} %bitcast.12), custom_call_target="tpu_custom_call" | custom-call | flops 100000000 | bytes 1000000 | tf_op jit(solution)/shard_map/pallas_call | solution.py:559
Async XLA Ops:
  1.8 10.0 %collective-permute-start = (f32[48,256]{1,0:T(8,128)S(1)}, f32[48,256]{1,0:T(8,128)S(1)}, u32[]{:S(2)}, u32[]{:S(2)}) collective-permute-start(f32[48,256]{1,0:T(8,128)S(1)} %shard_map.85.own_ref), channel_id=1, source_target_pairs={{0,31},{1,2},{2,1},{3,4},{4,3},{5,6},{6,5},{7,8},{8,7},{9,10},{10,... | collective-permute-start | bytes 147464 | tf_op jit(solution)/shard_map/ppermute | solution.py:548
  8.2 3.6 %collective-permute-start.1 = (f32[48,256]{1,0:T(8,128)S(1)}, f32[48,256]{1,0:T(8,128)S(1)}, u32[]{:S(2)}, u32[]{:S(2)}) collective-permute-start(f32[48,256]{1,0:T(8,128)S(1)} %shard_map.85.own_ref), channel_id=1, source_target_pairs={{0,1},{1,0},{2,3},{3,2},{4,5},{5,4},{6,7},{7,6},{8,9},{9,8},{10,11... | collective-permute-start | bytes 147464 | tf_op jit(solution)/shard_map/ppermute | solution.py:549
  28.8 10.8 %all-to-all-start.1 = ((f32[32,8,128]{2,1,0:T(8,128)}), f32[32,8,128]{2,1,0:T(8,128)S(1)}, u32[]{:S(2)}, u32[]{:S(2)}) async-start(f32[32,8,128]{2,1,0:T(8,128)} %bitcast.7), calls=%async_computation.1 | async-start | bytes 262144 | tf_op jit(solution)/shard_map/all_to_all | solution.py:556

commit v9 on v8

--- a/solution.py
+++ b/solution.py
@@ -177,7 +177,7 @@
 
 
 def before_kernel(peers, capacity, me_ref, routes_ref, branch_ref, neigh_ref, gcm_ref, own_ref, state_ref,
-                  pos_ref, base_ref, halo_map_ref, first_ref, sums_ref,
+                  pos_ref, base_ref, halo_map_ref, first_ref, grown_ref, sums_ref,
                   near_routes_ref, near_branch_ref, near_neigh_ref, near_gcm_ref, kept_ref, part_ref, sems):
     blocks, _, crm_levels, width, _ = kept_ref.shape
     count = width // 8
@@ -212,6 +212,7 @@
             if i:
                 for k, total in enumerate(dry.five(i - 1)):
                     first_ref[j, i - 1, k] = (0.2 * LOG2E) * total
+                    grown_ref[j, i - 1, k] = jnp.exp2((0.2 * LOG2E) * total)
         level = saturation(levels_of(crm_levels).astype(F32), crm_levels)
         dry_mean = rows_of_sums(part_ref.at[0], crm_levels) * (1.0 / width)
         start = dry_mean + rows_of_sums(part_ref.at[1], crm_levels) * (2.3 / width)
@@ -256,7 +257,7 @@
     return 0.15 + 0.25 * (code == 2.0).astype(F32)
 
 
-def cloud_kernel(capacity, arrived_ref, first_ref, sums_ref, last_ref, force_ref, code_ref, rain_ref,
+def cloud_kernel(capacity, arrived_ref, first_ref, grown_ref, sums_ref, last_ref, force_ref, code_ref, rain_ref,
                  reply_ref, push_ref, part_ref):
     blocks, crm_levels, count = last_ref.shape[:3]
     width = count * 8
@@ -276,9 +277,9 @@
     def block(j, _):
         lowered = jnp.broadcast_to((1.15 * LOG2E) * rate_of(code_ref[j]), (8, LANES))
         fields = [Field(crm_levels) for _ in range(STEPS)]
-        for i in range(crm_levels + STEPS - 1):
+        for i in range(crm_levels + 2 * (STEPS - 1)):
             for t in range(STEPS):
-                z = i - t
+                z = i - 2 * t
                 if not 0 <= z < crm_levels:
                     continue
                 push = jnp.broadcast_to(push_ref[j, min(t, 1), pl.ds(z, 1), :], (8, LANES))
@@ -286,7 +287,12 @@
                     values = [first_ref[j, z, k] + push for k in range(count)]
                 else:
                     values = [0.2 * total + push for total in fields[t - 1].five(z)]
-                values = [y - lowered * jnp.log(1.0 + jnp.exp2(y)) for y in values]
+                if t == 0:
+                    factor = jnp.exp2(push)
+                    powers = [factor * grown_ref[j, z, k] for k in range(count)]
+                else:
+                    powers = [jnp.exp2(y) for y in values]
+                values = [y - lowered * jnp.log(1.0 + e) for y, e in zip(values, powers)]
                 fields[t].rows.append(values)
                 if t == STEPS - 1:
                     for k in range(count):
@@ -471,6 +477,7 @@
             pltpu.VMEM((slots // 2, LANES), F32),
             pltpu.VMEM((slots, 2 * columns), BF16),
             pltpu.VMEM((blocks, crm_levels, width // 8, 8, LANES), F32),
+            pltpu.VMEM((blocks, crm_levels, width // 8, 8, LANES), F32),
             pltpu.VMEM((blocks, 2, crm_levels, LANES), F32),
         ),
         [
@@ -484,7 +491,7 @@
         ],
         (cells * 25 + 2e9, cells * 8 + 2e6, 0),
         in_specs=[pl.BlockSpec(memory_space=pltpu.SMEM)] + [HBM] * 4 + [VMEM, HBM],
-        out_specs=[VMEM] * 5,
+        out_specs=[VMEM] * 6,
     )(
         me.reshape(1),
         *from_hbm(routes.T, branch.reshape(1, -1), neighbours.T, gcm_state.T),
@@ -493,7 +500,7 @@
     )
 
 
-def cloud_steps(capacity, arrived, first, sums):
+def cloud_steps(capacity, arrived, first, grown, sums):
     blocks, crm_levels, count = first.shape[:3]
     cells = crm_levels * count * 8 * blocks * LANES
     return call(
@@ -507,9 +514,9 @@
         ),
         [pltpu.VMEM(sums.shape, F32), pltpu.VMEM((blocks, crm_levels * 8, LANES), F32)],
         (cells * 30, cells * 8, cells * 6),
-        in_specs=[VMEM] * 3,
+        in_specs=[VMEM] * 4,
         out_specs=[VMEM] * 5,
-    )(arrived, first, sums)
+    )(arrived, first, grown, sums)
 
 
 def cloud_after(crm_state, last, force, code, rain):
@@ -547,12 +554,12 @@
     )
     other = lax.ppermute(own, AXES, [(i, (((i + 1) ^ 1) - 1) % peers) for i in range(peers)])
     pair = lax.ppermute(own, AXES, [(i, i ^ 1) for i in range(peers)])
-    position, base, halo_map, first, sums = before(
+    position, base, halo_map, first, grown, sums = before(
         peers, capacity, me, routes, branch, neighbours, gcm_state, own, crm_state
     )
     outgoing = call(outgoing_kernel, shape((rows, LANES), F32), cost=(2e8, 1e6, 0))(base, halo_map, other, pair)
     arrived = lax.all_to_all(outgoing.reshape(peers, capacity // 2, LANES), AXES, 0, 0, tiled=True)
-    last, force, code, rain, reply = cloud_steps(capacity, arrived.reshape(rows, LANES), first, sums)
+    last, force, code, rain, reply = cloud_steps(capacity, arrived.reshape(rows, LANES), first, grown, sums)
     returned = lax.all_to_all(reply.reshape(peers, capacity // 2, LANES), AXES, 0, 0, tiled=True)
     updated, rain = cloud_after(crm_state, last, force, code, rain)
     levels = features // NV

time: 41.2 us -> 41.1 us (level)
  transfers between devices with their start and end apart: 3 -> 3, of which waited for: 1 -> 1; matrix products, arithmetic and copies ran while one was open for 0% -> 0% of each run, Pallas kernels for 22% -> 23%
where the time goes in v9:
time: 41.1 us; the launch traced here: 40.9 us
  Pallas kernels  16.8 us (41%)
  blocking collectives  11.8 us (29%)
  starting transfers between devices  9.01 us (22%)
  waiting for transfers between devices  2.68 us (7%)
  between operations  0.69 us (2%)
    all_to_all x1, blocking collectives, on_device(): lax.all_to_all(outgoing.reshape(peers, capacity // 2, LANES), AXES, 0, 0,...  11.8 us
    ppermute x1, starting transfers between devices, on_device(): lax.ppermute(own, AXES, [(i, ((i + 1 ^ 1) - 1) % peers) for i in range(pe...  6.44 us
    pallas_call x1, Pallas kernels, cloud_after(): call(after_kernel, (jax.ShapeDtypeStruct(crm_state.shape, F32), jax.Shape...  5.55 us
    pallas_call x1, Pallas kernels, cloud_steps(): call(functools.partial(cloud_kernel, capacity), (pltpu.VMEM(first.shape,...  4.7 us
    pallas_call x1, Pallas kernels, before(): call(functools.partial(before_kernel, peers, capacity), (pltpu.VMEM((1, c...  3.7 us
    all_to_all x1, waiting for transfers between devices, on_device(): lax.all_to_all(reply.reshape(peers, capacity // 2, LANES), AXES, 0, 0, ti...  2.67 us
    all_to_all x1, starting transfers between devices, on_device(): lax.all_to_all(reply.reshape(peers, capacity // 2, LANES), AXES, 0, 0, ti...  2.58 us
    pallas_call x1, Pallas kernels, on_device(): call(functools.partial(tendency_kernel, crm_levels), shape((features, col...  1.31 us
  transfers between devices with their start and end apart: 3, of which 1 were waited for; matrix products, arithmetic and copies ran while one was open for 0% of the time, Pallas kernels for 23%

profile of v9, /device:TPU:0, one launch (start us, length us, event | category | flops | bytes accessed | tf_op | source)
XLA Modules:
  0.0 40.9 jit_solution(2561909374238748035)
XLA Ops:
  0.6 1.2 %shard_map.85.own_ref = f32[48,256]{1,0:T(8,128)S(1)} custom-call(f32[64,4,144]{2,1,0:T(4,128)} %edge_ref.1), custom_call_target="tpu_custom_call" | custom-call | flops 10000000 | bytes 400000 | tf_op jit(solution)/shard_map/pallas_call | solution.py:552
  1.8 6.4 %collective-permute-start = (f32[48,256]{1,0:T(8,128)S(1)}, f32[48,256]{1,0:T(8,128)S(1)}, u32[]{:S(2)}, u32[]{:S(2)}) collective-permute-start(f32[48,256]{1,0:T(8,128)S(1)} %shard_map.85.own_ref), channel_id=1, source_target_pairs={{0,31},{1,2},{2,1},{3,4},{4,3},{5,6},{6,5},{7,8},{8,7},{9,10},{10,... | collective-permute-start | bytes 147464 | tf_op jit(solution)/shard_map/ppermute | solution.py:555
  8.2 0.0 collective-permute-start.1
  8.2 3.7 %shard_map.86 = (s32[1,256]{1,0:T(1,128)S(1)}, f32[256,128]{1,0:T(8,128)S(1)}, bf16[512,512]{1,0:T(8,128)(2,1)S(1)}, f32[4,48,4,8,128]{4,3,2,1,0:T(8,128)S(1)}, ...) custom-call(s32[1]{0:T(128)} %bitcast.me_ref, s32[1,256]{1,0:T(1,128)} %bitcast.18, s32[1,256]{1,0:T(1,128)} %bitcast.19, ...), custom_call_target="tpu_custom_call" | custom-call | flops 2019660800 | bytes 8291456 | tf_op jit(solution)/shard_map/pallas_call | solution.py:473
  11.9 0.0 collective-permute-done.other_ref
  12.0 0.0 collective-permute-done.1.pair_ref
  12.0 0.4 shard_map.87
  12.3 11.8 %all_to_all.10 = f32[32,8,128]{2,1,0:T(8,128)S(1)} all-to-all(f32[32,8,128]{2,1,0:T(8,128)S(1)} %bitcast.11), channel_id=1, replica_groups=mesh['elem'=8,'sub'=4] {'elem','sub'}, dimensions={0} | all-to-all | bytes 262144 | tf_op jit(solution)/shard_map/all_to_all | solution.py:561
  24.1 4.7 %shard_map.88 = (f32[4,48,4,8,128]{4,3,2,1,0:T(8,128)S(1)}, f32[4,48,128]{2,1,0:T(8,128)S(1)}, f32[4,1,128]{2,1,0:T(1,128)S(1)}, f32[4,1,128]{2,1,0:T(1,128)S(1)}, f32[256,128]{1,0:T(8,128)}) custom-call(f32[256,128]{1,0:T(8,128)S(1)} %bitcast.13, f32[4,48,4,8,128]{4,3,2,1,0:T(8,128)S(1)} %get-tuple-element.19.first_ref, ...), custom_call_target="tpu_custom_call" | custom-call | flops 23592960 | bytes 6291456 | tf_op jit(solution)/shard_map/pallas_call | solution.py:506
  28.8 2.6 %all-to-all-start.1 = ((f32[32,8,128]{2,1,0:T(8,128)}), f32[32,8,128]{2,1,0:T(8,128)S(1)}, u32[]{:S(2)}, u32[]{:S(2)}) async-start(f32[32,8,128]{2,1,0:T(8,128)} %bitcast.7), calls=%async_computation.1 | async-start | bytes 262144 | tf_op jit(solution)/shard_map/all_to_all | solution.py:563
  31.4 5.6 %shard_map.90 = (f32[2,48,32,512]{3,2,1,0:T(8,128)}, f32[4,1,128]{2,1,0:T(1,128)}) custom-call(f32[2,48,32,512]{3,2,1,0:T(8,128)} %state_ref.3, f32[4,48,4,8,128]{4,3,2,1,0:T(8,128)S(1)} %get-tuple-element.23.last_ref, f32[4,48,128]{2,1,0:T(8,128)S(1)} %get-tuple-element.24.force_ref, f32[4,1,128]{2,1,0:T(1,128)S(1)} %get-tuple-element.25.code_ref, ...), custom_call_target="tpu_custom_call" | custom-call | flops 7864320 | bytes 6291456 | tf_op jit(solution)/shard_map/pallas_call | solution.py:527
  37.0 2.7 %all-to-all-done.1 = f32[32,8,128]{2,1,0:T(8,128)S(1)} async-done(((f32[32,8,128]{2,1,0:T(8,128)}), f32[32,8,128]{2,1,0:T(8,128)S(1)}, u32[]{:S(2)}, u32[]{:S(2)}) %all-to-all-start.1) | async-done | bytes 131104 | tf_op jit(solution)/shard_map/all_to_all | solution.py:563
  39.6 1.3 %shard_map.89 = f32[576,256]{1,0:T(8,128)} custom-call(s32[1,256]{1,0:T(1,128)S(1)} %get-tuple-element.16.pos_ref, f32[256,128]{1,0:T(8,128)S(1)} %bitcast.12), custom_call_target="tpu_custom_call" | custom-call | flops 100000000 | bytes 1000000 | tf_op jit(solution)/shard_map/pallas_call | solution.py:566
Async XLA Ops:
  1.8 10.2 %collective-permute-start = (f32[48,256]{1,0:T(8,128)S(1)}, f32[48,256]{1,0:T(8,128)S(1)}, u32[]{:S(2)}, u32[]{:S(2)}) collective-permute-start(f32[48,256]{1,0:T(8,128)S(1)} %shard_map.85.own_ref), channel_id=1, source_target_pairs={{0,31},{1,2},{2,1},{3,4},{4,3},{5,6},{6,5},{7,8},{8,7},{9,10},{10,... | collective-permute-start | bytes 147464 | tf_op jit(solution)/shard_map/ppermute | solution.py:555
  8.2 3.7 %collective-permute-start.1 = (f32[48,256]{1,0:T(8,128)S(1)}, f32[48,256]{1,0:T(8,128)S(1)}, u32[]{:S(2)}, u32[]{:S(2)}) collective-permute-start(f32[48,256]{1,0:T(8,128)S(1)} %shard_map.85.own_ref), channel_id=1, source_target_pairs={{0,1},{1,0},{2,3},{3,2},{4,5},{5,4},{6,7},{7,6},{8,9},{9,8},{10,11... | collective-permute-start | bytes 147464 | tf_op jit(solution)/shard_map/ppermute | solution.py:556
  28.8 10.8 %all-to-all-start.1 = ((f32[32,8,128]{2,1,0:T(8,128)}), f32[32,8,128]{2,1,0:T(8,128)S(1)}, u32[]{:S(2)}, u32[]{:S(2)}) async-start(f32[32,8,128]{2,1,0:T(8,128)} %bitcast.7), calls=%async_computation.1 | async-start | bytes 262144 | tf_op jit(solution)/shard_map/all_to_all | solution.py:563

commit v10 on v9

--- a/solution.py
+++ b/solution.py
@@ -83,7 +83,7 @@
 
 def outgoing_kernel(base_ref, map_ref, other_ref, pair_ref, out_ref):
     window = jnp.concatenate([pair_ref[...], other_ref[...]], axis=1)
-    out_ref[...] = base_ref[...] + 0.25 * slot_rows(map_ref[...], padded(window))
+    out_ref[...] = base_ref[...] + slot_rows(map_ref[...], padded(window))
 
 
 class Field:
@@ -162,7 +162,7 @@
     second = ((column + 1) % 4) * elems + column // 4
     pair = ((row == first) | (row == second)).astype(BF16)
     mapped = dot(pair, chosen.astype(BF16), (1, 1)).astype(BF16)
-    halo_map_ref[...] = dot(place, mapped[:, columns:], (1, 0)).astype(BF16)
+    halo_map_ref[...] = (0.25 * dot(place, mapped[:, columns:], (1, 0))).astype(BF16)
 
     levels = gcm_ref.shape[0] // NV
     mixed = mixing(0) * gcm_ref[:levels, :]
@@ -247,8 +247,8 @@
 
 
 def respond(force):
-    q = jnp.zeros_like(force)
-    for _ in range(STEPS):
+    q = 0.5 * force
+    for _ in range(STEPS - 1):
         q = 0.6 * q + 0.2 * shifted(q) + 0.5 * force
     return q
 
@@ -263,14 +263,15 @@
     width = count * 8
     part = arrived_ref.shape[0] // blocks
     low, high = lane_maps(part, capacity)
+    dry_end, wall = dried(crm_levels), bounds(crm_levels)
     maps = jnp.concatenate([low, high], axis=1)
     maps = jnp.concatenate([maps, maps], axis=0)
     for j in range(blocks):
         got = dot(both_halves(arrived_ref[pl.ds(j * part, part), :]), maps, (0, 0))
         got = got[:HALF, :LANES] + got[HALF:, LANES:]
         push = (-0.65 * LOG2E) * got[:crm_levels]
-        push_ref[j, 0] = push - dried(crm_levels)
-        push_ref[j, 1] = push + bounds(crm_levels)
+        push_ref[j, 0] = push - dry_end
+        push_ref[j, 1] = push + wall
         force_ref[j] = got[:crm_levels]
         code_ref[j] = got[crm_levels : crm_levels + 1]
 

time: 41.1 us -> 41.1 us (level)
  no operation moved by 1% of the time
where the time goes in v10:
time: 41.1 us; the launch traced here: 40.9 us
  Pallas kernels  16.8 us (41%)
  blocking collectives  11.8 us (29%)
  starting transfers between devices  9.01 us (22%)
  waiting for transfers between devices  2.68 us (7%)
  between operations  0.69 us (2%)
    all_to_all x1, blocking collectives, on_device(): lax.all_to_all(outgoing.reshape(peers, capacity // 2, LANES), AXES, 0, 0,...  11.8 us
    ppermute x1, starting transfers between devices, on_device(): lax.ppermute(own, AXES, [(i, ((i + 1 ^ 1) - 1) % peers) for i in range(pe...  6.44 us
    pallas_call x1, Pallas kernels, cloud_after(): call(after_kernel, (jax.ShapeDtypeStruct(crm_state.shape, F32), jax.Shape...  5.55 us
    pallas_call x1, Pallas kernels, cloud_steps(): call(functools.partial(cloud_kernel, capacity), (pltpu.VMEM(first.shape,...  4.7 us
    pallas_call x1, Pallas kernels, before(): call(functools.partial(before_kernel, peers, capacity), (pltpu.VMEM((1, c...  3.71 us
    all_to_all x1, waiting for transfers between devices, on_device(): lax.all_to_all(reply.reshape(peers, capacity // 2, LANES), AXES, 0, 0, ti...  2.67 us
    all_to_all x1, starting transfers between devices, on_device(): lax.all_to_all(reply.reshape(peers, capacity // 2, LANES), AXES, 0, 0, ti...  2.58 us
    pallas_call x1, Pallas kernels, on_device(): call(functools.partial(tendency_kernel, crm_levels), shape((features, col...  1.31 us
  transfers between devices with their start and end apart: 3, of which 1 were waited for; matrix products, arithmetic and copies ran while one was open for 0% of the time, Pallas kernels for 23%

profile of v10, /device:TPU:0, one launch (start us, length us, event | category | flops | bytes accessed | tf_op | source)
XLA Modules:
  0.0 40.9 jit_solution(3301650795892789626)
XLA Ops:
  0.6 1.2 %shard_map.85.own_ref = f32[48,256]{1,0:T(8,128)S(1)} custom-call(f32[64,4,144]{2,1,0:T(4,128)} %edge_ref.1), custom_call_target="tpu_custom_call" | custom-call | flops 10000000 | bytes 400000 | tf_op jit(solution)/shard_map/pallas_call | solution.py:553
  1.8 6.4 %collective-permute-start = (f32[48,256]{1,0:T(8,128)S(1)}, f32[48,256]{1,0:T(8,128)S(1)}, u32[]{:S(2)}, u32[]{:S(2)}) collective-permute-start(f32[48,256]{1,0:T(8,128)S(1)} %shard_map.85.own_ref), channel_id=1, source_target_pairs={{0,31},{1,2},{2,1},{3,4},{4,3},{5,6},{6,5},{7,8},{8,7},{9,10},{10,... | collective-permute-start | bytes 147464 | tf_op jit(solution)/shard_map/ppermute | solution.py:556
  8.2 0.0 collective-permute-start.1
  8.2 3.7 %shard_map.86 = (s32[1,256]{1,0:T(1,128)S(1)}, f32[256,128]{1,0:T(8,128)S(1)}, bf16[512,512]{1,0:T(8,128)(2,1)S(1)}, f32[4,48,4,8,128]{4,3,2,1,0:T(8,128)S(1)}, ...) custom-call(s32[1]{0:T(128)} %bitcast.me_ref, s32[1,256]{1,0:T(1,128)} %bitcast.18, s32[1,256]{1,0:T(1,128)} %bitcast.19, ...), custom_call_target="tpu_custom_call" | custom-call | flops 2019660800 | bytes 8291456 | tf_op jit(solution)/shard_map/pallas_call | solution.py:474
  11.9 0.0 collective-permute-done.other_ref
  12.0 0.0 collective-permute-done.1.pair_ref
  12.0 0.4 shard_map.87
  12.3 11.8 %all_to_all.10 = f32[32,8,128]{2,1,0:T(8,128)S(1)} all-to-all(f32[32,8,128]{2,1,0:T(8,128)S(1)} %bitcast.11), channel_id=1, replica_groups=mesh['elem'=8,'sub'=4] {'elem','sub'}, dimensions={0} | all-to-all | bytes 262144 | tf_op jit(solution)/shard_map/all_to_all | solution.py:562
  24.1 4.7 %shard_map.88 = (f32[4,48,4,8,128]{4,3,2,1,0:T(8,128)S(1)}, f32[4,48,128]{2,1,0:T(8,128)S(1)}, f32[4,1,128]{2,1,0:T(1,128)S(1)}, f32[4,1,128]{2,1,0:T(1,128)S(1)}, f32[256,128]{1,0:T(8,128)}) custom-call(f32[256,128]{1,0:T(8,128)S(1)} %bitcast.13, f32[4,48,4,8,128]{4,3,2,1,0:T(8,128)S(1)} %get-tuple-element.19.first_ref, ...), custom_call_target="tpu_custom_call" | custom-call | flops 23592960 | bytes 6291456 | tf_op jit(solution)/shard_map/pallas_call | solution.py:507
  28.8 2.6 %all-to-all-start.1 = ((f32[32,8,128]{2,1,0:T(8,128)}), f32[32,8,128]{2,1,0:T(8,128)S(1)}, u32[]{:S(2)}, u32[]{:S(2)}) async-start(f32[32,8,128]{2,1,0:T(8,128)} %bitcast.7), calls=%async_computation.1 | async-start | bytes 262144 | tf_op jit(solution)/shard_map/all_to_all | solution.py:564
  31.4 5.6 %shard_map.90 = (f32[2,48,32,512]{3,2,1,0:T(8,128)}, f32[4,1,128]{2,1,0:T(1,128)}) custom-call(f32[2,48,32,512]{3,2,1,0:T(8,128)} %state_ref.3, f32[4,48,4,8,128]{4,3,2,1,0:T(8,128)S(1)} %get-tuple-element.23.last_ref, f32[4,48,128]{2,1,0:T(8,128)S(1)} %get-tuple-element.24.force_ref, f32[4,1,128]{2,1,0:T(1,128)S(1)} %get-tuple-element.25.code_ref, ...), custom_call_target="tpu_custom_call" | custom-call | flops 7864320 | bytes 6291456 | tf_op jit(solution)/shard_map/pallas_call | solution.py:528
  37.0 2.7 %all-to-all-done.1 = f32[32,8,128]{2,1,0:T(8,128)S(1)} async-done(((f32[32,8,128]{2,1,0:T(8,128)}), f32[32,8,128]{2,1,0:T(8,128)S(1)}, u32[]{:S(2)}, u32[]{:S(2)}) %all-to-all-start.1) | async-done | bytes 131104 | tf_op jit(solution)/shard_map/all_to_all | solution.py:564
  39.6 1.3 %shard_map.89 = f32[576,256]{1,0:T(8,128)} custom-call(s32[1,256]{1,0:T(1,128)S(1)} %get-tuple-element.16.pos_ref, f32[256,128]{1,0:T(8,128)S(1)} %bitcast.12), custom_call_target="tpu_custom_call" | custom-call | flops 100000000 | bytes 1000000 | tf_op jit(solution)/shard_map/pallas_call | solution.py:567
Async XLA Ops:
  1.8 10.2 %collective-permute-start = (f32[48,256]{1,0:T(8,128)S(1)}, f32[48,256]{1,0:T(8,128)S(1)}, u32[]{:S(2)}, u32[]{:S(2)}) collective-permute-start(f32[48,256]{1,0:T(8,128)S(1)} %shard_map.85.own_ref), channel_id=1, source_target_pairs={{0,31},{1,2},{2,1},{3,4},{4,3},{5,6},{6,5},{7,8},{8,7},{9,10},{10,... | collective-permute-start | bytes 147464 | tf_op jit(solution)/shard_map/ppermute | solution.py:556
  8.2 3.7 %collective-permute-start.1 = (f32[48,256]{1,0:T(8,128)S(1)}, f32[48,256]{1,0:T(8,128)S(1)}, u32[]{:S(2)}, u32[]{:S(2)}) collective-permute-start(f32[48,256]{1,0:T(8,128)S(1)} %shard_map.85.own_ref), channel_id=1, source_target_pairs={{0,1},{1,0},{2,3},{3,2},{4,5},{5,4},{6,7},{7,6},{8,9},{9,8},{10,11... | collective-permute-start | bytes 147464 | tf_op jit(solution)/shard_map/ppermute | solution.py:557
  28.8 10.8 %all-to-all-start.1 = ((f32[32,8,128]{2,1,0:T(8,128)}), f32[32,8,128]{2,1,0:T(8,128)S(1)}, u32[]{:S(2)}, u32[]{:S(2)}) async-start(f32[32,8,128]{2,1,0:T(8,128)} %bitcast.7), calls=%async_computation.1 | async-start | bytes 262144 | tf_op jit(solution)/shard_map/all_to_all | solution.py:564
